TPU v7x, 32 devices: a whole 2x2x4 slice. The times are simulated.
32 devices in a mesh: ctx: 8 (over z, y), fft: 4 (over x, core).
Axes of the slice: x: 2, y: 2, z: 4, core: 2. Of those that a mesh axis runs over, the one named last changes fastest.
Arguments:
- streams: bfloat16 [3, 1024, 2048], P(None, 'ctx', 'fft'), may hold values from -6 to 6
- taps: float32 [3, 7, 2048], P(None, None, 'fft'), may hold values from -2 to 2
- filters: bfloat16 [1024, 2048], P('ctx', 'fft')
- cotangent: bfloat16 [1024, 2048], P('ctx', 'fft')
Outputs:
- gated: bfloat16 [1024, 2048], P('ctx', 'fft')
- stream_grad: bfloat16 [3, 1024, 2048], P(None, 'ctx', 'fft')
- filter_grad: bfloat16 [1024, 2048], P('ctx', 'fft')
- tap_grad: float32 [3, 7, 2048], P(None, None, 'fft')
All inputs are finite; a program needn't handle non-finite values.
Results may differ from a plain program's by a relative error of at most 0.012.
Values may be sent and summed in bfloat16 or wider, within the bound.
No kernel may reach another device: no remote copies, remote signals or barrier semaphores. Data moves between devices by JAX's collectives and lax.ppermute only.
A program may use at most 64 MiB of HBM per device.

v0:
```python
import math

import jax
import jax.numpy as jnp
from jax import lax
from jax.sharding import PartitionSpec as P

exact_mode = lax.Precision.HIGHEST


def shifted(value, axis, steps):
    count = lax.axis_size(axis)
    first, last = (max(0, -steps), min(count, count - steps))
    return lax.ppermute(value, axis, [(source, source + steps) for source in range(first, last)])


def angle_table(row_count, col_count, col_start, period):
    row_ids = lax.iota(jnp.int32, row_count)
    col_ids = col_start + lax.iota(jnp.int32, col_count)
    turns = row_ids[:, None] * col_ids[None, :] % period
    angles = turns.astype(jnp.float32) * (2.0 * math.pi / period)
    return (jnp.cos(angles), jnp.sin(angles))


def column_start():
    return 0


def split_product(table, signal):
    high_part = table.astype(jnp.bfloat16)
    low_part = (table - high_part.astype(jnp.float32)).astype(jnp.bfloat16)
    first = jnp.einsum("kt,ctu->cku", high_part, signal, preferred_element_type=jnp.float32)
    second = jnp.einsum("kt,ctu->cku", low_part, signal, preferred_element_type=jnp.float32)
    return first + second


def forward_transform(signal):
    input_rows = signal.shape[1]
    row_count = 2 * input_rows
    col_count = signal.shape[2]
    period = row_count * col_count
    cos_first, sin_first = angle_table(row_count, input_rows, 0, row_count)
    first_re = split_product(cos_first, signal)
    first_im = -split_product(sin_first, signal)
    cos_twist, sin_twist = angle_table(row_count, col_count, column_start(), period)
    turned_re = first_re * cos_twist + first_im * sin_twist
    turned_im = first_im * cos_twist - first_re * sin_twist
    cos_second, sin_second = angle_table(col_count, col_count, 0, col_count)
    spec_re = jnp.einsum("cut,tk->cuk", turned_re, cos_second, precision=exact_mode) + jnp.einsum(
        "cut,tk->cuk", turned_im, sin_second, precision=exact_mode
    )
    spec_im = jnp.einsum("cut,tk->cuk", turned_im, cos_second, precision=exact_mode) - jnp.einsum(
        "cut,tk->cuk", turned_re, sin_second, precision=exact_mode
    )
    return (spec_re, spec_im)


def inverse_transform(spec_re, spec_im, keep_rows):
    full_width = spec_re.shape[2]
    cos_second, sin_second = angle_table(full_width, full_width, 0, full_width)
    back_re = jnp.einsum("cuk,kt->cut", spec_re, cos_second, precision=exact_mode) - jnp.einsum(
        "cuk,kt->cut", spec_im, sin_second, precision=exact_mode
    )
    back_im = jnp.einsum("cuk,kt->cut", spec_im, cos_second, precision=exact_mode) + jnp.einsum(
        "cuk,kt->cut", spec_re, sin_second, precision=exact_mode
    )
    row_count = back_re.shape[1]
    col_count = back_re.shape[2]
    period = row_count * full_width
    cos_twist, sin_twist = angle_table(row_count, col_count, column_start(), period)
    turned_re = back_re * cos_twist - back_im * sin_twist
    turned_im = back_im * cos_twist + back_re * sin_twist
    cos_first, sin_first = angle_table(keep_rows, row_count, 0, row_count)
    result = jnp.einsum("tk,cku->ctu", cos_first, turned_re, precision=exact_mode) - jnp.einsum(
        "tk,cku->ctu", sin_first, turned_im, precision=exact_mode
    )
    return result * (1.0 / period)


def regroup_out(stacked):
    count_here = stacked.shape[0]
    channel_count = stacked.shape[1]
    block_rows = stacked.shape[2]
    shaped = stacked.reshape(count_here, channel_count, 1, block_rows)
    return lax.all_to_all(shaped, "ctx", split_axis=1, concat_axis=2, tiled=True)


def regroup_back(stacked):
    count_here = stacked.shape[0]
    arrived = lax.all_to_all(stacked, "ctx", split_axis=2, concat_axis=1, tiled=True)
    return arrived.reshape(count_here, arrived.shape[1], arrived.shape[3])


def merged(block):
    return block.reshape(block.shape[0] * block.shape[1], block.shape[2], block.shape[3])


def local(streams, taps, filters, cotangent):
    block_rows = streams.shape[1]
    tap_reach = taps.shape[1] - 1
    earlier = shifted(streams[:, block_rows - tap_reach :, :], "ctx", 1)
    extended = jnp.concatenate([earlier, streams], axis=1).astype(jnp.float32)
    convolved = jnp.zeros((3, block_rows, streams.shape[2]), jnp.float32)
    for offset in range(tap_reach + 1):
        convolved = (
            convolved
            + taps[:, offset, None, :]
            * extended[:, tap_reach - offset : tap_reach - offset + block_rows, :]
        )
    query_side = convolved[0]
    key_side = convolved[1]
    value_side = convolved[2]
    product = (key_side * value_side).astype(jnp.bfloat16)
    seq_total = block_rows * lax.axis_size("ctx")
    scale_factor = 1.0 / math.sqrt(seq_total)
    arrived = regroup_out(jnp.stack([product, filters]).swapaxes(1, 2))
    per_stream = arrived.shape[1]
    grid_rows = arrived.shape[2]
    first_re, first_im = forward_transform(merged(arrived))
    prod_re = first_re[:per_stream]
    prod_im = first_im[:per_stream]
    filt_re = first_re[per_stream:]
    filt_im = first_im[per_stream:]
    mixed_re = prod_re * filt_re - prod_im * filt_im
    mixed_im = prod_re * filt_im + prod_im * filt_re
    mixed_cols = inverse_transform(mixed_re, mixed_im, grid_rows).astype(jnp.bfloat16)
    mixed_back = regroup_back(mixed_cols.reshape(1, per_stream, grid_rows, mixed_cols.shape[2]))
    mixed = mixed_back[0].T.astype(jnp.float32)
    gated = (query_side * mixed).astype(jnp.bfloat16)
    upstream = cotangent.astype(jnp.float32)
    mixed_grad = (upstream * query_side).astype(jnp.bfloat16)
    query_grad = upstream * mixed
    grad_cols = regroup_out(mixed_grad.T[None])
    grad_re, grad_im = forward_transform(merged(grad_cols))
    through_re = filt_re * grad_re + filt_im * grad_im
    through_im = filt_re * grad_im - filt_im * grad_re
    lagged_re = prod_re * grad_re + prod_im * grad_im
    lagged_im = prod_re * grad_im - prod_im * grad_re
    both_times = inverse_transform(
        jnp.concatenate([through_re, lagged_re], axis=0),
        jnp.concatenate([through_im, lagged_im], axis=0),
        grid_rows,
    )
    product_grad_cols = both_times[:per_stream].astype(jnp.bfloat16)
    filter_grad_cols = (both_times[per_stream:] * scale_factor).astype(jnp.bfloat16)
    returned = regroup_back(jnp.stack([product_grad_cols, filter_grad_cols]))
    product_grad = returned[0].T.astype(jnp.float32)
    filter_grad = returned[1].T
    conv_grad = jnp.stack([query_grad, product_grad * value_side, product_grad * key_side])
    following = shifted(conv_grad[:, :tap_reach, :].astype(jnp.bfloat16), "ctx", -1).astype(
        jnp.float32
    )
    extended_grad = jnp.concatenate([conv_grad, following], axis=1)
    running = jnp.zeros((3, block_rows, streams.shape[2]), jnp.float32)
    for offset in range(tap_reach + 1):
        running = (
            running + taps[:, offset, None, :] * extended_grad[:, offset : offset + block_rows, :]
        )
    stream_grad = running.astype(jnp.bfloat16)
    tap_terms = jnp.stack(
        [
            jnp.sum(
                conv_grad * extended[:, tap_reach - offset : tap_reach - offset + block_rows, :],
                axis=1,
            )
            for offset in range(tap_reach + 1)
        ],
        axis=1,
    )
    tap_grad = lax.psum(tap_terms, "ctx") * scale_factor
    return (gated, stream_grad, filter_grad, tap_grad)


def solution(mesh):
    in_specs = (P(None, "ctx", "fft"), P(None, None, "fft"), P("ctx", "fft"), P("ctx", "fft"))
    out_specs = (P("ctx", "fft"), P(None, "ctx", "fft"), P("ctx", "fft"), P(None, None, "fft"))
    return jax.shard_map(local, mesh=mesh, in_specs=in_specs, out_specs=out_specs, check_vma=False)
```

profile of v0, /device:TPU:0, one launch (start us, length us, event | category | flops | bytes accessed | tf_op | source)
XLA Modules:
  0.0 147.4 jit_solution(15587160972348075417)
XLA Ops:
  0.6 0.8 slice.118
  1.7 4.9 %collective-permute-start = (bf16[3,6,512]{1,2,0:T(8,128)(2,1)S(1)}, bf16[3,6,512]{1,2,0:T(8,128)(2,1)S(1)}, u32[]{:S(2)}, u32[]{:S(2)}) collective-permute-start(bf16[3,6,512]{1,2,0:T(8,128)(2,1)S(1)} %copy.54), channel_id=1, source_target_pairs={{0,4},{4,8},{8,12},{12,16},{16,20},{20,24},{24,28},{1,5},{5,9},{9,... | collective-permute-start | bytes 55304 | tf_op jit(solution)/shard_map/ppermute | solution.py:14
  6.6 1.2 fusion.289
  8.0 1.2 copy.55
  9.2 1.0 copy.70
  10.4 4.6 %collective-permute-done = bf16[3,6,512]{1,2,0:T(8,128)(2,1)S(1)} collective-permute-done((bf16[3,6,512]{1,2,0:T(8,128)(2,1)S(1)}, bf16[3,6,512]{1,2,0:T(8,128)(2,1)S(1)}, u32[]{:S(2)}, u32[]{:S(2)}) %collective-permute-start) | collective-permute-done | bytes 18464 | tf_op jit(solution)/shard_map/ppermute | solution.py:14
  15.3 3.0 %multiply_add_fusion.1 = f32[3,128,512]{1,2,0:T(8,128)S(1)} fusion(f32[3,134,512]{1,2,0:T(8,128)S(1)} %maximum_convert_fusion, f32[3,512]{1,0:T(4,128)S(1)} %get-tuple-element.45, f32[3,512]{1,0:T(4,128)S(1)} %get-tuple-element.46, f32[3,512]{1,0:T(4,128)S(1)} %get-tuple-element.47, f32[3,512]{1,0:T(4,128)S(1)} %get-tuple-element.48, ...), kind=kLoop, calls=%fused_computation.72 | loop fusion | flops 2555904 | bytes 6334464 | tf_op jit(solution)/shard_map/add | solution.py:106
  19.0 1.4 reduce
  21.1 6.8 %all-to-all-start.2 = ((bf16[8,2,4096]{2,1,0:T(2,128)(2,1)}), bf16[8,2,4096]{2,1,0:T(2,128)(2,1)S(1)}, u32[]{:S(2)}, u32[]{:S(2)}) async-start(bf16[8,2,4096]{2,1,0:T(2,128)(2,1)} %reshape.86), calls=%async_computation.2 | async-start | bytes 262144 | tf_op jit(solution)/shard_map/all_to_all | solution.py:85
  28.0 1.0 copy.57
  29.0 6.3 %all-to-all-done.2 = bf16[8,2,4096]{2,1,0:T(2,128)(2,1)S(1)} async-done(((bf16[8,2,4096]{2,1,0:T(2,128)(2,1)}), bf16[8,2,4096]{2,1,0:T(2,128)(2,1)S(1)}, u32[]{:S(2)}, u32[]{:S(2)}) %all-to-all-start.2) | async-done | bytes 131104 | tf_op jit(solution)/shard_map/all_to_all | solution.py:85
  35.3 4.2 %all-to-all-start = ((bf16[2,512,1,128]{3,0,2,1:T(2,128)(2,1)}), bf16[2,512,1,128]{3,0,2,1:T(2,128)(2,1)}, u32[]{:S(2)}, u32[]{:S(2)}) async-start(bf16[2,512,1,128]{3,0,2,1:T(2,128)(2,1)} %copy.57), calls=%async_computation | async-start | bytes 524288 | tf_op jit(solution)/shard_map/all_to_all | solution.py:85
  41.1 1.7 %fusion.48 = f32[64,16,128]{2,0,1:T(8,128)} fusion(f32[64,16,128]{2,1,0:T(8,128)S(1)} %get-tuple-element.30), kind=kOutput, calls=%fused_computation.92 | convolution fusion | flops 201555968 | bytes 1048576 | tf_op jit(solution)/shard_map/cut,tk->cuk/dot_general | solution.py:52
  42.8 0.9 fusion.52
  43.7 1.7 %convolution_add_fusion.6 = f32[64,16,128]{2,0,1:T(8,128)} fusion(f32[64,16,128]{2,0,1:T(8,128)S(1)} %fusion.52, f32[64,16,128]{2,1,0:T(8,128)S(1)} %get-tuple-element.30), kind=kOutput, calls=%fused_computation.19 | convolution fusion | flops 201687040 | bytes 1572864 | tf_op jit(solution)/shard_map/cut,tk->cuk/dot_general | solution.py:49
  45.3 2.2 %all-to-all-done = bf16[2,512,1,128]{3,0,2,1:T(2,128)(2,1)} async-done(((bf16[2,512,1,128]{3,0,2,1:T(2,128)(2,1)}), bf16[2,512,1,128]{3,0,2,1:T(2,128)(2,1)}, u32[]{:S(2)}, u32[]{:S(2)}) %all-to-all-start) | async-done | bytes 262176 | tf_op jit(solution)/shard_map/all_to_all | solution.py:85
  47.6 1.0 copy.58
  50.5 1.4 fusion.28
  52.0 1.4 fusion.24
  53.4 1.5 %convolution_add_fusion.1 = f32[128,16,128]{2,0,1:T(8,128)S(1)} fusion(f32[128,16,128]{2,0,1:T(8,128)S(1)} %fusion.28, f32[128,16,128]{2,1,0:T(8,128)S(1)} %get-tuple-element.27), kind=kOutput, calls=%fused_computation.4 | convolution fusion | flops 403144704 | bytes 3145728 | tf_op jit(solution)/shard_map/cut,tk->cuk/dot_general | solution.py:49
  54.9 1.5 %convolution_subtract_fusion.1 = f32[128,16,128]{2,0,1:T(8,128)S(1)} fusion(f32[128,16,128]{2,0,1:T(8,128)S(1)} %fusion.24, f32[128,16,128]{2,1,0:T(8,128)S(1)} %get-tuple-element.26), kind=kOutput, calls=%fused_computation.3 | convolution fusion | flops 403144704 | bytes 3145728 | tf_op jit(solution)/shard_map/cut,tk->cuk/dot_general | solution.py:52
  56.4 1.4 multiply_add_fusion.3
  57.9 1.7 %fusion.18 = f32[128,16,128]{2,1,0:T(8,128)S(1)} fusion(f32[128,16,128]{2,0,1:T(8,128)S(1)} %pad_maximum_fusion.2), kind=kOutput, calls=%fused_computation.37 | convolution fusion | flops 402882560 | bytes 2097152 | tf_op jit(solution)/shard_map/cuk,kt->cut/dot_general | solution.py:64
  59.7 1.7 %fusion.22 = f32[128,16,128]{2,1,0:T(8,128)S(1)} fusion(f32[128,16,128]{2,0,1:T(8,128)S(1)} %pad_maximum_fusion.1), kind=kOutput, calls=%fused_computation.41 | convolution fusion | flops 402882560 | bytes 2097152 | tf_op jit(solution)/shard_map/cuk,kt->cut/dot_general | solution.py:61
  61.4 1.7 %convolution_add_fusion = f32[128,16,128]{2,1,0:T(8,128)S(1)} fusion(f32[128,16,128]{2,1,0:T(8,128)S(1)} %fusion.18, f32[128,16,128]{2,0,1:T(8,128)S(1)} %pad_maximum_fusion.1), kind=kOutput, calls=%fused_computation.1 | convolution fusion | flops 403144704 | bytes 3145728 | tf_op jit(solution)/shard_map/cuk,kt->cut/dot_general | solution.py:64
  63.2 1.7 %convolution_subtract_fusion = f32[128,16,128]{2,1,0:T(8,128)S(1)} fusion(f32[128,16,128]{2,1,0:T(8,128)S(1)} %fusion.22, f32[128,16,128]{2,0,1:T(8,128)S(1)} %pad_maximum_fusion.2), kind=kOutput, calls=%fused_computation.2 | convolution fusion | flops 403144704 | bytes 3145728 | tf_op jit(solution)/shard_map/cuk,kt->cut/dot_general | solution.py:61
  64.9 0.8 fusion.14
  65.7 0.8 fusion.7
  66.6 1.0 fusion.54
  67.6 1.9 %fusion.58 = f32[64,16,128]{2,1,0:T(8,128)} fusion(f32[64,16,128]{2,0,1:T(8,128)S(1)} %get-tuple-element.29), kind=kOutput, calls=%fused_computation.102 | convolution fusion | flops 201555968 | bytes 1048576 | tf_op jit(solution)/shard_map/cuk,kt->cut/dot_general | solution.py:61
  69.5 1.3 convolution_add_fusion.7
  70.9 0.8 copy.81
  71.6 4.1 %all-to-all-start.3 = ((bf16[2,64,8,128]{3,1,0,2:T(8,128)(2,1)}), bf16[2,64,8,128]{3,1,0,2:T(8,128)(2,1)}, u32[]{:S(2)}, u32[]{:S(2)}) async-start(bf16[2,64,8,128]{3,1,0,2:T(8,128)(2,1)} %copy.81), calls=%async_computation.3 | async-start | bytes 524288 | tf_op jit(solution)/shard_map/all_to_all | solution.py:90
  75.7 2.1 %convolution_subtract_fusion.4 = f32[64,16,128]{2,1,0:T(8,128)S(1)} fusion(f32[64,16,128]{2,1,0:T(8,128)} %fusion.58, f32[64,16,128]{2,0,1:T(8,128)S(1)} %get-tuple-element.28), kind=kOutput, calls=%fused_computation.21 | convolution fusion | flops 201687040 | bytes 1572864 | tf_op jit(solution)/shard_map/cuk,kt->cut/dot_general | solution.py:61
  79.4 4.5 %all-to-all-done.3 = bf16[2,64,8,128]{3,1,0,2:T(8,128)(2,1)} async-done(((bf16[2,64,8,128]{3,1,0,2:T(8,128)(2,1)}), bf16[2,64,8,128]{3,1,0,2:T(8,128)(2,1)}, u32[]{:S(2)}, u32[]{:S(2)}) %all-to-all-start.3) | async-done | bytes 262176 | tf_op jit(solution)/shard_map/all_to_all | solution.py:90
  83.9 3.4 %all-to-all-start.1 = ((bf16[1,64,8,128]{3,1,0,2:T(8,128)(2,1)}), bf16[1,64,8,128]{3,1,0,2:T(8,128)(2,1)S(1)}, u32[]{:S(2)}, u32[]{:S(2)}) async-start(bf16[1,64,8,128]{3,1,0,2:T(8,128)(2,1)} %copy.68), calls=%async_computation.1 | async-start | bytes 262144 | tf_op jit(solution)/shard_map/all_to_all | solution.py:90
  87.3 1.0 copy.168
  88.3 0.7 fusion.288
  89.0 5.6 %all-to-all-done.1 = bf16[1,64,8,128]{3,1,0,2:T(8,128)(2,1)S(1)} async-done(((bf16[1,64,8,128]{3,1,0,2:T(8,128)(2,1)}), bf16[1,64,8,128]{3,1,0,2:T(8,128)(2,1)S(1)}, u32[]{:S(2)}, u32[]{:S(2)}) %all-to-all-start.1) | async-done | bytes 131104 | tf_op jit(solution)/shard_map/all_to_all | solution.py:90
  94.6 1.0 fusion.65
  95.6 2.8 %multiply_reduce_fusion = (f32[3,512]{1,0:T(4,128)S(1)}, f32[3,512]{1,0:T(4,128)S(1)}, f32[3,512]{1,0:T(4,128)S(1)}, f32[3,512]{1,0:T(4,128)S(1)}, f32[3,512]{1,...) fusion(f32[3,134,512]{1,2,0:T(8,128)S(1)} %maximum_convert_fusion, f32[1,128,512]{1,2,0:T(8,128)S(1)} %get-tuple-element.33, ...), kind=kLoop, calls=%fused_computation.65 | loop fusion | flops 3134976 | bytes 6334464 | tf_op jit(solution)/shard_map/reduce_sum | solution.py:162
  98.5 34.5 %psum.7 = f32[3,7,512]{2,0,1:T(4,128)S(1)} all-reduce(f32[3,7,512]{2,0,1:T(4,128)S(1)} %constant_dynamic-update-slice_fusion), channel_id=1, replica_groups=mesh['ctx'=8,'fft'=4] {'ctx'}, use_global_device_ids=true, to_apply=%region_7.8 | all-reduce | flops 10752 | bytes 86016 | tf_op jit(solution)/shard_map/psum | solution.py:170
  133.0 1.3 collective-permute-start.1
  134.4 0.8 copy.83
  135.1 0.8 copy.85
  136.5 6.2 %collective-permute-done.1 = bf16[3,6,512]{1,2,0:T(8,128)(2,1)S(1)} collective-permute-done((bf16[3,6,512]{1,2,0:T(8,128)(2,1)S(1)}, bf16[3,6,512]{1,2,0:T(8,128)(2,1)S(1)}, u32[]{:S(2)}, u32[]{:S(2)}) %collective-permute-start.1) | collective-permute-done | bytes 18464 | tf_op jit(solution)/shard_map/ppermute | solution.py:14
  143.6 2.9 %fusion.31 = bf16[3,128,512]{1,2,0:T(8,128)(2,1)S(1)} fusion(f32[3,134,512]{1,2,0:T(8,128)S(1)} %pad_maximum_fusion, f32[3,512]{1,0:T(4,128)S(1)} %copy-done.13, f32[3,512]{1,0:T(4,128)S(1)} %copy-done.15, f32[3,512]{1,0:T(4,128)S(1)} %copy-done.5, f32[3,512]{1,0:T(4,128)S(1)} %copy-done.7, f32[3,512]{1,0:T(4,128)S(1)} %copy-done.9, ...), kind=kLoop, calls=%fused_computation.51 | loop fusion | flops 3145728 | bytes 5941248 | tf_op jit(solution)/shard_map/convert_element_type | solution.py:159
  146.5 0.9 copy.84
  (81 shorter events, 9.2 us)
Async XLA Ops:
  0.6 9.6 %copy-start.3 = (bf16[128,512]{1,0:T(8,128)(2,1)S(1)}, bf16[128,512]{1,0:T(8,128)(2,1)}, u32[]{:S(2)}) copy-start(bf16[128,512]{1,0:T(8,128)(2,1)} %param.6) | copy-start | bytes 393220
  1.7 13.2 %collective-permute-start = (bf16[3,6,512]{1,2,0:T(8,128)(2,1)S(1)}, bf16[3,6,512]{1,2,0:T(8,128)(2,1)S(1)}, u32[]{:S(2)}, u32[]{:S(2)}) collective-permute-start(bf16[3,6,512]{1,2,0:T(8,128)(2,1)S(1)} %copy.54), channel_id=1, source_target_pairs={{0,4},{4,8},{8,12},{12,16},{16,20},{20,24},{24,28},{1,5},{5,9},{9,... | collective-permute-start | bytes 55304 | tf_op jit(solution)/shard_map/ppermute | solution.py:14
  7.8 7.4 %copy-start.4 = (f32[3,512]{1,0:T(4,128)}, f32[3,512]{1,0:T(4,128)S(1)}, u32[]{:S(2)}) copy-start(f32[3,512]{1,0:T(4,128)S(1)} %get-tuple-element.47) | copy-start | bytes 18436
  7.8 7.4 %copy-start.6 = (f32[3,512]{1,0:T(4,128)}, f32[3,512]{1,0:T(4,128)S(1)}, u32[]{:S(2)}) copy-start(f32[3,512]{1,0:T(4,128)S(1)} %get-tuple-element.48) | copy-start | bytes 18436
  7.8 7.4 %copy-start.8 = (f32[3,512]{1,0:T(4,128)}, f32[3,512]{1,0:T(4,128)S(1)}, u32[]{:S(2)}) copy-start(f32[3,512]{1,0:T(4,128)S(1)} %get-tuple-element.49) | copy-start | bytes 18436
  7.9 7.4 %copy-start.10 = (f32[3,512]{1,0:T(4,128)}, f32[3,512]{1,0:T(4,128)S(1)}, u32[]{:S(2)}) copy-start(f32[3,512]{1,0:T(4,128)S(1)} %get-tuple-element.50) | copy-start | bytes 18436
  7.9 7.4 %copy-start.12 = (f32[3,512]{1,0:T(4,128)}, f32[3,512]{1,0:T(4,128)S(1)}, u32[]{:S(2)}) copy-start(f32[3,512]{1,0:T(4,128)S(1)} %get-tuple-element.45) | copy-start | bytes 18436
  7.9 7.4 %copy-start.14 = (f32[3,512]{1,0:T(4,128)}, f32[3,512]{1,0:T(4,128)S(1)}, u32[]{:S(2)}) copy-start(f32[3,512]{1,0:T(4,128)S(1)} %get-tuple-element.46) | copy-start | bytes 18436
  9.2 9.1 %copy-start.16 = (f32[3,1,512]{2,0,1:T(4,128)}, f32[3,1,512]{2,0,1:T(4,128)S(1)}, u32[]{:S(2)}) copy-start(f32[3,1,512]{2,0,1:T(4,128)S(1)} %copy.169) | copy-start | bytes 18436
  21.1 14.1 %all-to-all-start.2 = ((bf16[8,2,4096]{2,1,0:T(2,128)(2,1)}), bf16[8,2,4096]{2,1,0:T(2,128)(2,1)S(1)}, u32[]{:S(2)}, u32[]{:S(2)}) async-start(bf16[8,2,4096]{2,1,0:T(2,128)(2,1)} %reshape.86), calls=%async_computation.2 | async-start | bytes 262144 | tf_op jit(solution)/shard_map/all_to_all | solution.py:85
  35.3 12.3 %all-to-all-start = ((bf16[2,512,1,128]{3,0,2,1:T(2,128)(2,1)}), bf16[2,512,1,128]{3,0,2,1:T(2,128)(2,1)}, u32[]{:S(2)}, u32[]{:S(2)}) async-start(bf16[2,512,1,128]{3,0,2,1:T(2,128)(2,1)} %copy.57), calls=%async_computation | async-start | bytes 524288 | tf_op jit(solution)/shard_map/all_to_all | solution.py:85
  54.9 1.5 %copy-start = (f32[64,16,128]{2,0,1:T(8,128)S(1)}, f32[64,16,128]{2,0,1:T(8,128)}, u32[]{:S(2)}) copy-start(f32[64,16,128]{2,0,1:T(8,128)} %convolution_add_fusion.6) | copy-start | bytes 1572868
  54.9 1.5 %copy-start.1 = (f32[64,16,128]{2,0,1:T(8,128)S(1)}, f32[64,16,128]{2,0,1:T(8,128)}, u32[]{:S(2)}) copy-start(f32[64,16,128]{2,0,1:T(8,128)} %fusion.48) | copy-start | bytes 1572868
  71.6 12.3 %all-to-all-start.3 = ((bf16[2,64,8,128]{3,1,0,2:T(8,128)(2,1)}), bf16[2,64,8,128]{3,1,0,2:T(8,128)(2,1)}, u32[]{:S(2)}, u32[]{:S(2)}) async-start(bf16[2,64,8,128]{3,1,0,2:T(8,128)(2,1)} %copy.81), calls=%async_computation.3 | async-start | bytes 524288 | tf_op jit(solution)/shard_map/all_to_all | solution.py:90
  83.9 10.7 %all-to-all-start.1 = ((bf16[1,64,8,128]{3,1,0,2:T(8,128)(2,1)}), bf16[1,64,8,128]{3,1,0,2:T(8,128)(2,1)S(1)}, u32[]{:S(2)}, u32[]{:S(2)}) async-start(bf16[1,64,8,128]{3,1,0,2:T(8,128)(2,1)} %copy.68), calls=%async_computation.1 | async-start | bytes 262144 | tf_op jit(solution)/shard_map/all_to_all | solution.py:90
  98.3 36.8 %copy-start.2 = (bf16[1,8,64,1,128]{4,2,1,3,0:T(8,128)(2,1)S(1)}, bf16[1,8,64,1,128]{4,2,1,3,0:T(8,128)(2,1)}, u32[]{:S(2)}) copy-start(bf16[1,8,64,1,128]{4,2,1,3,0:T(8,128)(2,1)} %get-tuple-element.35) | copy-start | bytes 393220
  133.0 9.7 %collective-permute-start.1 = (bf16[3,6,512]{1,2,0:T(8,128)(2,1)S(1)}, bf16[3,6,512]{1,2,0:T(8,128)(2,1)S(1)}, u32[]{:S(2)}, u32[]{:S(2)}) collective-permute-start(bf16[3,6,512]{1,2,0:T(8,128)(2,1)S(1)} %bitcast.220), channel_id=1, source_target_pairs={{4,0},{8,4},{12,8},{16,12},{20,16},{24,20},{28,24},{5,1},{9,5},{13... | collective-permute-start | bytes 55304 | tf_op jit(solution)/shard_map/ppermute | solution.py:14
  142.8 0.7 copy-start.5
  142.8 0.7 copy-start.7
  142.8 0.7 copy-start.9
  142.8 0.7 copy-start.11
  142.8 0.7 copy-start.13
  142.8 0.7 copy-start.15
  142.8 0.7 copy-start.17
where the time goes:
time: 148 us; the launch traced here: 147 us
  blocking collectives  34.5 us (23%)
  matrix products  30.4 us (21%)
  waiting for transfers between devices  29.3 us (20%)
  starting transfers between devices  24.6 us (17%)
  local copies, waits for them, and re-layouts  15.3 us (10%)
  other arithmetic  11.9 us (8%)
    psum x1, blocking collectives, local(): tap_grad = lax.psum(tap_terms, 'ctx') * scale_factor  34.5 us
    all_to_all x2, starting transfers between devices, regroup_out(): lax.all_to_all(shaped, 'ctx', split_axis=1, concat_axis=2, tiled=True)  11 us
    ppermute x2, waiting for transfers between devices, shifted(): lax.ppermute(value, axis, [(source, source + steps) for source in range(f...  10.7 us
    all_to_all x2, waiting for transfers between devices, regroup_back(): lax.all_to_all(stacked, 'ctx', split_axis=2, concat_axis=1, tiled=True)  10.1 us
    all_to_all x2, waiting for transfers between devices, regroup_out(): lax.all_to_all(shaped, 'ctx', split_axis=1, concat_axis=2, tiled=True)  8.54 us
    unnamed x57, local copies, waits for them, and re-layouts  7.55 us
    all_to_all x2, starting transfers between devices, regroup_back(): lax.all_to_all(stacked, 'ctx', split_axis=2, concat_axis=1, tiled=True)  7.43 us
    ppermute x2, starting transfers between devices, shifted(): lax.ppermute(value, axis, [(source, source + steps) for source in range(f...  6.19 us
  transfers between devices with their start and end apart: 6, of which 6 were waited for; matrix products, arithmetic and copies ran while one was open for 12% of the time, Pallas kernels for 0%

commit v1 on v0

--- a/solution.py
+++ b/solution.py
@@ -1,11 +1,295 @@
+import functools
 import math
 
 import jax
 import jax.numpy as jnp
+import numpy as np
 from jax import lax
+from jax.experimental import pallas as pl
+from jax.experimental.pallas import tpu as pltpu
 from jax.sharding import PartitionSpec as P
 
 exact_mode = lax.Precision.HIGHEST
+LANES = 128
+HALF = LANES // 2
+EDGE = 8
+TAP_ROWS = 32
+TABLE_BYTES = 16 * 1024 * 1024
+VMEM_BYTES = 48 * 1024 * 1024
+
+
+def odd_tables(total):
+    freq = 2 * np.arange(total)[:, None] + 1
+    angles = (freq * np.arange(total)[None, :] % (4 * total)) * (math.pi / (2 * total))
+    table = np.concatenate([np.cos(angles), -np.sin(angles)])
+    high = table.astype(jnp.bfloat16)
+    back = np.ascontiguousarray(table.T / total).astype(jnp.bfloat16)
+    return high, back
+
+
+def lower_lanes(rows):
+    return lax.broadcasted_iota(jnp.int32, (rows, LANES), 1) < HALF
+
+
+def turned(value):
+    return pltpu.roll(value, HALF, 1)
+
+
+def wide(value):
+    return value.astype(jnp.float32)
+
+
+def paired(first, second, odd, low):
+    left = jnp.where(odd, turned(first), first)
+    right = jnp.where(odd, second, turned(second))
+    return jnp.where(low, left, right).astype(jnp.bfloat16)
+
+
+def pack_kernel(count, streams_ref, filters_ref, cotangent_ref, taps_ref, *out_refs):
+    me = lax.axis_index("ctx")
+    rows = filters_ref.shape[0]
+    half_rows = rows // 2
+    tap_count = taps_ref.shape[1]
+    low = lower_lanes(rows)
+    low_half = lower_lanes(half_rows)
+    for step in range(count):
+        owner = lax.rem(me + step, count)
+        cols = pl.ds(pl.multiple_of(owner // 2 * LANES, LANES), LANES)
+        odd = lax.rem(owner, 2) == 1
+        out = out_refs[step]
+        out[0:rows, :] = paired(wide(streams_ref[1, :, cols]), wide(streams_ref[2, :, cols]), odd, low)
+        out[rows : 2 * rows, :] = paired(wide(streams_ref[0, :, cols]), wide(cotangent_ref[:, cols]), odd, low)
+        lag_block = wide(filters_ref[:, cols])
+        out[2 * rows :, :] = paired(lag_block[:half_rows], lag_block[half_rows:], odd, low_half)
+    cols = pl.ds(pl.multiple_of(me // 2 * LANES, LANES), LANES)
+    odd = lax.rem(me, 2) == 1
+    tap_out = out_refs[count]
+    low_taps = lower_lanes(tap_count)
+    here = [jnp.where(odd, turned(taps_ref[i, :, cols]), taps_ref[i, :, cols]) for i in range(3)]
+    first_tap = lax.broadcasted_iota(jnp.int32, (tap_count, LANES), 0) == 0
+    tap_out[...] = jnp.zeros_like(tap_out)
+    tap_out[0:tap_count, :] = jnp.where(low_taps, here[1], turned(here[2]))
+    tap_out[EDGE : EDGE + tap_count, :] = jnp.where(low_taps, here[0], jnp.where(first_tap, 1.0, 0.0))
+
+
+def main_kernel(count, tap_count, scale, *refs):
+    in_refs = refs[:count]
+    tap_ref, table_hbm, back_hbm = refs[count : count + 3]
+    out_refs = refs[count + 3 : 2 * count + 3]
+    (raw_kv, raw_qc, conv_kv, conv_qc, signals, spectra, grad_kv, grad_q, lag_grad,
+     table, back, sems) = refs[2 * count + 3 :]
+    me = lax.axis_index("ctx")
+    total = signals.shape[0]
+    rows = total // count
+    half_rows = rows // 2
+    low = lower_lanes(rows)
+    low_half = lower_lanes(half_rows)
+    table_copy = pltpu.make_async_copy(table_hbm, table, sems.at[0])
+    back_copy = pltpu.make_async_copy(back_hbm, back, sems.at[1])
+    table_copy.start()
+    back_copy.start()
+
+    raw_kv[0:EDGE, :] = jnp.zeros((EDGE, LANES), jnp.float32)
+    raw_qc[0:EDGE, :] = jnp.zeros((EDGE, LANES), jnp.float32)
+    grad_kv[total:, :] = jnp.zeros((EDGE, LANES), jnp.float32)
+    grad_q[total:, :] = jnp.zeros((EDGE, LANES), jnp.float32)
+    for step in range(count):
+        source = lax.rem(me - step + count, count)
+        base = pl.multiple_of(source * rows, rows)
+        block = in_refs[step]
+        raw_kv[pl.ds(base + EDGE, rows), :] = wide(block[0:rows, :])
+        raw_qc[pl.ds(base + EDGE, rows), :] = wide(block[rows : 2 * rows, :])
+        lag_block = wide(block[2 * rows :, :])
+        other = turned(lag_block)
+        signals[pl.ds(base, half_rows), LANES:] = jnp.where(low_half, lag_block, other).astype(jnp.bfloat16)
+        signals[pl.ds(base + half_rows, half_rows), LANES:] = jnp.where(low_half, other, lag_block).astype(jnp.bfloat16)
+
+    tap_kv = [tap_ref[j : j + 1, :] for j in range(tap_count)]
+    tap_q = [tap_ref[EDGE + j : EDGE + j + 1, :] for j in range(tap_count)]
+
+    for block in range(count):
+        base = block * rows
+        key_value = jnp.zeros((rows, LANES), jnp.float32)
+        query_cot = jnp.zeros((rows, LANES), jnp.float32)
+        for j in range(tap_count):
+            window = slice(base + EDGE - j, base + EDGE - j + rows)
+            key_value = key_value + tap_kv[j] * raw_kv[window, :]
+            query_cot = query_cot + tap_q[j] * raw_qc[window, :]
+        conv_kv[base : base + rows, :] = key_value
+        conv_qc[base : base + rows, :] = query_cot
+        product = key_value * turned(key_value)
+        mixed_grad = query_cot * turned(query_cot)
+        signals[base : base + rows, :LANES] = jnp.where(low, product, mixed_grad).astype(jnp.bfloat16)
+
+    table_copy.wait()
+    part = min(256, total)
+    low_part = lower_lanes(part)
+    for start in range(0, total, part):
+        real = jnp.dot(table[start : start + part, :], signals[...], preferred_element_type=jnp.float32)
+        imag = jnp.dot(
+            table[total + start : total + start + part, :], signals[...], preferred_element_type=jnp.float32
+        )
+        a_re, b_re = real[:, :LANES], real[:, LANES:]
+        a_im, b_im = imag[:, :LANES], imag[:, LANES:]
+        b_im = jnp.where(low_part, b_im, -b_im)
+        r_re, r_im = turned(a_re), turned(a_im)
+        spectra[start : start + part, :LANES] = (a_re * b_re - a_im * b_im).astype(jnp.bfloat16)
+        spectra[start : start + part, LANES:] = (a_re * r_re + a_im * r_im).astype(jnp.bfloat16)
+        spectra[total + start : total + start + part, :LANES] = (a_re * b_im + a_im * b_re).astype(jnp.bfloat16)
+        spectra[total + start : total + start + part, LANES:] = (a_re * r_im - a_im * r_re).astype(jnp.bfloat16)
+
+    back_copy.wait()
+    for block in range(count):
+        base = block * rows
+        here = slice(base, base + rows)
+        result = jnp.dot(back[here, :], spectra[...], preferred_element_type=jnp.float32)
+        pair = wide(result[:, :LANES].astype(jnp.bfloat16))
+        other = turned(pair)
+        gated_grad = conv_qc[here, :] * jnp.where(low, pair, other)
+        grad_q[here, :] = turned(gated_grad)
+        grad_kv[here, :] = jnp.where(low, other, pair) * turned(conv_kv[here, :])
+        lag_terms = result[:, LANES:] * scale
+        lag_grad[block * half_rows : (block + 1) * half_rows, :] = jnp.where(
+            low_half, lag_terms[:half_rows], turned(lag_terms[half_rows:])
+        )
+
+    tap_sum_kv = [jnp.zeros((EDGE, LANES), jnp.float32)] * tap_count
+    tap_sum_q = [jnp.zeros((EDGE, LANES), jnp.float32)] * tap_count
+    for step in range(count):
+        owner = lax.rem(me + step, count)
+        base = pl.multiple_of(owner * rows, rows)
+        out = out_refs[step]
+        stream_kv = jnp.zeros((rows, LANES), jnp.float32)
+        stream_q = jnp.zeros((rows, LANES), jnp.float32)
+        for j in range(tap_count):
+            stream_kv = stream_kv + tap_kv[j] * grad_kv[pl.ds(base + j, rows), :]
+            stream_q = stream_q + tap_q[j] * grad_q[pl.ds(base + j, rows), :]
+        out[0:rows, :] = stream_kv.astype(jnp.bfloat16)
+        out[rows : 2 * rows, :] = stream_q.astype(jnp.bfloat16)
+        lag_base = pl.multiple_of(owner * half_rows, half_rows)
+        out[2 * rows : 2 * rows + half_rows, :] = lag_grad[pl.ds(lag_base, half_rows), :].astype(jnp.bfloat16)
+    for block in range(count):
+        base = block * rows
+        kv = grad_kv[base : base + rows, :]
+        q = grad_q[base : base + rows, :]
+        for j in range(tap_count):
+            window = slice(base + EDGE - j, base + EDGE - j + rows)
+            tap_sum_kv[j] = tap_sum_kv[j] + jnp.sum((kv * raw_kv[window, :]).reshape(rows // EDGE, EDGE, LANES), axis=0)
+            tap_sum_q[j] = tap_sum_q[j] + jnp.sum((q * raw_qc[window, :]).reshape(rows // EDGE, EDGE, LANES), axis=0)
+    spare = [jnp.zeros((1, LANES), jnp.float32)] * (EDGE - tap_count)
+    sums = jnp.concatenate(
+        [jnp.sum(s, axis=0, keepdims=True) for s in tap_sum_kv] + spare
+        + [jnp.sum(s, axis=0, keepdims=True) for s in tap_sum_q] + spare, axis=0
+    ) * scale
+    high = sums.astype(jnp.bfloat16)
+    both = jnp.concatenate([wide(high), sums - wide(high)], axis=0).astype(jnp.bfloat16)
+    for step in range(count):
+        out_refs[step][2 * rows + half_rows :, :] = both
+
+
+def unpack_kernel(count, tap_count, *refs):
+    in_refs = refs[:count]
+    gated_ref, stream_ref, lag_ref, tap_ref = refs[count : count + 4]
+    blocks = refs[count + 4]
+    me = lax.axis_index("ctx")
+    rows = gated_ref.shape[0]
+    half_rows = rows // 2
+    low = lower_lanes(rows)
+    low_half = lower_lanes(half_rows)
+    low_taps = lower_lanes(EDGE)
+    for step in range(count):
+        owner = lax.rem(me - step + count, count)
+        blocks[owner, :, :] = in_refs[step][...]
+    for pair in range(count // 2):
+        cols = slice(pair * LANES, (pair + 1) * LANES)
+        even, odd = wide(blocks[2 * pair, :, :]), wide(blocks[2 * pair + 1, :, :])
+        turned_even, turned_odd = turned(even), turned(odd)
+
+        def lower_of(window, mask):
+            return jnp.where(mask, even[window], turned_odd[window])
+
+        def upper_of(window, mask):
+            return jnp.where(mask, turned_even[window], odd[window])
+
+        key_value, query_gated = slice(0, rows), slice(rows, 2 * rows)
+        stream_ref[1, :, cols] = lower_of(key_value, low).astype(jnp.bfloat16)
+        stream_ref[2, :, cols] = upper_of(key_value, low).astype(jnp.bfloat16)
+        stream_ref[0, :, cols] = lower_of(query_gated, low).astype(jnp.bfloat16)
+        gated_ref[:, cols] = upper_of(query_gated, low).astype(jnp.bfloat16)
+        lags = slice(2 * rows, 2 * rows + half_rows)
+        lag_ref[0:half_rows, cols] = lower_of(lags, low_half).astype(jnp.bfloat16)
+        lag_ref[half_rows:, cols] = upper_of(lags, low_half).astype(jnp.bfloat16)
+        start = 2 * rows + half_rows
+        high_kv, high_q, rest_kv, rest_q = [slice(start + g * EDGE, start + (g + 1) * EDGE) for g in range(4)]
+        tap_ref[1, :, cols] = (lower_of(high_kv, low_taps) + lower_of(rest_kv, low_taps))[:tap_count]
+        tap_ref[2, :, cols] = (upper_of(high_kv, low_taps) + upper_of(rest_kv, low_taps))[:tap_count]
+        tap_ref[0, :, cols] = (lower_of(high_q, low_taps) + lower_of(rest_q, low_taps))[:tap_count]
+
+
+def exchanged(blocks):
+    count = len(blocks)
+    return [blocks[0]] + [
+        lax.ppermute(blocks[step], "ctx", [(source, (source + step) % count) for source in range(count)])
+        for step in range(1, count)
+    ]
+
+
+def in_vmem(count):
+    return [pl.BlockSpec(memory_space=pltpu.VMEM)] * count
+
+
+def local_dense(streams, taps, filters, cotangent):
+    count = lax.axis_size("ctx")
+    rows, channels = filters.shape
+    tap_count = taps.shape[1]
+    total = rows * count
+    params = pltpu.CompilerParams(vmem_limit_bytes=VMEM_BYTES)
+    sent_rows = 2 * rows + rows // 2
+    packed = pl.pallas_call(
+        functools.partial(pack_kernel, count),
+        out_shape=[jax.ShapeDtypeStruct((sent_rows, LANES), jnp.bfloat16)] * count
+        + [jax.ShapeDtypeStruct((2 * EDGE, LANES), jnp.float32)],
+        in_specs=in_vmem(4),
+        out_specs=in_vmem(count + 1),
+        compiler_params=params,
+        name="pack",
+    )(streams, filters, cotangent, taps)
+    arrived = exchanged(packed[:count])
+    table, back = odd_tables(total)
+    back_rows = sent_rows + TAP_ROWS
+    f32_rows = lambda extent: pltpu.VMEM((extent, LANES), jnp.float32)
+    made = pl.pallas_call(
+        functools.partial(main_kernel, count, tap_count, 1.0 / math.sqrt(total)),
+        out_shape=[jax.ShapeDtypeStruct((back_rows, LANES), jnp.bfloat16)] * count,
+        in_specs=in_vmem(count + 1) + [pl.BlockSpec(memory_space=pl.ANY)] * 2,
+        out_specs=in_vmem(count),
+        scratch_shapes=[
+            f32_rows(total + EDGE), f32_rows(total + EDGE), f32_rows(total), f32_rows(total),
+            pltpu.VMEM((total, 2 * LANES), jnp.bfloat16), pltpu.VMEM((2 * total, 2 * LANES), jnp.bfloat16),
+            f32_rows(total + EDGE), f32_rows(total + EDGE), f32_rows(total // 2),
+            pltpu.VMEM(table.shape, jnp.bfloat16), pltpu.VMEM(back.shape, jnp.bfloat16),
+            pltpu.SemaphoreType.DMA((2,)),
+        ],
+        compiler_params=params,
+        name="channels",
+    )(*arrived, packed[count], jnp.asarray(table), jnp.asarray(back))
+    returned = exchanged(made)
+    return tuple(
+        pl.pallas_call(
+            functools.partial(unpack_kernel, count, tap_count),
+            out_shape=[
+                jax.ShapeDtypeStruct(filters.shape, jnp.bfloat16),
+                jax.ShapeDtypeStruct(streams.shape, jnp.bfloat16),
+                jax.ShapeDtypeStruct(filters.shape, jnp.bfloat16),
+                jax.ShapeDtypeStruct(taps.shape, jnp.float32),
+            ],
+            in_specs=in_vmem(count),
+            out_specs=in_vmem(4),
+            scratch_shapes=[pltpu.VMEM((count, back_rows, LANES), jnp.bfloat16)],
+            compiler_params=params,
+            name="unpack",
+        )(*returned)
+    )
 
 
 def shifted(value, axis, steps):
@@ -95,7 +379,7 @@
     return block.reshape(block.shape[0] * block.shape[1], block.shape[2], block.shape[3])
 
 
-def local(streams, taps, filters, cotangent):
+def local_factored(streams, taps, filters, cotangent):
     block_rows = streams.shape[1]
     tap_reach = taps.shape[1] - 1
     earlier = shifted(streams[:, block_rows - tap_reach :, :], "ctx", 1)
@@ -171,6 +455,17 @@
     return (gated, stream_grad, filter_grad, tap_grad)
 
 
+def local(streams, taps, filters, cotangent):
+    count = lax.axis_size("ctx")
+    rows, channels = filters.shape
+    tap_count = taps.shape[1]
+    pairs_fill_lanes = channels == count * HALF and count % 2 == 0
+    short_enough = rows % LANES == 0 and 8 * (rows * count) ** 2 <= TABLE_BYTES and tap_count < EDGE
+    if pairs_fill_lanes and short_enough:
+        return local_dense(streams, taps, filters, cotangent)
+    return local_factored(streams, taps, filters, cotangent)
+
+
 def solution(mesh):
     in_specs = (P(None, "ctx", "fft"), P(None, None, "fft"), P("ctx", "fft"), P("ctx", "fft"))
     out_specs = (P("ctx", "fft"), P(None, "ctx", "fft"), P("ctx", "fft"), P(None, None, "fft"))

time: 148 us -> 52.2 us (0.35)
  the two profiles are of different devices: /device:TPU:0 before, /device:TPU:22 now
where the time goes in v1:
time: 52.2 us; the launch traced here: 51.9 us
  waiting for transfers between devices  24.2 us (46%)
  starting transfers between devices  14.2 us (27%)
  Pallas kernels  7.04 us (13%)
  local copies, waits for them, and re-layouts  5.78 us (11%)
  between operations  0.69 us (1%)
    ppermute x14, waiting for transfers between devices, exchanged(): lax.ppermute(blocks[step], 'ctx', [(source, (source + step) % count) for...  24.2 us
    ppermute x14, starting transfers between devices, exchanged(): lax.ppermute(blocks[step], 'ctx', [(source, (source + step) % count) for...  14.2 us
    unnamed x10, local copies, waits for them, and re-layouts  5.78 us
    pallas_call x1, Pallas kernels, local_dense(): pl.pallas_call(functools.partial(main_kernel, count, tap_count, 1.0 / mat...  5.37 us
    pallas_call x1, Pallas kernels, local_dense(): pl.pallas_call(functools.partial(unpack_kernel, count, tap_count), out_sh...  1.13 us
  transfers between devices with their start and end apart: 14, of which 6 were waited for; matrix products, arithmetic and copies ran while one was open for 0% of the time, Pallas kernels for 0%

profile of v1, /device:TPU:22, one launch (start us, length us, event | category | flops | bytes accessed | tf_op | source)
XLA Modules:
  0.0 51.9 jit_solution(13254185644611423460)
XLA Ops:
  0.6 0.0 copy-start.1
  0.6 1.0 %copy-done.1 = bf16[3,128,512]{2,1,0:T(8,128)(2,1)S(1)} copy-done((bf16[3,128,512]{2,1,0:T(8,128)(2,1)S(1)}, bf16[3,128,512]{2,1,0:T(8,128)(2,1)}, u32[]{:S(2)}) %copy-start.1) | copy-done | bytes 393240
  1.6 0.0 copy-start.2
  1.6 0.9 %copy-done.2 = bf16[128,512]{1,0:T(8,128)(2,1)S(1)} copy-done((bf16[128,512]{1,0:T(8,128)(2,1)S(1)}, bf16[128,512]{1,0:T(8,128)(2,1)}, u32[]{:S(2)}) %copy-start.2) | copy-done | bytes 131096
  2.5 0.0 copy-start.3
  2.5 0.9 %copy-done.3 = bf16[128,512]{1,0:T(8,128)(2,1)S(1)} copy-done((bf16[128,512]{1,0:T(8,128)(2,1)S(1)}, bf16[128,512]{1,0:T(8,128)(2,1)}, u32[]{:S(2)}) %copy-start.3) | copy-done | bytes 131096
  3.4 0.0 copy-start.4
  3.4 0.8 %copy-done.4 = f32[3,7,512]{2,1,0:T(8,128)S(1)} copy-done((f32[3,7,512]{2,1,0:T(8,128)S(1)}, f32[3,7,512]{2,1,0:T(8,128)}, u32[]{:S(2)}) %copy-start.4) | copy-done | bytes 43032
  4.2 0.5 %pack.1 = (bf16[320,128]{1,0:T(8,128)(2,1)S(1)}, bf16[320,128]{1,0:T(8,128)(2,1)S(1)}, bf16[320,128]{1,0:T(8,128)(2,1)S(1)}, bf16[320,128]{1,0:T(8,128)(2,1)S(1)...) custom-call(bf16[3,128,512]{2,1,0:T(8,128)(2,1)S(1)} %copy-done.1, ...), custom_call_target="tpu_custom_call" | custom-call | tf_op jit(solution)/shard_map/pack/pallas_call | solution.py:248
  4.8 1.6 %collective-permute-start = (bf16[320,128]{1,0:T(8,128)(2,1)S(1)}, bf16[320,128]{1,0:T(8,128)(2,1)S(1)}, u32[]{:S(2)}, u32[]{:S(2)}) collective-permute-start(bf16[320,128]{1,0:T(8,128)(2,1)S(1)} %get-tuple-element.22), channel_id=1, source_target_pairs={{0,4},{4,8},{8,12},{12,16},{16,20},{20,24},{24,28},{28,0},{1,5},{5... | collective-permute-start | bytes 245768 | tf_op jit(solution)/shard_map/ppermute | solution.py:232
  6.3 0.2 collective-permute-start.1
  6.6 1.6 %collective-permute-start.2 = (bf16[320,128]{1,0:T(8,128)(2,1)S(1)}, bf16[320,128]{1,0:T(8,128)(2,1)S(1)}, u32[]{:S(2)}, u32[]{:S(2)}) collective-permute-start(bf16[320,128]{1,0:T(8,128)(2,1)S(1)} %get-tuple-element.24), channel_id=1, source_target_pairs={{0,12},{4,16},{8,20},{12,24},{16,28},{20,0},{24,4},{28,8},{1,13},{... | collective-permute-start | bytes 245768 | tf_op jit(solution)/shard_map/ppermute | solution.py:232
  8.2 2.6 %collective-permute-start.3 = (bf16[320,128]{1,0:T(8,128)(2,1)S(1)}, bf16[320,128]{1,0:T(8,128)(2,1)S(1)}, u32[]{:S(2)}, u32[]{:S(2)}) collective-permute-start(bf16[320,128]{1,0:T(8,128)(2,1)S(1)} %get-tuple-element.25), channel_id=1, source_target_pairs={{0,16},{4,20},{8,24},{12,28},{16,0},{20,4},{24,8},{28,12},{1,17},{... | collective-permute-start | bytes 245768 | tf_op jit(solution)/shard_map/ppermute | solution.py:232
  10.8 1.3 %collective-permute-start.4 = (bf16[320,128]{1,0:T(8,128)(2,1)S(1)}, bf16[320,128]{1,0:T(8,128)(2,1)S(1)}, u32[]{:S(2)}, u32[]{:S(2)}) collective-permute-start(bf16[320,128]{1,0:T(8,128)(2,1)S(1)} %get-tuple-element.26), channel_id=1, source_target_pairs={{0,20},{4,24},{8,28},{12,0},{16,4},{20,8},{24,12},{28,16},{1,21},{... | collective-permute-start | bytes 245768 | tf_op jit(solution)/shard_map/ppermute | solution.py:232
  12.1 0.0 collective-permute-done.refs_1_
  12.1 0.5 collective-permute-start.5
  12.5 6.2 %collective-permute-done.1.refs_2_ = bf16[320,128]{1,0:T(8,128)(2,1)S(1)} collective-permute-done((bf16[320,128]{1,0:T(8,128)(2,1)S(1)}, bf16[320,128]{1,0:T(8,128)(2,1)S(1)}, u32[]{:S(2)}, u32[]{:S(2)}) %collective-permute-start.1) | collective-permute-done | bytes 81952 | tf_op jit(solution)/shard_map/ppermute | solution.py:232
  18.7 0.0 collective-permute-start.6
  18.7 0.0 collective-permute-done.2.refs_3_
  18.7 0.0 collective-permute-done.3.refs_4_
  18.7 0.0 collective-permute-done.4.refs_5_
  18.7 1.6 %collective-permute-done.5.refs_6_ = bf16[320,128]{1,0:T(8,128)(2,1)S(1)} collective-permute-done((bf16[320,128]{1,0:T(8,128)(2,1)S(1)}, bf16[320,128]{1,0:T(8,128)(2,1)S(1)}, u32[]{:S(2)}, u32[]{:S(2)}) %collective-permute-start.5) | collective-permute-done | bytes 81952 | tf_op jit(solution)/shard_map/ppermute | solution.py:232
  20.3 3.7 %collective-permute-done.6.refs_7_ = bf16[320,128]{1,0:T(8,128)(2,1)S(1)} collective-permute-done((bf16[320,128]{1,0:T(8,128)(2,1)S(1)}, bf16[320,128]{1,0:T(8,128)(2,1)S(1)}, u32[]{:S(2)}, u32[]{:S(2)}) %collective-permute-start.6) | collective-permute-done | bytes 81952 | tf_op jit(solution)/shard_map/ppermute | solution.py:232
  24.0 0.0 copy-start
  24.0 2.2 %copy-done = bf16[2048,1024]{1,0:T(8,128)(2,1)S(1)} copy-done((bf16[2048,1024]{1,0:T(8,128)(2,1)S(1)}, bf16[2048,1024]{1,0:T(8,128)(2,1)}, u32[]{:S(2)}) %copy-start) | copy-done | bytes 4194328
  26.2 5.4 %channels.1 = (bf16[352,128]{1,0:T(8,128)(2,1)S(1)}, bf16[352,128]{1,0:T(8,128)(2,1)S(1)}, bf16[352,128]{1,0:T(8,128)(2,1)S(1)}, bf16[352,128]{1,0:T(8,128)(2,1)...) custom-call(bf16[320,128]{1,0:T(8,128)(2,1)S(1)} %get-tuple-element., ...), custom_call_target="tpu_custom_call" | custom-call | tf_op jit(solution)/shard_map/channels/pallas_call | solution.py:261
  31.6 0.1 collective-permute-start.7
  31.7 0.2 collective-permute-start.8
  31.8 3.0 %collective-permute-start.9 = (bf16[352,128]{1,0:T(8,128)(2,1)S(1)}, bf16[352,128]{1,0:T(8,128)(2,1)S(1)}, u32[]{:S(2)}, u32[]{:S(2)}) collective-permute-start(bf16[352,128]{1,0:T(8,128)(2,1)S(1)} %get-tuple-element.33), channel_id=1, source_target_pairs={{0,12},{4,16},{8,20},{12,24},{16,28},{20,0},{24,4},{28,8},{1,13},{... | collective-permute-start | bytes 270344 | tf_op jit(solution)/shard_map/ppermute | solution.py:232
  34.8 1.3 %collective-permute-start.10 = (bf16[352,128]{1,0:T(8,128)(2,1)S(1)}, bf16[352,128]{1,0:T(8,128)(2,1)S(1)}, u32[]{:S(2)}, u32[]{:S(2)}) collective-permute-start(bf16[352,128]{1,0:T(8,128)(2,1)S(1)} %get-tuple-element.34), channel_id=1, source_target_pairs={{0,16},{4,20},{8,24},{12,28},{16,0},{20,4},{24,8},{28,12},{1,17},{... | collective-permute-start | bytes 270344 | tf_op jit(solution)/shard_map/ppermute | solution.py:232
  36.1 1.4 %collective-permute-start.11 = (bf16[352,128]{1,0:T(8,128)(2,1)S(1)}, bf16[352,128]{1,0:T(8,128)(2,1)S(1)}, u32[]{:S(2)}, u32[]{:S(2)}) collective-permute-start(bf16[352,128]{1,0:T(8,128)(2,1)S(1)} %get-tuple-element.35), channel_id=1, source_target_pairs={{0,20},{4,24},{8,28},{12,0},{16,4},{20,8},{24,12},{28,16},{1,21},{... | collective-permute-start | bytes 270344 | tf_op jit(solution)/shard_map/ppermute | solution.py:232
  37.5 0.0 collective-permute-done.7.refs_1_
  37.5 0.6 %collective-permute-start.12 = (bf16[352,128]{1,0:T(8,128)(2,1)S(1)}, bf16[352,128]{1,0:T(8,128)(2,1)S(1)}, u32[]{:S(2)}, u32[]{:S(2)}) collective-permute-start(bf16[352,128]{1,0:T(8,128)(2,1)S(1)} %get-tuple-element.36), channel_id=1, source_target_pairs={{0,24},{4,28},{8,0},{12,4},{16,8},{20,12},{24,16},{28,20},{1,25},{... | collective-permute-start | bytes 270344 | tf_op jit(solution)/shard_map/ppermute | solution.py:232
  38.1 7.3 %collective-permute-done.8.refs_2_ = bf16[352,128]{1,0:T(8,128)(2,1)S(1)} collective-permute-done((bf16[352,128]{1,0:T(8,128)(2,1)S(1)}, bf16[352,128]{1,0:T(8,128)(2,1)S(1)}, u32[]{:S(2)}, u32[]{:S(2)}) %collective-permute-start.8) | collective-permute-done | bytes 90144 | tf_op jit(solution)/shard_map/ppermute | solution.py:232
  45.3 0.0 collective-permute-start.13
  45.3 2.3 %collective-permute-done.9.refs_3_ = bf16[352,128]{1,0:T(8,128)(2,1)S(1)} collective-permute-done((bf16[352,128]{1,0:T(8,128)(2,1)S(1)}, bf16[352,128]{1,0:T(8,128)(2,1)S(1)}, u32[]{:S(2)}, u32[]{:S(2)}) %collective-permute-start.9) | collective-permute-done | bytes 90144 | tf_op jit(solution)/shard_map/ppermute | solution.py:232
  47.7 0.0 collective-permute-done.10.refs_4_
  47.7 0.0 collective-permute-done.11.refs_5_
  47.7 0.0 collective-permute-done.12.refs_6_
  47.7 3.1 %collective-permute-done.13.refs_7_ = bf16[352,128]{1,0:T(8,128)(2,1)S(1)} collective-permute-done((bf16[352,128]{1,0:T(8,128)(2,1)S(1)}, bf16[352,128]{1,0:T(8,128)(2,1)S(1)}, u32[]{:S(2)}, u32[]{:S(2)}) %collective-permute-start.13) | collective-permute-done | bytes 90144 | tf_op jit(solution)/shard_map/ppermute | solution.py:232
  50.8 1.1 %unpack.1 = (bf16[128,512]{1,0:T(8,128)(2,1)}, bf16[3,128,512]{2,1,0:T(8,128)(2,1)}, bf16[128,512]{1,0:T(8,128)(2,1)}, f32[3,7,512]{2,1,0:T(8,128)}) custom-call(bf16[352,128]{1,0:T(8,128)(2,1)S(1)} %get-tuple-element.30.refs_0_, bf16[352,128]{1,0:T(8,128)(2,1)S(1)} %collective-permute-done.7.refs_1_, bf16[352,128]{1,0:T(8,128)(2,1)S(1)} %collective-permute-done.8.refs_2_, ...), custom_call_target="tpu_custom_call" | custom-call | tf_op jit(solution)/shard_map/unpack/pallas_call | solution.py:278
Async XLA Ops:
  0.6 1.0 %copy-start.1 = (bf16[3,128,512]{2,1,0:T(8,128)(2,1)S(1)}, bf16[3,128,512]{2,1,0:T(8,128)(2,1)}, u32[]{:S(2)}) copy-start(bf16[3,128,512]{2,1,0:T(8,128)(2,1)} %streams_ref.1) | copy-start | bytes 1179652
  1.6 0.9 %copy-start.2 = (bf16[128,512]{1,0:T(8,128)(2,1)S(1)}, bf16[128,512]{1,0:T(8,128)(2,1)}, u32[]{:S(2)}) copy-start(bf16[128,512]{1,0:T(8,128)(2,1)} %filters_ref.1) | copy-start | bytes 393220
  2.5 0.9 %copy-start.3 = (bf16[128,512]{1,0:T(8,128)(2,1)S(1)}, bf16[128,512]{1,0:T(8,128)(2,1)}, u32[]{:S(2)}) copy-start(bf16[128,512]{1,0:T(8,128)(2,1)} %cotangent_ref.1) | copy-start | bytes 393220
  3.4 0.8 %copy-start.4 = (f32[3,7,512]{2,1,0:T(8,128)S(1)}, f32[3,7,512]{2,1,0:T(8,128)}, u32[]{:S(2)}) copy-start(f32[3,7,512]{2,1,0:T(8,128)} %taps_ref.1) | copy-start | bytes 129028
  4.8 7.3 %collective-permute-start = (bf16[320,128]{1,0:T(8,128)(2,1)S(1)}, bf16[320,128]{1,0:T(8,128)(2,1)S(1)}, u32[]{:S(2)}, u32[]{:S(2)}) collective-permute-start(bf16[320,128]{1,0:T(8,128)(2,1)S(1)} %get-tuple-element.22), channel_id=1, source_target_pairs={{0,4},{4,8},{8,12},{12,16},{16,20},{20,24},{24,28},{28,0},{1,5},{5... | collective-permute-start | bytes 245768 | tf_op jit(solution)/shard_map/ppermute | solution.py:232
  6.3 12.4 %collective-permute-start.1 = (bf16[320,128]{1,0:T(8,128)(2,1)S(1)}, bf16[320,128]{1,0:T(8,128)(2,1)S(1)}, u32[]{:S(2)}, u32[]{:S(2)}) collective-permute-start(bf16[320,128]{1,0:T(8,128)(2,1)S(1)} %get-tuple-element.23), channel_id=1, source_target_pairs={{0,8},{4,12},{8,16},{12,20},{16,24},{20,28},{24,0},{28,4},{1,9},{5... | collective-permute-start | bytes 245768 | tf_op jit(solution)/shard_map/ppermute | solution.py:232
  6.6 12.1 %collective-permute-start.2 = (bf16[320,128]{1,0:T(8,128)(2,1)S(1)}, bf16[320,128]{1,0:T(8,128)(2,1)S(1)}, u32[]{:S(2)}, u32[]{:S(2)}) collective-permute-start(bf16[320,128]{1,0:T(8,128)(2,1)S(1)} %get-tuple-element.24), channel_id=1, source_target_pairs={{0,12},{4,16},{8,20},{12,24},{16,28},{20,0},{24,4},{28,8},{1,13},{... | collective-permute-start | bytes 245768 | tf_op jit(solution)/shard_map/ppermute | solution.py:232
  8.2 10.5 %collective-permute-start.3 = (bf16[320,128]{1,0:T(8,128)(2,1)S(1)}, bf16[320,128]{1,0:T(8,128)(2,1)S(1)}, u32[]{:S(2)}, u32[]{:S(2)}) collective-permute-start(bf16[320,128]{1,0:T(8,128)(2,1)S(1)} %get-tuple-element.25), channel_id=1, source_target_pairs={{0,16},{4,20},{8,24},{12,28},{16,0},{20,4},{24,8},{28,12},{1,17},{... | collective-permute-start | bytes 245768 | tf_op jit(solution)/shard_map/ppermute | solution.py:232
  10.8 7.9 %collective-permute-start.4 = (bf16[320,128]{1,0:T(8,128)(2,1)S(1)}, bf16[320,128]{1,0:T(8,128)(2,1)S(1)}, u32[]{:S(2)}, u32[]{:S(2)}) collective-permute-start(bf16[320,128]{1,0:T(8,128)(2,1)S(1)} %get-tuple-element.26), channel_id=1, source_target_pairs={{0,20},{4,24},{8,28},{12,0},{16,4},{20,8},{24,12},{28,16},{1,21},{... | collective-permute-start | bytes 245768 | tf_op jit(solution)/shard_map/ppermute | solution.py:232
  12.1 8.2 %collective-permute-start.5 = (bf16[320,128]{1,0:T(8,128)(2,1)S(1)}, bf16[320,128]{1,0:T(8,128)(2,1)S(1)}, u32[]{:S(2)}, u32[]{:S(2)}) collective-permute-start(bf16[320,128]{1,0:T(8,128)(2,1)S(1)} %get-tuple-element.27), channel_id=1, source_target_pairs={{0,24},{4,28},{8,0},{12,4},{16,8},{20,12},{24,16},{28,20},{1,25},{... | collective-permute-start | bytes 245768 | tf_op jit(solution)/shard_map/ppermute | solution.py:232
  18.7 5.3 %collective-permute-start.6 = (bf16[320,128]{1,0:T(8,128)(2,1)S(1)}, bf16[320,128]{1,0:T(8,128)(2,1)S(1)}, u32[]{:S(2)}, u32[]{:S(2)}) collective-permute-start(bf16[320,128]{1,0:T(8,128)(2,1)S(1)} %get-tuple-element.28), channel_id=1, source_target_pairs={{0,28},{4,0},{8,4},{12,8},{16,12},{20,16},{24,20},{28,24},{1,29},{... | collective-permute-start | bytes 245768 | tf_op jit(solution)/shard_map/ppermute | solution.py:232
  24.0 2.2 %copy-start = (bf16[2048,1024]{1,0:T(8,128)(2,1)S(1)}, bf16[2048,1024]{1,0:T(8,128)(2,1)}, u32[]{:S(2)}) copy-start(bf16[2048,1024]{1,0:T(8,128)(2,1)} %constant.4.clone.refs_9_) | copy-start | bytes 12582916
  31.6 5.9 %collective-permute-start.7 = (bf16[352,128]{1,0:T(8,128)(2,1)S(1)}, bf16[352,128]{1,0:T(8,128)(2,1)S(1)}, u32[]{:S(2)}, u32[]{:S(2)}) collective-permute-start(bf16[352,128]{1,0:T(8,128)(2,1)S(1)} %get-tuple-element.31), channel_id=1, source_target_pairs={{0,4},{4,8},{8,12},{12,16},{16,20},{20,24},{24,28},{28,0},{1,5},{5... | collective-permute-start | bytes 270344 | tf_op jit(solution)/shard_map/ppermute | solution.py:232
  31.7 13.7 %collective-permute-start.8 = (bf16[352,128]{1,0:T(8,128)(2,1)S(1)}, bf16[352,128]{1,0:T(8,128)(2,1)S(1)}, u32[]{:S(2)}, u32[]{:S(2)}) collective-permute-start(bf16[352,128]{1,0:T(8,128)(2,1)S(1)} %get-tuple-element.32), channel_id=1, source_target_pairs={{0,8},{4,12},{8,16},{12,20},{16,24},{20,28},{24,0},{28,4},{1,9},{5... | collective-permute-start | bytes 270344 | tf_op jit(solution)/shard_map/ppermute | solution.py:232
  31.8 15.9 %collective-permute-start.9 = (bf16[352,128]{1,0:T(8,128)(2,1)S(1)}, bf16[352,128]{1,0:T(8,128)(2,1)S(1)}, u32[]{:S(2)}, u32[]{:S(2)}) collective-permute-start(bf16[352,128]{1,0:T(8,128)(2,1)S(1)} %get-tuple-element.33), channel_id=1, source_target_pairs={{0,12},{4,16},{8,20},{12,24},{16,28},{20,0},{24,4},{28,8},{1,13},{... | collective-permute-start | bytes 270344 | tf_op jit(solution)/shard_map/ppermute | solution.py:232
  34.8 12.8 %collective-permute-start.10 = (bf16[352,128]{1,0:T(8,128)(2,1)S(1)}, bf16[352,128]{1,0:T(8,128)(2,1)S(1)}, u32[]{:S(2)}, u32[]{:S(2)}) collective-permute-start(bf16[352,128]{1,0:T(8,128)(2,1)S(1)} %get-tuple-element.34), channel_id=1, source_target_pairs={{0,16},{4,20},{8,24},{12,28},{16,0},{20,4},{24,8},{28,12},{1,17},{... | collective-permute-start | bytes 270344 | tf_op jit(solution)/shard_map/ppermute | solution.py:232
  36.1 11.5 %collective-permute-start.11 = (bf16[352,128]{1,0:T(8,128)(2,1)S(1)}, bf16[352,128]{1,0:T(8,128)(2,1)S(1)}, u32[]{:S(2)}, u32[]{:S(2)}) collective-permute-start(bf16[352,128]{1,0:T(8,128)(2,1)S(1)} %get-tuple-element.35), channel_id=1, source_target_pairs={{0,20},{4,24},{8,28},{12,0},{16,4},{20,8},{24,12},{28,16},{1,21},{... | collective-permute-start | bytes 270344 | tf_op jit(solution)/shard_map/ppermute | solution.py:232
  37.5 10.2 %collective-permute-start.12 = (bf16[352,128]{1,0:T(8,128)(2,1)S(1)}, bf16[352,128]{1,0:T(8,128)(2,1)S(1)}, u32[]{:S(2)}, u32[]{:S(2)}) collective-permute-start(bf16[352,128]{1,0:T(8,128)(2,1)S(1)} %get-tuple-element.36), channel_id=1, source_target_pairs={{0,24},{4,28},{8,0},{12,4},{16,8},{20,12},{24,16},{28,20},{1,25},{... | collective-permute-start | bytes 270344 | tf_op jit(solution)/shard_map/ppermute | solution.py:232
  45.3 5.4 %collective-permute-start.13 = (bf16[352,128]{1,0:T(8,128)(2,1)S(1)}, bf16[352,128]{1,0:T(8,128)(2,1)S(1)}, u32[]{:S(2)}, u32[]{:S(2)}) collective-permute-start(bf16[352,128]{1,0:T(8,128)(2,1)S(1)} %get-tuple-element.37), channel_id=1, source_target_pairs={{0,28},{4,0},{8,4},{12,8},{16,12},{20,16},{24,20},{28,24},{1,29},{... | collective-permute-start | bytes 270344 | tf_op jit(solution)/shard_map/ppermute | solution.py:232

commit v2 on v1

--- a/solution.py
+++ b/solution.py
@@ -27,6 +27,22 @@
     return high, back
 
 
+def step_offsets(count):
+    groups = count // 2
+    far = groups // 2
+    near = [g for g in range(1, groups) if g != far]
+    order = [(far, 0)] + [(g, 1) for g in near] + [(far, 1)] + [(g, 0) for g in near] + [(0, 1)]
+    return [(0, 0)] + [offset for offset in order if offset != (0, 0)]
+
+
+def partner(index, offset, sign, count):
+    group, member = offset
+    groups = count // 2
+    moved = (index // 2 + sign * group + groups) % groups
+    flipped = (index + member) % 2
+    return moved * 2 + flipped
+
+
 def lower_lanes(rows):
     return lax.broadcasted_iota(jnp.int32, (rows, LANES), 1) < HALF
 
@@ -45,15 +61,24 @@
     return jnp.where(low, left, right).astype(jnp.bfloat16)
 
 
-def pack_kernel(count, streams_ref, filters_ref, cotangent_ref, taps_ref, *out_refs):
+def pack_kernel(count, *refs):
+    in_hbm, out_refs = refs[:4], refs[4 : 5 + count]
+    held, sems = refs[5 + count : 9 + count], refs[9 + count]
+    copies = [pltpu.make_async_copy(here, there, sems.at[k]) for k, (here, there) in enumerate(zip(in_hbm, held))]
+    for copy in copies:
+        copy.start()
+    for copy in copies:
+        copy.wait()
+    streams_ref, filters_ref, cotangent_ref, taps_ref = held
     me = lax.axis_index("ctx")
+    offsets = step_offsets(count)
     rows = filters_ref.shape[0]
     half_rows = rows // 2
     tap_count = taps_ref.shape[1]
     low = lower_lanes(rows)
     low_half = lower_lanes(half_rows)
     for step in range(count):
-        owner = lax.rem(me + step, count)
+        owner = partner(me, offsets[step], 1, count)
         cols = pl.ds(pl.multiple_of(owner // 2 * LANES, LANES), LANES)
         odd = lax.rem(owner, 2) == 1
         out = out_refs[step]
@@ -79,6 +104,7 @@
     (raw_kv, raw_qc, conv_kv, conv_qc, signals, spectra, grad_kv, grad_q, lag_grad,
      table, back, sems) = refs[2 * count + 3 :]
     me = lax.axis_index("ctx")
+    offsets = step_offsets(count)
     total = signals.shape[0]
     rows = total // count
     half_rows = rows // 2
@@ -94,7 +120,7 @@
     grad_kv[total:, :] = jnp.zeros((EDGE, LANES), jnp.float32)
     grad_q[total:, :] = jnp.zeros((EDGE, LANES), jnp.float32)
     for step in range(count):
-        source = lax.rem(me - step + count, count)
+        source = partner(me, offsets[step], -1, count)
         base = pl.multiple_of(source * rows, rows)
         block = in_refs[step]
         raw_kv[pl.ds(base + EDGE, rows), :] = wide(block[0:rows, :])
@@ -156,7 +182,7 @@
     tap_sum_kv = [jnp.zeros((EDGE, LANES), jnp.float32)] * tap_count
     tap_sum_q = [jnp.zeros((EDGE, LANES), jnp.float32)] * tap_count
     for step in range(count):
-        owner = lax.rem(me + step, count)
+        owner = partner(me, offsets[step], 1, count)
         base = pl.multiple_of(owner * rows, rows)
         out = out_refs[step]
         stream_kv = jnp.zeros((rows, LANES), jnp.float32)
@@ -192,13 +218,14 @@
     gated_ref, stream_ref, lag_ref, tap_ref = refs[count : count + 4]
     blocks = refs[count + 4]
     me = lax.axis_index("ctx")
+    offsets = step_offsets(count)
     rows = gated_ref.shape[0]
     half_rows = rows // 2
     low = lower_lanes(rows)
     low_half = lower_lanes(half_rows)
     low_taps = lower_lanes(EDGE)
     for step in range(count):
-        owner = lax.rem(me - step + count, count)
+        owner = partner(me, offsets[step], -1, count)
         blocks[owner, :, :] = in_refs[step][...]
     for pair in range(count // 2):
         cols = slice(pair * LANES, (pair + 1) * LANES)
@@ -229,9 +256,13 @@
 def exchanged(blocks):
     count = len(blocks)
     return [blocks[0]] + [
-        lax.ppermute(blocks[step], "ctx", [(source, (source + step) % count) for source in range(count)])
-        for step in range(1, count)
+        lax.ppermute(block, "ctx", [(source, partner(source, offset, 1, count)) for source in range(count)])
+        for block, offset in zip(blocks[1:], step_offsets(count)[1:])
     ]
+
+
+def in_hbm(array):
+    return pltpu.with_memory_space_constraint(array, pltpu.HBM)
 
 
 def in_vmem(count):
@@ -249,11 +280,13 @@
         functools.partial(pack_kernel, count),
         out_shape=[jax.ShapeDtypeStruct((sent_rows, LANES), jnp.bfloat16)] * count
         + [jax.ShapeDtypeStruct((2 * EDGE, LANES), jnp.float32)],
-        in_specs=in_vmem(4),
+        in_specs=[pl.BlockSpec(memory_space=pltpu.HBM)] * 4,
         out_specs=in_vmem(count + 1),
+        scratch_shapes=[pltpu.VMEM(a.shape, a.dtype) for a in (streams, filters, cotangent, taps)]
+        + [pltpu.SemaphoreType.DMA((4,))],
         compiler_params=params,
         name="pack",
-    )(streams, filters, cotangent, taps)
+    )(*[in_hbm(a) for a in (streams, filters, cotangent, taps)])
     arrived = exchanged(packed[:count])
     table, back = odd_tables(total)
     back_rows = sent_rows + TAP_ROWS
@@ -261,7 +294,7 @@
     made = pl.pallas_call(
         functools.partial(main_kernel, count, tap_count, 1.0 / math.sqrt(total)),
         out_shape=[jax.ShapeDtypeStruct((back_rows, LANES), jnp.bfloat16)] * count,
-        in_specs=in_vmem(count + 1) + [pl.BlockSpec(memory_space=pl.ANY)] * 2,
+        in_specs=in_vmem(count + 1) + [pl.BlockSpec(memory_space=pltpu.HBM)] * 2,
         out_specs=in_vmem(count),
         scratch_shapes=[
             f32_rows(total + EDGE), f32_rows(total + EDGE), f32_rows(total), f32_rows(total),
@@ -272,7 +305,7 @@
         ],
         compiler_params=params,
         name="channels",
-    )(*arrived, packed[count], jnp.asarray(table), jnp.asarray(back))
+    )(*arrived, packed[count], in_hbm(jnp.asarray(table)), in_hbm(jnp.asarray(back)))
     returned = exchanged(made)
     return tuple(
         pl.pallas_call(

time: 52.2 us -> 47.5 us (0.910)
  the two profiles are of different devices: /device:TPU:22 before, /device:TPU:0 now
where the time goes in v2:
time: 47.5 us; the launch traced here: 47.4 us
  starting transfers between devices  26.9 us (57%)
  waiting for transfers between devices  10.5 us (22%)
  Pallas kernels  9.24 us (19%)
  between operations  0.67 us (1%)
    ppermute x14, starting transfers between devices, exchanged(): lax.ppermute(block, 'ctx', [(source, partner(source, offset, 1, count)) f...  26.9 us
    ppermute x14, waiting for transfers between devices, exchanged(): lax.ppermute(block, 'ctx', [(source, partner(source, offset, 1, count)) f...  10.5 us
    pallas_call x1, Pallas kernels, local_dense(): pl.pallas_call(functools.partial(main_kernel, count, tap_count, 1.0 / mat...  6.44 us
    pallas_call x1, Pallas kernels, local_dense(): pl.pallas_call(functools.partial(pack_kernel, count), out_shape=[jax.Shap...  1.64 us
    pallas_call x1, Pallas kernels, local_dense(): pl.pallas_call(functools.partial(unpack_kernel, count, tap_count), out_sh...  1.15 us
  transfers between devices with their start and end apart: 14, of which 3 were waited for; matrix products, arithmetic and copies ran while one was open for 0% of the time, Pallas kernels for 0%

profile of v2, /device:TPU:0, one launch (start us, length us, event | category | flops | bytes accessed | tf_op | source)
XLA Modules:
  0.0 47.4 jit_solution(8844564253733252585)
XLA Ops:
  0.6 1.6 %pack.1 = (bf16[320,128]{1,0:T(8,128)(2,1)S(1)}, bf16[320,128]{1,0:T(8,128)(2,1)S(1)}, bf16[320,128]{1,0:T(8,128)(2,1)S(1)}, bf16[320,128]{1,0:T(8,128)(2,1)S(1)...) custom-call(bf16[3,128,512]{2,1,0:T(8,128)(2,1)} %refs_0_.1, ...), custom_call_target="tpu_custom_call" | custom-call | tf_op jit(solution)/shard_map/pack/pallas_call | solution.py:279
  2.3 4.1 %collective-permute-start = (bf16[320,128]{1,0:T(8,128)(2,1)S(1)}, bf16[320,128]{1,0:T(8,128)(2,1)S(1)}, u32[]{:S(2)}, u32[]{:S(2)}) collective-permute-start(bf16[320,128]{1,0:T(8,128)(2,1)S(1)} %get-tuple-element.22), channel_id=1, source_target_pairs={{0,16},{4,20},{8,24},{12,28},{16,0},{20,4},{24,8},{28,12},{1,17},{... | collective-permute-start | bytes 245768 | tf_op jit(solution)/shard_map/ppermute | solution.py:259
  6.4 2.5 %collective-permute-start.1 = (bf16[320,128]{1,0:T(8,128)(2,1)S(1)}, bf16[320,128]{1,0:T(8,128)(2,1)S(1)}, u32[]{:S(2)}, u32[]{:S(2)}) collective-permute-start(bf16[320,128]{1,0:T(8,128)(2,1)S(1)} %get-tuple-element.23), channel_id=1, source_target_pairs={{0,12},{4,8},{8,20},{12,16},{16,28},{20,24},{24,4},{28,0},{1,13},{... | collective-permute-start | bytes 245768 | tf_op jit(solution)/shard_map/ppermute | solution.py:259
  8.9 2.2 %collective-permute-start.2 = (bf16[320,128]{1,0:T(8,128)(2,1)S(1)}, bf16[320,128]{1,0:T(8,128)(2,1)S(1)}, u32[]{:S(2)}, u32[]{:S(2)}) collective-permute-start(bf16[320,128]{1,0:T(8,128)(2,1)S(1)} %get-tuple-element.24), channel_id=1, source_target_pairs={{0,28},{4,24},{8,4},{12,0},{16,12},{20,8},{24,20},{28,16},{1,29},{... | collective-permute-start | bytes 245768 | tf_op jit(solution)/shard_map/ppermute | solution.py:259
  11.1 0.0 collective-permute-start.3
  11.1 1.1 %collective-permute-start.4 = (bf16[320,128]{1,0:T(8,128)(2,1)S(1)}, bf16[320,128]{1,0:T(8,128)(2,1)S(1)}, u32[]{:S(2)}, u32[]{:S(2)}) collective-permute-start(bf16[320,128]{1,0:T(8,128)(2,1)S(1)} %get-tuple-element.26), channel_id=1, source_target_pairs={{0,8},{4,12},{8,16},{12,20},{16,24},{20,28},{24,0},{28,4},{1,9},{5... | collective-permute-start | bytes 245768 | tf_op jit(solution)/shard_map/ppermute | solution.py:259
  12.2 0.0 collective-permute-done.refs_1_
  12.2 2.8 %collective-permute-start.5 = (bf16[320,128]{1,0:T(8,128)(2,1)S(1)}, bf16[320,128]{1,0:T(8,128)(2,1)S(1)}, u32[]{:S(2)}, u32[]{:S(2)}) collective-permute-start(bf16[320,128]{1,0:T(8,128)(2,1)S(1)} %get-tuple-element.27), channel_id=1, source_target_pairs={{0,24},{4,28},{8,0},{12,4},{16,8},{20,12},{24,16},{28,20},{1,25},{... | collective-permute-start | bytes 245768 | tf_op jit(solution)/shard_map/ppermute | solution.py:259
  14.9 0.0 collective-permute-done.1.refs_2_
  14.9 1.5 %collective-permute-start.6 = (bf16[320,128]{1,0:T(8,128)(2,1)S(1)}, bf16[320,128]{1,0:T(8,128)(2,1)S(1)}, u32[]{:S(2)}, u32[]{:S(2)}) collective-permute-start(bf16[320,128]{1,0:T(8,128)(2,1)S(1)} %get-tuple-element.28), channel_id=1, source_target_pairs={{0,4},{4,0},{8,12},{12,8},{16,20},{20,16},{24,28},{28,24},{1,5},{5... | collective-permute-start | bytes 245768 | tf_op jit(solution)/shard_map/ppermute | solution.py:259
  16.5 0.0 collective-permute-done.2.refs_3_
  16.5 4.7 %collective-permute-done.3.refs_4_ = bf16[320,128]{1,0:T(8,128)(2,1)S(1)} collective-permute-done((bf16[320,128]{1,0:T(8,128)(2,1)S(1)}, bf16[320,128]{1,0:T(8,128)(2,1)S(1)}, u32[]{:S(2)}, u32[]{:S(2)}) %collective-permute-start.3) | collective-permute-done | bytes 81952 | tf_op jit(solution)/shard_map/ppermute | solution.py:259
  21.1 0.0 collective-permute-done.4.refs_5_
  21.1 0.0 collective-permute-done.5.refs_6_
  21.1 0.0 collective-permute-done.6.refs_7_
  21.1 6.4 %channels.1 = (bf16[352,128]{1,0:T(8,128)(2,1)S(1)}, bf16[352,128]{1,0:T(8,128)(2,1)S(1)}, bf16[352,128]{1,0:T(8,128)(2,1)S(1)}, bf16[352,128]{1,0:T(8,128)(2,1)...) custom-call(bf16[320,128]{1,0:T(8,128)(2,1)S(1)} %get-tuple-element., ...), custom_call_target="tpu_custom_call" | custom-call | tf_op jit(solution)/shard_map/channels/pallas_call | solution.py:294
  27.6 4.0 %collective-permute-start.7 = (bf16[352,128]{1,0:T(8,128)(2,1)S(1)}, bf16[352,128]{1,0:T(8,128)(2,1)S(1)}, u32[]{:S(2)}, u32[]{:S(2)}) collective-permute-start(bf16[352,128]{1,0:T(8,128)(2,1)S(1)} %get-tuple-element.31), channel_id=1, source_target_pairs={{0,16},{4,20},{8,24},{12,28},{16,0},{20,4},{24,8},{28,12},{1,17},{... | collective-permute-start | bytes 270344 | tf_op jit(solution)/shard_map/ppermute | solution.py:259
  31.5 0.0 collective-permute-start.8
  31.5 4.7 %collective-permute-start.9 = (bf16[352,128]{1,0:T(8,128)(2,1)S(1)}, bf16[352,128]{1,0:T(8,128)(2,1)S(1)}, u32[]{:S(2)}, u32[]{:S(2)}) collective-permute-start(bf16[352,128]{1,0:T(8,128)(2,1)S(1)} %get-tuple-element.33), channel_id=1, source_target_pairs={{0,28},{4,24},{8,4},{12,0},{16,12},{20,8},{24,20},{28,16},{1,29},{... | collective-permute-start | bytes 270344 | tf_op jit(solution)/shard_map/ppermute | solution.py:259
  36.3 0.0 collective-permute-start.10
  36.3 0.6 %collective-permute-start.11 = (bf16[352,128]{1,0:T(8,128)(2,1)S(1)}, bf16[352,128]{1,0:T(8,128)(2,1)S(1)}, u32[]{:S(2)}, u32[]{:S(2)}) collective-permute-start(bf16[352,128]{1,0:T(8,128)(2,1)S(1)} %get-tuple-element.35), channel_id=1, source_target_pairs={{0,8},{4,12},{8,16},{12,20},{16,24},{20,28},{24,0},{28,4},{1,9},{5... | collective-permute-start | bytes 270344 | tf_op jit(solution)/shard_map/ppermute | solution.py:259
  36.8 0.0 collective-permute-done.7.refs_1_
  36.8 3.3 %collective-permute-start.12 = (bf16[352,128]{1,0:T(8,128)(2,1)S(1)}, bf16[352,128]{1,0:T(8,128)(2,1)S(1)}, u32[]{:S(2)}, u32[]{:S(2)}) collective-permute-start(bf16[352,128]{1,0:T(8,128)(2,1)S(1)} %get-tuple-element.36), channel_id=1, source_target_pairs={{0,24},{4,28},{8,0},{12,4},{16,8},{20,12},{24,16},{28,20},{1,25},{... | collective-permute-start | bytes 270344 | tf_op jit(solution)/shard_map/ppermute | solution.py:259
  40.1 0.0 collective-permute-done.8.refs_2_
  40.1 0.3 collective-permute-start.13
  40.4 0.0 collective-permute-done.9.refs_3_
  40.4 5.5 %collective-permute-done.10.refs_4_ = bf16[352,128]{1,0:T(8,128)(2,1)S(1)} collective-permute-done((bf16[352,128]{1,0:T(8,128)(2,1)S(1)}, bf16[352,128]{1,0:T(8,128)(2,1)S(1)}, u32[]{:S(2)}, u32[]{:S(2)}) %collective-permute-start.10) | collective-permute-done | bytes 90144 | tf_op jit(solution)/shard_map/ppermute | solution.py:259
  45.8 0.0 collective-permute-done.11.refs_5_
  45.9 0.0 collective-permute-done.12.refs_6_
  45.9 0.3 collective-permute-done.13.refs_7_
  46.2 1.2 %unpack.1 = (bf16[128,512]{1,0:T(8,128)(2,1)}, bf16[3,128,512]{2,1,0:T(8,128)(2,1)}, bf16[128,512]{1,0:T(8,128)(2,1)}, f32[3,7,512]{2,1,0:T(8,128)}) custom-call(bf16[352,128]{1,0:T(8,128)(2,1)S(1)} %get-tuple-element.30.refs_0_, bf16[352,128]{1,0:T(8,128)(2,1)S(1)} %collective-permute-done.7.refs_1_, bf16[352,128]{1,0:T(8,128)(2,1)S(1)} %collective-permute-done.8.refs_2_, ...), custom_call_target="tpu_custom_call" | custom-call | tf_op jit(solution)/shard_map/unpack/pallas_call | solution.py:311
Async XLA Ops:
  2.3 9.9 %collective-permute-start = (bf16[320,128]{1,0:T(8,128)(2,1)S(1)}, bf16[320,128]{1,0:T(8,128)(2,1)S(1)}, u32[]{:S(2)}, u32[]{:S(2)}) collective-permute-start(bf16[320,128]{1,0:T(8,128)(2,1)S(1)} %get-tuple-element.22), channel_id=1, source_target_pairs={{0,16},{4,20},{8,24},{12,28},{16,0},{20,4},{24,8},{28,12},{1,17},{... | collective-permute-start | bytes 245768 | tf_op jit(solution)/shard_map/ppermute | solution.py:259
  6.4 8.6 %collective-permute-start.1 = (bf16[320,128]{1,0:T(8,128)(2,1)S(1)}, bf16[320,128]{1,0:T(8,128)(2,1)S(1)}, u32[]{:S(2)}, u32[]{:S(2)}) collective-permute-start(bf16[320,128]{1,0:T(8,128)(2,1)S(1)} %get-tuple-element.23), channel_id=1, source_target_pairs={{0,12},{4,8},{8,20},{12,16},{16,28},{20,24},{24,4},{28,0},{1,13},{... | collective-permute-start | bytes 245768 | tf_op jit(solution)/shard_map/ppermute | solution.py:259
  8.9 7.5 %collective-permute-start.2 = (bf16[320,128]{1,0:T(8,128)(2,1)S(1)}, bf16[320,128]{1,0:T(8,128)(2,1)S(1)}, u32[]{:S(2)}, u32[]{:S(2)}) collective-permute-start(bf16[320,128]{1,0:T(8,128)(2,1)S(1)} %get-tuple-element.24), channel_id=1, source_target_pairs={{0,28},{4,24},{8,4},{12,0},{16,12},{20,8},{24,20},{28,16},{1,29},{... | collective-permute-start | bytes 245768 | tf_op jit(solution)/shard_map/ppermute | solution.py:259
  11.1 10.0 %collective-permute-start.3 = (bf16[320,128]{1,0:T(8,128)(2,1)S(1)}, bf16[320,128]{1,0:T(8,128)(2,1)S(1)}, u32[]{:S(2)}, u32[]{:S(2)}) collective-permute-start(bf16[320,128]{1,0:T(8,128)(2,1)S(1)} %get-tuple-element.25), channel_id=1, source_target_pairs={{0,20},{4,16},{8,28},{12,24},{16,4},{20,0},{24,12},{28,8},{1,21},{... | collective-permute-start | bytes 245768 | tf_op jit(solution)/shard_map/ppermute | solution.py:259
  11.1 10.0 %collective-permute-start.4 = (bf16[320,128]{1,0:T(8,128)(2,1)S(1)}, bf16[320,128]{1,0:T(8,128)(2,1)S(1)}, u32[]{:S(2)}, u32[]{:S(2)}) collective-permute-start(bf16[320,128]{1,0:T(8,128)(2,1)S(1)} %get-tuple-element.26), channel_id=1, source_target_pairs={{0,8},{4,12},{8,16},{12,20},{16,24},{20,28},{24,0},{28,4},{1,9},{5... | collective-permute-start | bytes 245768 | tf_op jit(solution)/shard_map/ppermute | solution.py:259
  12.2 8.9 %collective-permute-start.5 = (bf16[320,128]{1,0:T(8,128)(2,1)S(1)}, bf16[320,128]{1,0:T(8,128)(2,1)S(1)}, u32[]{:S(2)}, u32[]{:S(2)}) collective-permute-start(bf16[320,128]{1,0:T(8,128)(2,1)S(1)} %get-tuple-element.27), channel_id=1, source_target_pairs={{0,24},{4,28},{8,0},{12,4},{16,8},{20,12},{24,16},{28,20},{1,25},{... | collective-permute-start | bytes 245768 | tf_op jit(solution)/shard_map/ppermute | solution.py:259
  14.9 6.2 %collective-permute-start.6 = (bf16[320,128]{1,0:T(8,128)(2,1)S(1)}, bf16[320,128]{1,0:T(8,128)(2,1)S(1)}, u32[]{:S(2)}, u32[]{:S(2)}) collective-permute-start(bf16[320,128]{1,0:T(8,128)(2,1)S(1)} %get-tuple-element.28), channel_id=1, source_target_pairs={{0,4},{4,0},{8,12},{12,8},{16,20},{20,16},{24,28},{28,24},{1,5},{5... | collective-permute-start | bytes 245768 | tf_op jit(solution)/shard_map/ppermute | solution.py:259
  27.6 9.2 %collective-permute-start.7 = (bf16[352,128]{1,0:T(8,128)(2,1)S(1)}, bf16[352,128]{1,0:T(8,128)(2,1)S(1)}, u32[]{:S(2)}, u32[]{:S(2)}) collective-permute-start(bf16[352,128]{1,0:T(8,128)(2,1)S(1)} %get-tuple-element.31), channel_id=1, source_target_pairs={{0,16},{4,20},{8,24},{12,28},{16,0},{20,4},{24,8},{28,12},{1,17},{... | collective-permute-start | bytes 270344 | tf_op jit(solution)/shard_map/ppermute | solution.py:259
  31.5 8.6 %collective-permute-start.8 = (bf16[352,128]{1,0:T(8,128)(2,1)S(1)}, bf16[352,128]{1,0:T(8,128)(2,1)S(1)}, u32[]{:S(2)}, u32[]{:S(2)}) collective-permute-start(bf16[352,128]{1,0:T(8,128)(2,1)S(1)} %get-tuple-element.32), channel_id=1, source_target_pairs={{0,12},{4,8},{8,20},{12,16},{16,28},{20,24},{24,4},{28,0},{1,13},{... | collective-permute-start | bytes 270344 | tf_op jit(solution)/shard_map/ppermute | solution.py:259
  31.5 8.8 %collective-permute-start.9 = (bf16[352,128]{1,0:T(8,128)(2,1)S(1)}, bf16[352,128]{1,0:T(8,128)(2,1)S(1)}, u32[]{:S(2)}, u32[]{:S(2)}) collective-permute-start(bf16[352,128]{1,0:T(8,128)(2,1)S(1)} %get-tuple-element.33), channel_id=1, source_target_pairs={{0,28},{4,24},{8,4},{12,0},{16,12},{20,8},{24,20},{28,16},{1,29},{... | collective-permute-start | bytes 270344 | tf_op jit(solution)/shard_map/ppermute | solution.py:259
  36.3 9.6 %collective-permute-start.10 = (bf16[352,128]{1,0:T(8,128)(2,1)S(1)}, bf16[352,128]{1,0:T(8,128)(2,1)S(1)}, u32[]{:S(2)}, u32[]{:S(2)}) collective-permute-start(bf16[352,128]{1,0:T(8,128)(2,1)S(1)} %get-tuple-element.34), channel_id=1, source_target_pairs={{0,20},{4,16},{8,28},{12,24},{16,4},{20,0},{24,12},{28,8},{1,21},{... | collective-permute-start | bytes 270344 | tf_op jit(solution)/shard_map/ppermute | solution.py:259
  36.3 9.6 %collective-permute-start.11 = (bf16[352,128]{1,0:T(8,128)(2,1)S(1)}, bf16[352,128]{1,0:T(8,128)(2,1)S(1)}, u32[]{:S(2)}, u32[]{:S(2)}) collective-permute-start(bf16[352,128]{1,0:T(8,128)(2,1)S(1)} %get-tuple-element.35), channel_id=1, source_target_pairs={{0,8},{4,12},{8,16},{12,20},{16,24},{20,28},{24,0},{28,4},{1,9},{5... | collective-permute-start | bytes 270344 | tf_op jit(solution)/shard_map/ppermute | solution.py:259
  36.8 9.0 %collective-permute-start.12 = (bf16[352,128]{1,0:T(8,128)(2,1)S(1)}, bf16[352,128]{1,0:T(8,128)(2,1)S(1)}, u32[]{:S(2)}, u32[]{:S(2)}) collective-permute-start(bf16[352,128]{1,0:T(8,128)(2,1)S(1)} %get-tuple-element.36), channel_id=1, source_target_pairs={{0,24},{4,28},{8,0},{12,4},{16,8},{20,12},{24,16},{28,20},{1,25},{... | collective-permute-start | bytes 270344 | tf_op jit(solution)/shard_map/ppermute | solution.py:259
  40.1 6.1 %collective-permute-start.13 = (bf16[352,128]{1,0:T(8,128)(2,1)S(1)}, bf16[352,128]{1,0:T(8,128)(2,1)S(1)}, u32[]{:S(2)}, u32[]{:S(2)}) collective-permute-start(bf16[352,128]{1,0:T(8,128)(2,1)S(1)} %get-tuple-element.37), channel_id=1, source_target_pairs={{0,4},{4,0},{8,12},{12,8},{16,20},{20,16},{24,28},{28,24},{1,5},{5... | collective-permute-start | bytes 270344 | tf_op jit(solution)/shard_map/ppermute | solution.py:259

commit v3 on v2

--- a/solution.py
+++ b/solution.py
@@ -12,26 +12,18 @@
 exact_mode = lax.Precision.HIGHEST
 LANES = 128
 HALF = LANES // 2
+PHASES = 4
 EDGE = 8
-TAP_ROWS = 32
 TABLE_BYTES = 16 * 1024 * 1024
-VMEM_BYTES = 48 * 1024 * 1024
-
-
-def odd_tables(total):
-    freq = 2 * np.arange(total)[:, None] + 1
-    angles = (freq * np.arange(total)[None, :] % (4 * total)) * (math.pi / (2 * total))
-    table = np.concatenate([np.cos(angles), -np.sin(angles)])
-    high = table.astype(jnp.bfloat16)
-    back = np.ascontiguousarray(table.T / total).astype(jnp.bfloat16)
-    return high, back
+VMEM_BYTES = 32 * 1024 * 1024
 
 
 def step_offsets(count):
     groups = count // 2
     far = groups // 2
     near = [g for g in range(1, groups) if g != far]
-    order = [(far, 0)] + [(g, 1) for g in near] + [(far, 1)] + [(g, 0) for g in near] + [(0, 1)]
+    order = [(g, 0) for g in near[:1]] + [(far, 0), (far, 1)] + [(g, 1) for g in near]
+    order = order + [(0, 1)] + [(g, 0) for g in near[1:]]
     return [(0, 0)] + [offset for offset in order if offset != (0, 0)]
 
 
@@ -97,23 +89,48 @@
     tap_out[EDGE : EDGE + tap_count, :] = jnp.where(low_taps, here[0], jnp.where(first_tap, 1.0, 0.0))
 
 
+def phase_tables(total):
+    quarter = total // PHASES
+    freq = 2 * np.arange(quarter)[:, None] + 1
+    ahead, back = [], []
+    for phase in range(PHASES):
+        place = PHASES * np.arange(quarter)[None, :] + phase
+        angles = (freq * place % (4 * total)) * (math.pi / (2 * total))
+        table = np.concatenate([np.cos(angles), -np.sin(angles)])
+        ahead.append(table)
+        back.append(table.T / total)
+    ahead = np.stack(ahead)
+    high = ahead.astype(jnp.bfloat16)
+    rest = (ahead - high.astype(np.float64)).astype(jnp.bfloat16)
+    return high, rest, np.stack(back).astype(jnp.bfloat16)
+
+
+def quarter_turns(parts):
+    (r0, i0), (r1, i1), (r2, i2), (r3, i3) = parts
+    even_r, even_i, odd_r, odd_i = r0 + r2, i0 + i2, r1 + r3, i1 + i3
+    gap_r, gap_i, side_r, side_i = r0 - r2, i0 - i2, r1 - r3, i1 - i3
+    return [
+        (even_r + odd_r, even_i + odd_i),
+        (gap_r - side_i, gap_i + side_r),
+        (even_r - odd_r, even_i - odd_i),
+        (gap_r + side_i, gap_i - side_r),
+    ]
+
+
 def main_kernel(count, tap_count, scale, *refs):
     in_refs = refs[:count]
-    tap_ref, table_hbm, back_hbm = refs[count : count + 3]
-    out_refs = refs[count + 3 : 2 * count + 3]
-    (raw_kv, raw_qc, conv_kv, conv_qc, signals, spectra, grad_kv, grad_q, lag_grad,
-     table, back, sems) = refs[2 * count + 3 :]
+    tap_ref, high, rest, back = refs[count : count + 4]
+    out_refs = refs[count + 4 : 2 * count + 4]
+    (raw_kv, raw_qc, raw_lag, conv_kv, conv_qc, signals, phased, spectra, pairs, grad_kv, grad_q, lag_grad) = refs[
+        2 * count + 4 :
+    ]
     me = lax.axis_index("ctx")
     offsets = step_offsets(count)
-    total = signals.shape[0]
+    total = raw_lag.shape[0]
+    quarter = total // PHASES
     rows = total // count
     half_rows = rows // 2
-    low = lower_lanes(rows)
     low_half = lower_lanes(half_rows)
-    table_copy = pltpu.make_async_copy(table_hbm, table, sems.at[0])
-    back_copy = pltpu.make_async_copy(back_hbm, back, sems.at[1])
-    table_copy.start()
-    back_copy.start()
 
     raw_kv[0:EDGE, :] = jnp.zeros((EDGE, LANES), jnp.float32)
     raw_qc[0:EDGE, :] = jnp.zeros((EDGE, LANES), jnp.float32)
@@ -127,130 +144,181 @@
         raw_qc[pl.ds(base + EDGE, rows), :] = wide(block[rows : 2 * rows, :])
         lag_block = wide(block[2 * rows :, :])
         other = turned(lag_block)
-        signals[pl.ds(base, half_rows), LANES:] = jnp.where(low_half, lag_block, other).astype(jnp.bfloat16)
-        signals[pl.ds(base + half_rows, half_rows), LANES:] = jnp.where(low_half, other, lag_block).astype(jnp.bfloat16)
+        raw_lag[pl.ds(base, half_rows), :] = jnp.where(low_half, lag_block, other)
+        raw_lag[pl.ds(base + half_rows, half_rows), :] = jnp.where(low_half, other, lag_block)
 
     tap_kv = [tap_ref[j : j + 1, :] for j in range(tap_count)]
     tap_q = [tap_ref[EDGE + j : EDGE + j + 1, :] for j in range(tap_count)]
 
-    for block in range(count):
-        base = block * rows
-        key_value = jnp.zeros((rows, LANES), jnp.float32)
-        query_cot = jnp.zeros((rows, LANES), jnp.float32)
-        for j in range(tap_count):
-            window = slice(base + EDGE - j, base + EDGE - j + rows)
-            key_value = key_value + tap_kv[j] * raw_kv[window, :]
-            query_cot = query_cot + tap_q[j] * raw_qc[window, :]
-        conv_kv[base : base + rows, :] = key_value
-        conv_qc[base : base + rows, :] = query_cot
-        product = key_value * turned(key_value)
-        mixed_grad = query_cot * turned(query_cot)
-        signals[base : base + rows, :LANES] = jnp.where(low, product, mixed_grad).astype(jnp.bfloat16)
-
-    table_copy.wait()
-    part = min(256, total)
-    low_part = lower_lanes(part)
-    for start in range(0, total, part):
-        real = jnp.dot(table[start : start + part, :], signals[...], preferred_element_type=jnp.float32)
-        imag = jnp.dot(
-            table[total + start : total + start + part, :], signals[...], preferred_element_type=jnp.float32
+    part = min(32, quarter)
+    low = lower_lanes(part)
+    for start in range(0, quarter, part):
+        for phase in range(PHASES):
+            first = PHASES * start + phase
+            here = slice(phase * quarter + start, phase * quarter + start + part)
+            key_value = jnp.zeros((part, LANES), jnp.float32)
+            query_cot = jnp.zeros((part, LANES), jnp.float32)
+            for j in range(tap_count):
+                window = pl.ds(first + EDGE - j, part, stride=PHASES)
+                key_value = key_value + tap_kv[j] * raw_kv[window, :]
+                query_cot = query_cot + tap_q[j] * raw_qc[window, :]
+            conv_kv[here, :] = key_value
+            conv_qc[here, :] = query_cot
+            product = key_value * turned(key_value)
+            mixed_grad = query_cot * turned(query_cot)
+            signals[here, :LANES] = jnp.where(low, product, mixed_grad).astype(jnp.bfloat16)
+            signals[here, LANES:] = raw_lag[pl.ds(first, part, stride=PHASES), :].astype(jnp.bfloat16)
+
+    for phase in range(PHASES):
+        signal = signals[phase * quarter : (phase + 1) * quarter, :]
+        phased[phase, :, :] = jnp.dot(high[phase], signal, preferred_element_type=jnp.float32) + jnp.dot(
+            rest[phase], signal, preferred_element_type=jnp.float32
         )
-        a_re, b_re = real[:, :LANES], real[:, LANES:]
-        a_im, b_im = imag[:, :LANES], imag[:, LANES:]
-        b_im = jnp.where(low_part, b_im, -b_im)
-        r_re, r_im = turned(a_re), turned(a_im)
-        spectra[start : start + part, :LANES] = (a_re * b_re - a_im * b_im).astype(jnp.bfloat16)
-        spectra[start : start + part, LANES:] = (a_re * r_re + a_im * r_im).astype(jnp.bfloat16)
-        spectra[total + start : total + start + part, :LANES] = (a_re * b_im + a_im * b_re).astype(jnp.bfloat16)
-        spectra[total + start : total + start + part, LANES:] = (a_re * r_im - a_im * r_re).astype(jnp.bfloat16)
-
-    back_copy.wait()
-    for block in range(count):
-        base = block * rows
-        here = slice(base, base + rows)
-        result = jnp.dot(back[here, :], spectra[...], preferred_element_type=jnp.float32)
+
+    part = min(16, quarter)
+    low = lower_lanes(part)
+    for start in range(0, quarter, part):
+        real, imag = slice(start, start + part), slice(quarter + start, quarter + start + part)
+        signal_turns = quarter_turns([(phased[p, real, :LANES], phased[p, imag, :LANES]) for p in range(PHASES)])
+        lag_turns = quarter_turns([(phased[p, real, LANES:], phased[p, imag, LANES:]) for p in range(PHASES)])
+        through, lagged = [], []
+        for (a_re, a_im), (b_re, b_im) in zip(signal_turns, lag_turns):
+            b_im = jnp.where(low, b_im, -b_im)
+            r_re, r_im = turned(a_re), turned(a_im)
+            through.append((a_re * b_re - a_im * b_im, a_re * b_im + a_im * b_re))
+            lagged.append((a_re * r_re + a_im * r_im, a_re * r_im - a_im * r_re))
+        for cols, parts in ((slice(0, LANES), through), (slice(LANES, 2 * LANES), lagged)):
+            turns = quarter_turns(parts)
+            for phase in range(PHASES):
+                value_re, value_im = turns[-phase % PHASES]
+                spectra[phase, real, cols] = value_re.astype(jnp.bfloat16)
+                spectra[phase, imag, cols] = value_im.astype(jnp.bfloat16)
+
+    low = lower_lanes(quarter)
+    for phase in range(PHASES):
+        here = slice(phase * quarter, (phase + 1) * quarter)
+        spread = pl.ds(phase, quarter, stride=PHASES)
+        result = jnp.dot(back[phase], spectra[phase], preferred_element_type=jnp.float32)
         pair = wide(result[:, :LANES].astype(jnp.bfloat16))
         other = turned(pair)
-        gated_grad = conv_qc[here, :] * jnp.where(low, pair, other)
-        grad_q[here, :] = turned(gated_grad)
-        grad_kv[here, :] = jnp.where(low, other, pair) * turned(conv_kv[here, :])
-        lag_terms = result[:, LANES:] * scale
-        lag_grad[block * half_rows : (block + 1) * half_rows, :] = jnp.where(
-            low_half, lag_terms[:half_rows], turned(lag_terms[half_rows:])
-        )
+        pairs[spread, :] = pair
+        grad_q[spread, :] = turned(conv_qc[here, :]) * jnp.where(low, pair, other)
+        grad_kv[spread, :] = jnp.where(low, other, pair) * turned(conv_kv[here, :])
+        lag_grad[spread, :] = result[:, LANES:] * scale
 
     tap_sum_kv = [jnp.zeros((EDGE, LANES), jnp.float32)] * tap_count
     tap_sum_q = [jnp.zeros((EDGE, LANES), jnp.float32)] * tap_count
+    part = min(32, rows)
+    for base in range(0, total, part):
+        kv = grad_kv[base : base + part, :]
+        q = grad_q[base : base + part, :]
+        for j in range(tap_count):
+            window = slice(base + EDGE - j, base + EDGE - j + part)
+            tap_sum_kv[j] = tap_sum_kv[j] + jnp.sum((kv * raw_kv[window, :]).reshape(part // EDGE, EDGE, LANES), axis=0)
+            tap_sum_q[j] = tap_sum_q[j] + jnp.sum((q * raw_qc[window, :]).reshape(part // EDGE, EDGE, LANES), axis=0)
+    spare = [jnp.zeros((1, LANES), jnp.float32)] * (EDGE - tap_count)
+    sums = [
+        jnp.concatenate([jnp.sum(s, axis=0, keepdims=True) for s in parts] + spare, axis=0) * scale
+        for parts in (tap_sum_kv, tap_sum_q)
+    ]
+    sums_high = [wide(s.astype(jnp.bfloat16)) for s in sums]
+    low_edge = lower_lanes(EDGE)
+    sums_q = jnp.where(low_edge, sums_high[1], turned(sums[1] - sums_high[1]))
     for step in range(count):
         owner = partner(me, offsets[step], 1, count)
         base = pl.multiple_of(owner * rows, rows)
         out = out_refs[step]
-        stream_kv = jnp.zeros((rows, LANES), jnp.float32)
-        stream_q = jnp.zeros((rows, LANES), jnp.float32)
-        for j in range(tap_count):
-            stream_kv = stream_kv + tap_kv[j] * grad_kv[pl.ds(base + j, rows), :]
-            stream_q = stream_q + tap_q[j] * grad_q[pl.ds(base + j, rows), :]
-        out[0:rows, :] = stream_kv.astype(jnp.bfloat16)
-        out[rows : 2 * rows, :] = stream_q.astype(jnp.bfloat16)
-        lag_base = pl.multiple_of(owner * half_rows, half_rows)
-        out[2 * rows : 2 * rows + half_rows, :] = lag_grad[pl.ds(lag_base, half_rows), :].astype(jnp.bfloat16)
-    for block in range(count):
-        base = block * rows
-        kv = grad_kv[base : base + rows, :]
-        q = grad_q[base : base + rows, :]
-        for j in range(tap_count):
-            window = slice(base + EDGE - j, base + EDGE - j + rows)
-            tap_sum_kv[j] = tap_sum_kv[j] + jnp.sum((kv * raw_kv[window, :]).reshape(rows // EDGE, EDGE, LANES), axis=0)
-            tap_sum_q[j] = tap_sum_q[j] + jnp.sum((q * raw_qc[window, :]).reshape(rows // EDGE, EDGE, LANES), axis=0)
-    spare = [jnp.zeros((1, LANES), jnp.float32)] * (EDGE - tap_count)
-    sums = jnp.concatenate(
-        [jnp.sum(s, axis=0, keepdims=True) for s in tap_sum_kv] + spare
-        + [jnp.sum(s, axis=0, keepdims=True) for s in tap_sum_q] + spare, axis=0
-    ) * scale
-    high = sums.astype(jnp.bfloat16)
-    both = jnp.concatenate([wide(high), sums - wide(high)], axis=0).astype(jnp.bfloat16)
-    for step in range(count):
-        out_refs[step][2 * rows + half_rows :, :] = both
-
-
-def unpack_kernel(count, tap_count, *refs):
+        out[0:rows, :] = pairs[pl.ds(base, rows), :].astype(jnp.bfloat16)
+        out[rows : rows + half_rows, :] = jnp.where(
+            low_half, lag_grad[pl.ds(base, half_rows), :], turned(lag_grad[pl.ds(base + half_rows, half_rows), :])
+        ).astype(jnp.bfloat16)
+        edge_q = jnp.where(
+            low_edge, raw_qc[pl.ds(base, EDGE), :], turned(grad_q[pl.ds(base + rows, EDGE), :])
+        )
+        extra = [raw_kv[pl.ds(base, EDGE), :], grad_kv[pl.ds(base + rows, EDGE), :], edge_q]
+        extra = extra + [sums_high[0], sums[0] - sums_high[0], sums_q]
+        out[rows + half_rows :, :] = jnp.concatenate(extra, axis=0).astype(jnp.bfloat16)
+
+
+def shifted_sum(taps, padded, first, direction, rows):
+    return sum(taps[j] * padded[first + direction * j : first + direction * j + rows, :] for j in range(len(taps)))
+
+
+def local_kernel(tap_count, streams_hbm, taps_hbm, cotangent_hbm, high_hbm, rest_hbm, back_hbm, arrived_ref, *refs):
+    conv_ref, taps_ref, cotangent_ref, high_ref, rest_ref, back_ref, streams_ref, padded, sems = refs
+    pairs = (
+        (streams_hbm, streams_ref), (taps_hbm, taps_ref), (cotangent_hbm, cotangent_ref),
+        (high_hbm, high_ref), (rest_hbm, rest_ref), (back_hbm, back_ref),
+    )
+    copies = [pltpu.make_async_copy(here, there, sems.at[k]) for k, (here, there) in enumerate(pairs)]
+    for copy in copies:
+        copy.start()
+    copies[0].wait()
+    copies[1].wait()
+    streams, rows, channels = conv_ref.shape
+    padded[0:EDGE, :] = jnp.zeros((EDGE, LANES), jnp.float32)
+    for i in range(streams):
+        for start in range(0, channels, LANES):
+            cols = slice(start, start + LANES)
+            padded[EDGE:, :] = wide(streams_ref[i, :, cols])
+            taps = [taps_ref[i, j : j + 1, cols] for j in range(tap_count)]
+            conv_ref[i, :, cols] = shifted_sum(taps, padded, EDGE, -1, rows)
+    for copy in copies[2:]:
+        copy.wait()
+
+
+def finish_kernel(count, tap_count, *refs):
     in_refs = refs[:count]
-    gated_ref, stream_ref, lag_ref, tap_ref = refs[count : count + 4]
-    blocks = refs[count + 4]
+    conv_ref, taps_ref, cotangent_ref = refs[count : count + 3]
+    gated_ref, stream_ref, lag_ref, tap_ref = refs[count + 3 : count + 7]
+    blocks, edges, grads = refs[count + 7 :]
     me = lax.axis_index("ctx")
     offsets = step_offsets(count)
     rows = gated_ref.shape[0]
     half_rows = rows // 2
     low = lower_lanes(rows)
     low_half = lower_lanes(half_rows)
-    low_taps = lower_lanes(EDGE)
+    low_edge = lower_lanes(EDGE)
     for step in range(count):
         owner = partner(me, offsets[step], -1, count)
         blocks[owner, :, :] = in_refs[step][...]
+    edges[EDGE:, :] = jnp.zeros((EDGE, LANES), jnp.float32)
     for pair in range(count // 2):
         cols = slice(pair * LANES, (pair + 1) * LANES)
-        even, odd = wide(blocks[2 * pair, :, :]), wide(blocks[2 * pair + 1, :, :])
-        turned_even, turned_odd = turned(even), turned(odd)
-
-        def lower_of(window, mask):
-            return jnp.where(mask, even[window], turned_odd[window])
-
-        def upper_of(window, mask):
-            return jnp.where(mask, turned_even[window], odd[window])
-
-        key_value, query_gated = slice(0, rows), slice(rows, 2 * rows)
-        stream_ref[1, :, cols] = lower_of(key_value, low).astype(jnp.bfloat16)
-        stream_ref[2, :, cols] = upper_of(key_value, low).astype(jnp.bfloat16)
-        stream_ref[0, :, cols] = lower_of(query_gated, low).astype(jnp.bfloat16)
-        gated_ref[:, cols] = upper_of(query_gated, low).astype(jnp.bfloat16)
-        lags = slice(2 * rows, 2 * rows + half_rows)
-        lag_ref[0:half_rows, cols] = lower_of(lags, low_half).astype(jnp.bfloat16)
-        lag_ref[half_rows:, cols] = upper_of(lags, low_half).astype(jnp.bfloat16)
-        start = 2 * rows + half_rows
-        high_kv, high_q, rest_kv, rest_q = [slice(start + g * EDGE, start + (g + 1) * EDGE) for g in range(4)]
-        tap_ref[1, :, cols] = (lower_of(high_kv, low_taps) + lower_of(rest_kv, low_taps))[:tap_count]
-        tap_ref[2, :, cols] = (upper_of(high_kv, low_taps) + upper_of(rest_kv, low_taps))[:tap_count]
-        tap_ref[0, :, cols] = (lower_of(high_q, low_taps) + lower_of(rest_q, low_taps))[:tap_count]
+
+        def both(start, extent, mask):
+            window = slice(start, start + extent)
+            even, odd = wide(blocks[2 * pair, window, :]), wide(blocks[2 * pair + 1, window, :])
+            return jnp.where(mask, even, turned(odd)), jnp.where(mask, turned(even), odd)
+
+        start = rows + half_rows
+        mixed, product_grad = both(0, rows, low)
+        lag_lower, lag_upper = both(rows, half_rows, low_half)
+        lag_ref[0:half_rows, cols] = lag_lower.astype(jnp.bfloat16)
+        lag_ref[half_rows:, cols] = lag_upper.astype(jnp.bfloat16)
+        before_key, before_value = both(start, EDGE, low_edge)
+        after_key, after_value = both(start + EDGE, EDGE, low_edge)
+        before_query, after_query = both(start + 2 * EDGE, EDGE, low_edge)
+        taps = [[taps_ref[i, j : j + 1, cols] for j in range(tap_count)] for i in range(3)]
+        convolved = []
+        for i, before in enumerate((before_query, before_key, before_value)):
+            edges[0:EDGE, :] = before
+            first = conv_ref[i, 0:EDGE, cols] + shifted_sum(taps[i], edges, EDGE, -1, EDGE)
+            convolved.append(jnp.concatenate([first, conv_ref[i, EDGE:, cols]], axis=0))
+        query, key, value = convolved
+        gated_ref[:, cols] = (query * mixed).astype(jnp.bfloat16)
+        own = (wide(cotangent_ref[:, cols]) * mixed, product_grad * value, product_grad * key)
+        for i, after in enumerate((after_query, after_key, after_value)):
+            grads[i, 0:rows, :] = own[i]
+            grads[i, rows:, :] = after
+            stream_ref[i, :, cols] = shifted_sum(taps[i], grads.at[i], 0, 1, rows).astype(jnp.bfloat16)
+        high_key, high_value = both(start + 3 * EDGE, EDGE, low_edge)
+        rest_key, rest_value = both(start + 4 * EDGE, EDGE, low_edge)
+        tap_ref[1, :, cols] = (high_key + rest_key)[:tap_count]
+        tap_ref[2, :, cols] = (high_value + rest_value)[:tap_count]
+        query_parts = [wide(blocks[2 * pair + k, start + 5 * EDGE : start + 6 * EDGE, :]) for k in range(2)]
+        query_sums = [part + turned(part) for part in query_parts]
+        tap_ref[0, :, cols] = jnp.where(low_edge, query_sums[0], query_sums[1])[:tap_count]
 
 
 def exchanged(blocks):
@@ -288,40 +356,64 @@
         name="pack",
     )(*[in_hbm(a) for a in (streams, filters, cotangent, taps)])
     arrived = exchanged(packed[:count])
-    table, back = odd_tables(total)
-    back_rows = sent_rows + TAP_ROWS
+    quarter = total // PHASES
+    tables = phase_tables(total)
+    hbm = pl.BlockSpec(memory_space=pltpu.HBM)
+    conv, taps_here, cotangent_here, *tables_here = pl.pallas_call(
+        functools.partial(local_kernel, tap_count),
+        out_shape=[
+            jax.ShapeDtypeStruct(streams.shape, jnp.float32),
+            jax.ShapeDtypeStruct(taps.shape, taps.dtype),
+            jax.ShapeDtypeStruct(cotangent.shape, cotangent.dtype),
+            *[jax.ShapeDtypeStruct(table.shape, jnp.bfloat16) for table in tables],
+        ],
+        in_specs=[hbm] * (3 + len(tables)) + [pl.BlockSpec(memory_space=pl.ANY)],
+        out_specs=in_vmem(3 + len(tables)),
+        scratch_shapes=[
+            pltpu.VMEM(streams.shape, streams.dtype),
+            pltpu.VMEM((rows + EDGE, LANES), jnp.float32),
+            pltpu.SemaphoreType.DMA((3 + len(tables),)),
+        ],
+        compiler_params=params,
+        name="local",
+    )(*[in_hbm(jnp.asarray(a)) for a in (streams, taps, cotangent, *tables)], arrived[count - 2])
+    back_rows = rows + rows // 2 + 6 * EDGE
     f32_rows = lambda extent: pltpu.VMEM((extent, LANES), jnp.float32)
     made = pl.pallas_call(
         functools.partial(main_kernel, count, tap_count, 1.0 / math.sqrt(total)),
         out_shape=[jax.ShapeDtypeStruct((back_rows, LANES), jnp.bfloat16)] * count,
-        in_specs=in_vmem(count + 1) + [pl.BlockSpec(memory_space=pltpu.HBM)] * 2,
+        in_specs=in_vmem(count + 1 + len(tables)),
         out_specs=in_vmem(count),
         scratch_shapes=[
-            f32_rows(total + EDGE), f32_rows(total + EDGE), f32_rows(total), f32_rows(total),
-            pltpu.VMEM((total, 2 * LANES), jnp.bfloat16), pltpu.VMEM((2 * total, 2 * LANES), jnp.bfloat16),
-            f32_rows(total + EDGE), f32_rows(total + EDGE), f32_rows(total // 2),
-            pltpu.VMEM(table.shape, jnp.bfloat16), pltpu.VMEM(back.shape, jnp.bfloat16),
-            pltpu.SemaphoreType.DMA((2,)),
+            f32_rows(total + EDGE), f32_rows(total + EDGE), f32_rows(total), f32_rows(total), f32_rows(total),
+            pltpu.VMEM((total, 2 * LANES), jnp.bfloat16),
+            pltpu.VMEM((PHASES, 2 * quarter, 2 * LANES), jnp.float32),
+            pltpu.VMEM((PHASES, 2 * quarter, 2 * LANES), jnp.bfloat16),
+            f32_rows(total), f32_rows(total + EDGE), f32_rows(total + EDGE), f32_rows(total),
         ],
         compiler_params=params,
         name="channels",
-    )(*arrived, packed[count], in_hbm(jnp.asarray(table)), in_hbm(jnp.asarray(back)))
+    )(*arrived, packed[count], *tables_here)
     returned = exchanged(made)
     return tuple(
         pl.pallas_call(
-            functools.partial(unpack_kernel, count, tap_count),
+            functools.partial(finish_kernel, count, tap_count),
             out_shape=[
                 jax.ShapeDtypeStruct(filters.shape, jnp.bfloat16),
                 jax.ShapeDtypeStruct(streams.shape, jnp.bfloat16),
                 jax.ShapeDtypeStruct(filters.shape, jnp.bfloat16),
                 jax.ShapeDtypeStruct(taps.shape, jnp.float32),
             ],
-            in_specs=in_vmem(count),
+            in_specs=in_vmem(count + 3),
             out_specs=in_vmem(4),
-            scratch_shapes=[pltpu.VMEM((count, back_rows, LANES), jnp.bfloat16)],
+            scratch_shapes=[
+                pltpu.VMEM((count, back_rows, LANES), jnp.bfloat16),
+                f32_rows(2 * EDGE),
+                pltpu.VMEM((3, rows + EDGE, LANES), jnp.float32),
+            ],
             compiler_params=params,
-            name="unpack",
-        )(*returned)
+            name="finish",
+        )(*returned, conv, taps_here, cotangent_here)
     )
 
 
@@ -493,7 +585,7 @@
     rows, channels = filters.shape
     tap_count = taps.shape[1]
     pairs_fill_lanes = channels == count * HALF and count % 2 == 0
-    short_enough = rows % LANES == 0 and 8 * (rows * count) ** 2 <= TABLE_BYTES and tap_count < EDGE
+    short_enough = rows % LANES == 0 and 3 * (rows * count) ** 2 <= TABLE_BYTES and tap_count < EDGE
     if pairs_fill_lanes and short_enough:
         return local_dense(streams, taps, filters, cotangent)
     return local_factored(streams, taps, filters, cotangent)

time: 47.5 us -> 41.1 us (0.87)
  waiting for transfers between devices: 10.5 us -> 6.42 us
  starting transfers between devices: 26.9 us -> 25.4 us
  Pallas kernels: 9.24 us -> 8.46 us
    ppermute x14, waiting for transfers between devices: 10.5 us -> 6.42 us  [exchanged(): lax.ppermute(block, 'ctx', [(source, partner(source, offset, 1, count)) f...]
    pallas_call x1, Pallas kernels: 6.44 us -> 3.1 us  [local_dense(): pl.pallas_call(functools.partial(main_kernel, count, tap_count, 1.0 / mat...]
    pallas_call x1 -> x2, Pallas kernels: 1.15 us -> 3.71 us  [the longest x1 2.12 us: local_dense(): pl.pallas_call(functools.partial(local_kernel, tap_count), out_shape=[jax...]
    ppermute x14, starting transfers between devices: 26.9 us -> 25.4 us  [exchanged(): lax.ppermute(block, 'ctx', [(source, partner(source, offset, 1, count)) f...]
  transfers between devices with their start and end apart: 14 -> 14, of which waited for: 3 -> 7; matrix products, arithmetic and copies ran while one was open for 0% -> 0% of each run, Pallas kernels for 0% -> 5%
where the time goes in v3:
time: 41.1 us; the launch traced here: 41 us
  starting transfers between devices  25.4 us (62%)
  Pallas kernels  8.46 us (21%)
  waiting for transfers between devices  6.42 us (16%)
  between operations  0.67 us (2%)
    ppermute x14, starting transfers between devices, exchanged(): lax.ppermute(block, 'ctx', [(source, partner(source, offset, 1, count)) f...  25.4 us
    ppermute x14, waiting for transfers between devices, exchanged(): lax.ppermute(block, 'ctx', [(source, partner(source, offset, 1, count)) f...  6.42 us
    pallas_call x1, Pallas kernels, local_dense(): pl.pallas_call(functools.partial(main_kernel, count, tap_count, 1.0 / mat...  3.1 us
    pallas_call x1, Pallas kernels, local_dense(): pl.pallas_call(functools.partial(local_kernel, tap_count), out_shape=[jax...  2.12 us
    pallas_call x1, Pallas kernels, local_dense(): pl.pallas_call(functools.partial(pack_kernel, count), out_shape=[jax.Shap...  1.64 us
    pallas_call x1, Pallas kernels, local_dense(): pl.pallas_call(functools.partial(finish_kernel, count, tap_count), out_sh...  1.59 us
  transfers between devices with their start and end apart: 14, of which 7 were waited for; matrix products, arithmetic and copies ran while one was open for 0% of the time, Pallas kernels for 5%

profile of v3, /device:TPU:0, one launch (start us, length us, event | category | flops | bytes accessed | tf_op | source)
XLA Modules:
  0.0 41.0 jit_solution(11148206361789688998)
XLA Ops:
  0.6 1.6 %pack.1 = (bf16[320,128]{1,0:T(8,128)(2,1)S(1)}, bf16[320,128]{1,0:T(8,128)(2,1)S(1)}, bf16[320,128]{1,0:T(8,128)(2,1)S(1)}, bf16[320,128]{1,0:T(8,128)(2,1)S(1)...) custom-call(bf16[3,128,512]{2,1,0:T(8,128)(2,1)} %streams_hbm.1, ...), custom_call_target="tpu_custom_call" | custom-call | tf_op jit(solution)/shard_map/pack/pallas_call | solution.py:347
  2.3 3.1 %collective-permute-start = (bf16[320,128]{1,0:T(8,128)(2,1)S(1)}, bf16[320,128]{1,0:T(8,128)(2,1)S(1)}, u32[]{:S(2)}, u32[]{:S(2)}) collective-permute-start(bf16[320,128]{1,0:T(8,128)(2,1)S(1)} %get-tuple-element.28), channel_id=1, source_target_pairs={{0,8},{4,12},{8,16},{12,20},{16,24},{20,28},{24,0},{28,4},{1,9},{5... | collective-permute-start | bytes 245768 | tf_op jit(solution)/shard_map/ppermute | solution.py:327
  5.4 1.5 %collective-permute-start.5 = (bf16[320,128]{1,0:T(8,128)(2,1)S(1)}, bf16[320,128]{1,0:T(8,128)(2,1)S(1)}, u32[]{:S(2)}, u32[]{:S(2)}) collective-permute-start(bf16[320,128]{1,0:T(8,128)(2,1)S(1)} %get-tuple-element.33), channel_id=1, source_target_pairs={{0,4},{4,0},{8,12},{12,8},{16,20},{20,16},{24,28},{28,24},{1,5},{5... | collective-permute-start | bytes 245768 | tf_op jit(solution)/shard_map/ppermute | solution.py:327
  6.9 2.6 %collective-permute-start.1 = (bf16[320,128]{1,0:T(8,128)(2,1)S(1)}, bf16[320,128]{1,0:T(8,128)(2,1)S(1)}, u32[]{:S(2)}, u32[]{:S(2)}) collective-permute-start(bf16[320,128]{1,0:T(8,128)(2,1)S(1)} %get-tuple-element.29), channel_id=1, source_target_pairs={{0,16},{4,20},{8,24},{12,28},{16,0},{20,4},{24,8},{28,12},{1,17},{... | collective-permute-start | bytes 245768 | tf_op jit(solution)/shard_map/ppermute | solution.py:327
  9.5 0.3 collective-permute-start.2
  9.7 2.5 %collective-permute-start.3 = (bf16[320,128]{1,0:T(8,128)(2,1)S(1)}, bf16[320,128]{1,0:T(8,128)(2,1)S(1)}, u32[]{:S(2)}, u32[]{:S(2)}) collective-permute-start(bf16[320,128]{1,0:T(8,128)(2,1)S(1)} %get-tuple-element.31), channel_id=1, source_target_pairs={{0,12},{4,8},{8,20},{12,16},{16,28},{20,24},{24,4},{28,0},{1,13},{... | collective-permute-start | bytes 245768 | tf_op jit(solution)/shard_map/ppermute | solution.py:327
  12.3 0.0 collective-permute-done.refs_1_
  12.3 2.2 %collective-permute-start.4 = (bf16[320,128]{1,0:T(8,128)(2,1)S(1)}, bf16[320,128]{1,0:T(8,128)(2,1)S(1)}, u32[]{:S(2)}, u32[]{:S(2)}) collective-permute-start(bf16[320,128]{1,0:T(8,128)(2,1)S(1)} %get-tuple-element.32), channel_id=1, source_target_pairs={{0,28},{4,24},{8,4},{12,0},{16,12},{20,8},{24,20},{28,16},{1,29},{... | collective-permute-start | bytes 245768 | tf_op jit(solution)/shard_map/ppermute | solution.py:327
  14.5 0.0 collective-permute-done.5.arrived_ref.refs_6_
  14.5 1.6 %collective-permute-start.6 = (bf16[320,128]{1,0:T(8,128)(2,1)S(1)}, bf16[320,128]{1,0:T(8,128)(2,1)S(1)}, u32[]{:S(2)}, u32[]{:S(2)}) collective-permute-start(bf16[320,128]{1,0:T(8,128)(2,1)S(1)} %get-tuple-element.34), channel_id=1, source_target_pairs={{0,24},{4,28},{8,0},{12,4},{16,8},{20,12},{24,16},{28,20},{1,25},{... | collective-permute-start | bytes 245768 | tf_op jit(solution)/shard_map/ppermute | solution.py:327
  16.1 2.1 %local.1 = (f32[3,128,512]{2,1,0:T(8,128)S(1)}, f32[3,7,512]{2,1,0:T(8,128)S(1)}, bf16[128,512]{1,0:T(8,128)(2,1)S(1)}, bf16[4,512,256]{2,1,0:T(8,128)(2,1)S(1)}...) custom-call(bf16[3,128,512]{2,1,0:T(8,128)(2,1)} %streams_hbm.1, f32[3,7,512]{2,1,0:T(8,128)} %taps_hbm.1, ...), custom_call_target="tpu_custom_call" | custom-call | tf_op jit(solution)/shard_map/local/pallas_call | solution.py:362
  18.2 0.0 collective-permute-done.1.refs_2_
  18.3 1.5 %collective-permute-done.2.refs_3_ = bf16[320,128]{1,0:T(8,128)(2,1)S(1)} collective-permute-done((bf16[320,128]{1,0:T(8,128)(2,1)S(1)}, bf16[320,128]{1,0:T(8,128)(2,1)S(1)}, u32[]{:S(2)}, u32[]{:S(2)}) %collective-permute-start.2) | collective-permute-done | bytes 81952 | tf_op jit(solution)/shard_map/ppermute | solution.py:327
  19.8 0.0 collective-permute-done.3.refs_4_
  19.8 1.6 %collective-permute-done.4.refs_5_ = bf16[320,128]{1,0:T(8,128)(2,1)S(1)} collective-permute-done((bf16[320,128]{1,0:T(8,128)(2,1)S(1)}, bf16[320,128]{1,0:T(8,128)(2,1)S(1)}, u32[]{:S(2)}, u32[]{:S(2)}) %collective-permute-start.4) | collective-permute-done | bytes 81952 | tf_op jit(solution)/shard_map/ppermute | solution.py:327
  21.3 0.0 collective-permute-done.6.refs_7_
  21.3 3.1 %channels.1 = (bf16[240,128]{1,0:T(8,128)(2,1)S(1)}, bf16[240,128]{1,0:T(8,128)(2,1)S(1)}, bf16[240,128]{1,0:T(8,128)(2,1)S(1)}, bf16[240,128]{1,0:T(8,128)(2,1)...) custom-call(bf16[320,128]{1,0:T(8,128)(2,1)S(1)} %get-tuple-element., ...), custom_call_target="tpu_custom_call" | custom-call | tf_op jit(solution)/shard_map/channels/pallas_call | solution.py:382
  24.4 1.4 %collective-permute-start.7 = (bf16[240,128]{1,0:T(8,128)(2,1)S(1)}, bf16[240,128]{1,0:T(8,128)(2,1)S(1)}, u32[]{:S(2)}, u32[]{:S(2)}) collective-permute-start(bf16[240,128]{1,0:T(8,128)(2,1)S(1)} %get-tuple-element.40), channel_id=1, source_target_pairs={{0,8},{4,12},{8,16},{12,20},{16,24},{20,28},{24,0},{28,4},{1,9},{5... | collective-permute-start | bytes 184328 | tf_op jit(solution)/shard_map/ppermute | solution.py:327
  25.8 1.7 %collective-permute-start.8 = (bf16[240,128]{1,0:T(8,128)(2,1)S(1)}, bf16[240,128]{1,0:T(8,128)(2,1)S(1)}, u32[]{:S(2)}, u32[]{:S(2)}) collective-permute-start(bf16[240,128]{1,0:T(8,128)(2,1)S(1)} %get-tuple-element.41), channel_id=1, source_target_pairs={{0,16},{4,20},{8,24},{12,28},{16,0},{20,4},{24,8},{28,12},{1,17},{... | collective-permute-start | bytes 184328 | tf_op jit(solution)/shard_map/ppermute | solution.py:327
  27.6 2.1 %collective-permute-start.9 = (bf16[240,128]{1,0:T(8,128)(2,1)S(1)}, bf16[240,128]{1,0:T(8,128)(2,1)S(1)}, u32[]{:S(2)}, u32[]{:S(2)}) collective-permute-start(bf16[240,128]{1,0:T(8,128)(2,1)S(1)} %get-tuple-element.42), channel_id=1, source_target_pairs={{0,20},{4,16},{8,28},{12,24},{16,4},{20,0},{24,12},{28,8},{1,21},{... | collective-permute-start | bytes 184328 | tf_op jit(solution)/shard_map/ppermute | solution.py:327
  29.7 1.9 %collective-permute-start.10 = (bf16[240,128]{1,0:T(8,128)(2,1)S(1)}, bf16[240,128]{1,0:T(8,128)(2,1)S(1)}, u32[]{:S(2)}, u32[]{:S(2)}) collective-permute-start(bf16[240,128]{1,0:T(8,128)(2,1)S(1)} %get-tuple-element.43), channel_id=1, source_target_pairs={{0,12},{4,8},{8,20},{12,16},{16,28},{20,24},{24,4},{28,0},{1,13},{... | collective-permute-start | bytes 184328 | tf_op jit(solution)/shard_map/ppermute | solution.py:327
  31.6 2.8 %collective-permute-start.11 = (bf16[240,128]{1,0:T(8,128)(2,1)S(1)}, bf16[240,128]{1,0:T(8,128)(2,1)S(1)}, u32[]{:S(2)}, u32[]{:S(2)}) collective-permute-start(bf16[240,128]{1,0:T(8,128)(2,1)S(1)} %get-tuple-element.44), channel_id=1, source_target_pairs={{0,28},{4,24},{8,4},{12,0},{16,12},{20,8},{24,20},{28,16},{1,29},{... | collective-permute-start | bytes 184328 | tf_op jit(solution)/shard_map/ppermute | solution.py:327
  34.4 0.0 collective-permute-done.7.refs_1_
  34.4 0.6 %collective-permute-start.12 = (bf16[240,128]{1,0:T(8,128)(2,1)S(1)}, bf16[240,128]{1,0:T(8,128)(2,1)S(1)}, u32[]{:S(2)}, u32[]{:S(2)}) collective-permute-start(bf16[240,128]{1,0:T(8,128)(2,1)S(1)} %get-tuple-element.45), channel_id=1, source_target_pairs={{0,4},{4,0},{8,12},{12,8},{16,20},{20,16},{24,28},{28,24},{1,5},{5... | collective-permute-start | bytes 184328 | tf_op jit(solution)/shard_map/ppermute | solution.py:327
  34.9 0.2 collective-permute-done.8.refs_2_
  35.2 1.1 %collective-permute-start.13 = (bf16[240,128]{1,0:T(8,128)(2,1)S(1)}, bf16[240,128]{1,0:T(8,128)(2,1)S(1)}, u32[]{:S(2)}, u32[]{:S(2)}) collective-permute-start(bf16[240,128]{1,0:T(8,128)(2,1)S(1)} %get-tuple-element.46), channel_id=1, source_target_pairs={{0,24},{4,28},{8,0},{12,4},{16,8},{20,12},{24,16},{28,20},{1,25},{... | collective-permute-start | bytes 184328 | tf_op jit(solution)/shard_map/ppermute | solution.py:327
  36.3 1.0 %collective-permute-done.9.refs_3_ = bf16[240,128]{1,0:T(8,128)(2,1)S(1)} collective-permute-done((bf16[240,128]{1,0:T(8,128)(2,1)S(1)}, bf16[240,128]{1,0:T(8,128)(2,1)S(1)}, u32[]{:S(2)}, u32[]{:S(2)}) %collective-permute-start.9) | collective-permute-done | bytes 61472 | tf_op jit(solution)/shard_map/ppermute | solution.py:327
  37.3 0.0 collective-permute-done.10.refs_4_
  37.3 1.0 %collective-permute-done.11.refs_5_ = bf16[240,128]{1,0:T(8,128)(2,1)S(1)} collective-permute-done((bf16[240,128]{1,0:T(8,128)(2,1)S(1)}, bf16[240,128]{1,0:T(8,128)(2,1)S(1)}, u32[]{:S(2)}, u32[]{:S(2)}) %collective-permute-start.11) | collective-permute-done | bytes 61472 | tf_op jit(solution)/shard_map/ppermute | solution.py:327
  38.3 0.7 %collective-permute-done.12.refs_6_ = bf16[240,128]{1,0:T(8,128)(2,1)S(1)} collective-permute-done((bf16[240,128]{1,0:T(8,128)(2,1)S(1)}, bf16[240,128]{1,0:T(8,128)(2,1)S(1)}, u32[]{:S(2)}, u32[]{:S(2)}) %collective-permute-start.12) | collective-permute-done | bytes 61472 | tf_op jit(solution)/shard_map/ppermute | solution.py:327
  39.0 0.3 collective-permute-done.13.refs_7_
  39.4 1.6 %finish.1 = (bf16[128,512]{1,0:T(8,128)(2,1)}, bf16[3,128,512]{2,1,0:T(8,128)(2,1)}, bf16[128,512]{1,0:T(8,128)(2,1)}, f32[3,7,512]{2,1,0:T(8,128)}) custom-call(bf16[240,128]{1,0:T(8,128)(2,1)S(1)} %get-tuple-element.39.refs_0_, bf16[240,128]{1,0:T(8,128)(2,1)S(1)} %collective-permute-done.7.refs_1_, bf16[240,128]{1,0:T(8,128)(2,1)S(1)} %collective-permute-done.8.refs_2_, ...), custom_call_target="tpu_custom_call" | custom-call | tf_op jit(solution)/shard_map/finish/pallas_call | solution.py:399
Async XLA Ops:
  2.3 10.0 %collective-permute-start = (bf16[320,128]{1,0:T(8,128)(2,1)S(1)}, bf16[320,128]{1,0:T(8,128)(2,1)S(1)}, u32[]{:S(2)}, u32[]{:S(2)}) collective-permute-start(bf16[320,128]{1,0:T(8,128)(2,1)S(1)} %get-tuple-element.28), channel_id=1, source_target_pairs={{0,8},{4,12},{8,16},{12,20},{16,24},{20,28},{24,0},{28,4},{1,9},{5... | collective-permute-start | bytes 245768 | tf_op jit(solution)/shard_map/ppermute | solution.py:327
  5.4 9.1 %collective-permute-start.5 = (bf16[320,128]{1,0:T(8,128)(2,1)S(1)}, bf16[320,128]{1,0:T(8,128)(2,1)S(1)}, u32[]{:S(2)}, u32[]{:S(2)}) collective-permute-start(bf16[320,128]{1,0:T(8,128)(2,1)S(1)} %get-tuple-element.33), channel_id=1, source_target_pairs={{0,4},{4,0},{8,12},{12,8},{16,20},{20,16},{24,28},{28,24},{1,5},{5... | collective-permute-start | bytes 245768 | tf_op jit(solution)/shard_map/ppermute | solution.py:327
  6.9 11.4 %collective-permute-start.1 = (bf16[320,128]{1,0:T(8,128)(2,1)S(1)}, bf16[320,128]{1,0:T(8,128)(2,1)S(1)}, u32[]{:S(2)}, u32[]{:S(2)}) collective-permute-start(bf16[320,128]{1,0:T(8,128)(2,1)S(1)} %get-tuple-element.29), channel_id=1, source_target_pairs={{0,16},{4,20},{8,24},{12,28},{16,0},{20,4},{24,8},{28,12},{1,17},{... | collective-permute-start | bytes 245768 | tf_op jit(solution)/shard_map/ppermute | solution.py:327
  9.5 10.3 %collective-permute-start.2 = (bf16[320,128]{1,0:T(8,128)(2,1)S(1)}, bf16[320,128]{1,0:T(8,128)(2,1)S(1)}, u32[]{:S(2)}, u32[]{:S(2)}) collective-permute-start(bf16[320,128]{1,0:T(8,128)(2,1)S(1)} %get-tuple-element.30), channel_id=1, source_target_pairs={{0,20},{4,16},{8,28},{12,24},{16,4},{20,0},{24,12},{28,8},{1,21},{... | collective-permute-start | bytes 245768 | tf_op jit(solution)/shard_map/ppermute | solution.py:327
  9.7 10.0 %collective-permute-start.3 = (bf16[320,128]{1,0:T(8,128)(2,1)S(1)}, bf16[320,128]{1,0:T(8,128)(2,1)S(1)}, u32[]{:S(2)}, u32[]{:S(2)}) collective-permute-start(bf16[320,128]{1,0:T(8,128)(2,1)S(1)} %get-tuple-element.31), channel_id=1, source_target_pairs={{0,12},{4,8},{8,20},{12,16},{16,28},{20,24},{24,4},{28,0},{1,13},{... | collective-permute-start | bytes 245768 | tf_op jit(solution)/shard_map/ppermute | solution.py:327
  12.3 9.0 %collective-permute-start.4 = (bf16[320,128]{1,0:T(8,128)(2,1)S(1)}, bf16[320,128]{1,0:T(8,128)(2,1)S(1)}, u32[]{:S(2)}, u32[]{:S(2)}) collective-permute-start(bf16[320,128]{1,0:T(8,128)(2,1)S(1)} %get-tuple-element.32), channel_id=1, source_target_pairs={{0,28},{4,24},{8,4},{12,0},{16,12},{20,8},{24,20},{28,16},{1,29},{... | collective-permute-start | bytes 245768 | tf_op jit(solution)/shard_map/ppermute | solution.py:327
  14.5 6.8 %collective-permute-start.6 = (bf16[320,128]{1,0:T(8,128)(2,1)S(1)}, bf16[320,128]{1,0:T(8,128)(2,1)S(1)}, u32[]{:S(2)}, u32[]{:S(2)}) collective-permute-start(bf16[320,128]{1,0:T(8,128)(2,1)S(1)} %get-tuple-element.34), channel_id=1, source_target_pairs={{0,24},{4,28},{8,0},{12,4},{16,8},{20,12},{24,16},{28,20},{1,25},{... | collective-permute-start | bytes 245768 | tf_op jit(solution)/shard_map/ppermute | solution.py:327
  24.4 10.0 %collective-permute-start.7 = (bf16[240,128]{1,0:T(8,128)(2,1)S(1)}, bf16[240,128]{1,0:T(8,128)(2,1)S(1)}, u32[]{:S(2)}, u32[]{:S(2)}) collective-permute-start(bf16[240,128]{1,0:T(8,128)(2,1)S(1)} %get-tuple-element.40), channel_id=1, source_target_pairs={{0,8},{4,12},{8,16},{12,20},{16,24},{20,28},{24,0},{28,4},{1,9},{5... | collective-permute-start | bytes 184328 | tf_op jit(solution)/shard_map/ppermute | solution.py:327
  25.8 9.3 %collective-permute-start.8 = (bf16[240,128]{1,0:T(8,128)(2,1)S(1)}, bf16[240,128]{1,0:T(8,128)(2,1)S(1)}, u32[]{:S(2)}, u32[]{:S(2)}) collective-permute-start(bf16[240,128]{1,0:T(8,128)(2,1)S(1)} %get-tuple-element.41), channel_id=1, source_target_pairs={{0,16},{4,20},{8,24},{12,28},{16,0},{20,4},{24,8},{28,12},{1,17},{... | collective-permute-start | bytes 184328 | tf_op jit(solution)/shard_map/ppermute | solution.py:327
  27.6 9.7 %collective-permute-start.9 = (bf16[240,128]{1,0:T(8,128)(2,1)S(1)}, bf16[240,128]{1,0:T(8,128)(2,1)S(1)}, u32[]{:S(2)}, u32[]{:S(2)}) collective-permute-start(bf16[240,128]{1,0:T(8,128)(2,1)S(1)} %get-tuple-element.42), channel_id=1, source_target_pairs={{0,20},{4,16},{8,28},{12,24},{16,4},{20,0},{24,12},{28,8},{1,21},{... | collective-permute-start | bytes 184328 | tf_op jit(solution)/shard_map/ppermute | solution.py:327
  29.7 7.6 %collective-permute-start.10 = (bf16[240,128]{1,0:T(8,128)(2,1)S(1)}, bf16[240,128]{1,0:T(8,128)(2,1)S(1)}, u32[]{:S(2)}, u32[]{:S(2)}) collective-permute-start(bf16[240,128]{1,0:T(8,128)(2,1)S(1)} %get-tuple-element.43), channel_id=1, source_target_pairs={{0,12},{4,8},{8,20},{12,16},{16,28},{20,24},{24,4},{28,0},{1,13},{... | collective-permute-start | bytes 184328 | tf_op jit(solution)/shard_map/ppermute | solution.py:327
  31.6 6.8 %collective-permute-start.11 = (bf16[240,128]{1,0:T(8,128)(2,1)S(1)}, bf16[240,128]{1,0:T(8,128)(2,1)S(1)}, u32[]{:S(2)}, u32[]{:S(2)}) collective-permute-start(bf16[240,128]{1,0:T(8,128)(2,1)S(1)} %get-tuple-element.44), channel_id=1, source_target_pairs={{0,28},{4,24},{8,4},{12,0},{16,12},{20,8},{24,20},{28,16},{1,29},{... | collective-permute-start | bytes 184328 | tf_op jit(solution)/shard_map/ppermute | solution.py:327
  34.4 4.6 %collective-permute-start.12 = (bf16[240,128]{1,0:T(8,128)(2,1)S(1)}, bf16[240,128]{1,0:T(8,128)(2,1)S(1)}, u32[]{:S(2)}, u32[]{:S(2)}) collective-permute-start(bf16[240,128]{1,0:T(8,128)(2,1)S(1)} %get-tuple-element.45), channel_id=1, source_target_pairs={{0,4},{4,0},{8,12},{12,8},{16,20},{20,16},{24,28},{28,24},{1,5},{5... | collective-permute-start | bytes 184328 | tf_op jit(solution)/shard_map/ppermute | solution.py:327
  35.2 4.2 %collective-permute-start.13 = (bf16[240,128]{1,0:T(8,128)(2,1)S(1)}, bf16[240,128]{1,0:T(8,128)(2,1)S(1)}, u32[]{:S(2)}, u32[]{:S(2)}) collective-permute-start(bf16[240,128]{1,0:T(8,128)(2,1)S(1)} %get-tuple-element.46), channel_id=1, source_target_pairs={{0,24},{4,28},{8,0},{12,4},{16,8},{20,12},{24,16},{28,20},{1,25},{... | collective-permute-start | bytes 184328 | tf_op jit(solution)/shard_map/ppermute | solution.py:327

commit v4 on v3

--- a/solution.py
+++ b/solution.py
@@ -14,6 +14,7 @@
 HALF = LANES // 2
 PHASES = 4
 EDGE = 8
+ROW_TILE = 16
 TABLE_BYTES = 16 * 1024 * 1024
 VMEM_BYTES = 32 * 1024 * 1024
 
@@ -22,8 +23,8 @@
     groups = count // 2
     far = groups // 2
     near = [g for g in range(1, groups) if g != far]
-    order = [(g, 0) for g in near[:1]] + [(far, 0), (far, 1)] + [(g, 1) for g in near]
-    order = order + [(0, 1)] + [(g, 0) for g in near[1:]]
+    order = [(g, 0) for g in near[:1]] + [(far, 0)] + [(g, 1) for g in near[:1]] + [(far, 1)]
+    order = order + [(g, 1) for g in near[1:]] + [(0, 1)] + [(g, 0) for g in near[1:]]
     return [(0, 0)] + [offset for offset in order if offset != (0, 0)]
 
 
@@ -48,20 +49,15 @@
 
 
 def paired(first, second, odd, low):
-    left = jnp.where(odd, turned(first), first)
-    right = jnp.where(odd, second, turned(second))
+    left = pltpu.roll(first, odd * HALF, 1)
+    right = pltpu.roll(second, HALF - odd * HALF, 1)
     return jnp.where(low, left, right).astype(jnp.bfloat16)
 
 
 def pack_kernel(count, *refs):
-    in_hbm, out_refs = refs[:4], refs[4 : 5 + count]
-    held, sems = refs[5 + count : 9 + count], refs[9 + count]
-    copies = [pltpu.make_async_copy(here, there, sems.at[k]) for k, (here, there) in enumerate(zip(in_hbm, held))]
-    for copy in copies:
-        copy.start()
-    for copy in copies:
-        copy.wait()
-    streams_ref, filters_ref, cotangent_ref, taps_ref = held
+    streams_hbm, filters_hbm, cotangent_hbm, taps_hbm = refs[:4]
+    out_refs = refs[4 : 5 + count]
+    streams_ref, filters_ref, cotangent_ref, taps_ref, sems = refs[5 + count :]
     me = lax.axis_index("ctx")
     offsets = step_offsets(count)
     rows = filters_ref.shape[0]
@@ -69,20 +65,34 @@
     tap_count = taps_ref.shape[1]
     low = lower_lanes(rows)
     low_half = lower_lanes(half_rows)
-    for step in range(count):
-        owner = partner(me, offsets[step], 1, count)
-        cols = pl.ds(pl.multiple_of(owner // 2 * LANES, LANES), LANES)
-        odd = lax.rem(owner, 2) == 1
-        out = out_refs[step]
-        out[0:rows, :] = paired(wide(streams_ref[1, :, cols]), wide(streams_ref[2, :, cols]), odd, low)
-        out[rows : 2 * rows, :] = paired(wide(streams_ref[0, :, cols]), wide(cotangent_ref[:, cols]), odd, low)
+    moves = (
+        (filters_hbm, filters_ref), (streams_hbm.at[1:], streams_ref.at[1:]), (streams_hbm.at[:1], streams_ref.at[:1]),
+        (cotangent_hbm, cotangent_ref), (taps_hbm, taps_ref),
+    )
+    copies = [pltpu.make_async_copy(here, there, sems.at[k]) for k, (here, there) in enumerate(moves)]
+    for copy in copies:
+        copy.start()
+
+    def place(owner):
+        return pl.ds(pl.multiple_of(owner // 2 * LANES, LANES), LANES), lax.rem(owner, 2)
+
+    places = [place(partner(me, offsets[step], 1, count)) for step in range(count)]
+    copies[0].wait()
+    for (cols, odd), out in zip(places, out_refs):
         lag_block = wide(filters_ref[:, cols])
         out[2 * rows :, :] = paired(lag_block[:half_rows], lag_block[half_rows:], odd, low_half)
-    cols = pl.ds(pl.multiple_of(me // 2 * LANES, LANES), LANES)
-    odd = lax.rem(me, 2) == 1
+    copies[1].wait()
+    for (cols, odd), out in zip(places, out_refs):
+        out[0:rows, :] = paired(wide(streams_ref[1, :, cols]), wide(streams_ref[2, :, cols]), odd, low)
+    copies[2].wait()
+    copies[3].wait()
+    for (cols, odd), out in zip(places, out_refs):
+        out[rows : 2 * rows, :] = paired(wide(streams_ref[0, :, cols]), wide(cotangent_ref[:, cols]), odd, low)
+    copies[4].wait()
+    cols, odd = place(me)
     tap_out = out_refs[count]
     low_taps = lower_lanes(tap_count)
-    here = [jnp.where(odd, turned(taps_ref[i, :, cols]), taps_ref[i, :, cols]) for i in range(3)]
+    here = [pltpu.roll(taps_ref[i, :, cols], odd * HALF, 1) for i in range(3)]
     first_tap = lax.broadcasted_iota(jnp.int32, (tap_count, LANES), 0) == 0
     tap_out[...] = jnp.zeros_like(tap_out)
     tap_out[0:tap_count, :] = jnp.where(low_taps, here[1], turned(here[2]))
@@ -121,7 +131,7 @@
     in_refs = refs[:count]
     tap_ref, high, rest, back = refs[count : count + 4]
     out_refs = refs[count + 4 : 2 * count + 4]
-    (raw_kv, raw_qc, raw_lag, conv_kv, conv_qc, signals, phased, spectra, pairs, grad_kv, grad_q, lag_grad) = refs[
+    (raw_kv, raw_qc, raw_lag, conv_kv, conv_qc, signals, phased, spectra, pairs, grad_kv, grad_q, lag_grad, extra) = refs[
         2 * count + 4 :
     ]
     me = lax.axis_index("ctx")
@@ -206,6 +216,7 @@
         grad_kv[spread, :] = jnp.where(low, other, pair) * turned(conv_kv[here, :])
         lag_grad[spread, :] = result[:, LANES:] * scale
 
+    extra[...] = jnp.zeros_like(extra)
     tap_sum_kv = [jnp.zeros((EDGE, LANES), jnp.float32)] * tap_count
     tap_sum_q = [jnp.zeros((EDGE, LANES), jnp.float32)] * tap_count
     part = min(32, rows)
@@ -221,9 +232,12 @@
         jnp.concatenate([jnp.sum(s, axis=0, keepdims=True) for s in parts] + spare, axis=0) * scale
         for parts in (tap_sum_kv, tap_sum_q)
     ]
-    sums_high = [wide(s.astype(jnp.bfloat16)) for s in sums]
-    low_edge = lower_lanes(EDGE)
-    sums_q = jnp.where(low_edge, sums_high[1], turned(sums[1] - sums_high[1]))
+    reach = tap_count - 1
+    low_taps, low_reach = lower_lanes(tap_count), lower_lanes(reach)
+    sums_kv, sums_q = [s[:tap_count] for s in sums]
+    high_q = wide(sums_q.astype(jnp.bfloat16))
+    extra[3 * reach : 3 * reach + tap_count, :] = sums_kv
+    extra[3 * reach + tap_count : 3 * reach + 2 * tap_count, :] = jnp.where(low_taps, high_q, turned(sums_q - high_q))
     for step in range(count):
         owner = partner(me, offsets[step], 1, count)
         base = pl.multiple_of(owner * rows, rows)
@@ -232,12 +246,12 @@
         out[rows : rows + half_rows, :] = jnp.where(
             low_half, lag_grad[pl.ds(base, half_rows), :], turned(lag_grad[pl.ds(base + half_rows, half_rows), :])
         ).astype(jnp.bfloat16)
-        edge_q = jnp.where(
-            low_edge, raw_qc[pl.ds(base, EDGE), :], turned(grad_q[pl.ds(base + rows, EDGE), :])
+        extra[0:reach, :] = raw_kv[pl.ds(base + EDGE - reach, reach), :]
+        extra[reach : 2 * reach, :] = grad_kv[pl.ds(base + rows, reach), :]
+        extra[2 * reach : 3 * reach, :] = jnp.where(
+            low_reach, raw_qc[pl.ds(base + EDGE - reach, reach), :], turned(grad_q[pl.ds(base + rows, reach), :])
         )
-        extra = [raw_kv[pl.ds(base, EDGE), :], grad_kv[pl.ds(base + rows, EDGE), :], edge_q]
-        extra = extra + [sums_high[0], sums[0] - sums_high[0], sums_q]
-        out[rows + half_rows :, :] = jnp.concatenate(extra, axis=0).astype(jnp.bfloat16)
+        out[rows + half_rows :, :] = extra[...].astype(jnp.bfloat16)
 
 
 def shifted_sum(taps, padded, first, direction, rows):
@@ -270,55 +284,64 @@
 def finish_kernel(count, tap_count, *refs):
     in_refs = refs[:count]
     conv_ref, taps_ref, cotangent_ref = refs[count : count + 3]
-    gated_ref, stream_ref, lag_ref, tap_ref = refs[count + 3 : count + 7]
-    blocks, edges, grads = refs[count + 7 :]
+    out_hbm = refs[count + 3 : count + 7]
+    gated_ref, stream_ref, lag_ref, tap_ref, blocks, extras, edges, grads, sems, tap_sem = refs[count + 7 :]
     me = lax.axis_index("ctx")
     offsets = step_offsets(count)
     rows = gated_ref.shape[0]
     half_rows = rows // 2
+    reach = tap_count - 1
     low = lower_lanes(rows)
     low_half = lower_lanes(half_rows)
-    low_edge = lower_lanes(EDGE)
+    low_extra = lower_lanes(extras.shape[1])
+    low_taps = lower_lanes(tap_count)
     for step in range(count):
         owner = partner(me, offsets[step], -1, count)
         blocks[owner, :, :] = in_refs[step][...]
-    edges[EDGE:, :] = jnp.zeros((EDGE, LANES), jnp.float32)
+    edges[...] = jnp.zeros_like(edges)
+    copies = []
     for pair in range(count // 2):
         cols = slice(pair * LANES, (pair + 1) * LANES)
 
-        def both(start, extent, mask):
-            window = slice(start, start + extent)
+        def both(window, mask):
             even, odd = wide(blocks[2 * pair, window, :]), wide(blocks[2 * pair + 1, window, :])
             return jnp.where(mask, even, turned(odd)), jnp.where(mask, turned(even), odd)
 
-        start = rows + half_rows
-        mixed, product_grad = both(0, rows, low)
-        lag_lower, lag_upper = both(rows, half_rows, low_half)
+        extra_rows = slice(rows + half_rows, None)
+        extras[0, :, :], extras[1, :, :] = both(extra_rows, low_extra)
+        mixed, product_grad = both(slice(0, rows), low)
+        lag_lower, lag_upper = both(slice(rows, rows + half_rows), low_half)
         lag_ref[0:half_rows, cols] = lag_lower.astype(jnp.bfloat16)
         lag_ref[half_rows:, cols] = lag_upper.astype(jnp.bfloat16)
-        before_key, before_value = both(start, EDGE, low_edge)
-        after_key, after_value = both(start + EDGE, EDGE, low_edge)
-        before_query, after_query = both(start + 2 * EDGE, EDGE, low_edge)
         taps = [[taps_ref[i, j : j + 1, cols] for j in range(tap_count)] for i in range(3)]
+        befores = (extras[0, 2 * reach : 3 * reach, :], extras[0, 0:reach, :], extras[1, 0:reach, :])
+        afters = (extras[1, 2 * reach : 3 * reach, :], extras[0, reach : 2 * reach, :], extras[1, reach : 2 * reach, :])
         convolved = []
-        for i, before in enumerate((before_query, before_key, before_value)):
-            edges[0:EDGE, :] = before
-            first = conv_ref[i, 0:EDGE, cols] + shifted_sum(taps[i], edges, EDGE, -1, EDGE)
+        for i in range(3):
+            edges[i, EDGE - reach : EDGE, :] = befores[i]
+            first = conv_ref[i, 0:EDGE, cols] + shifted_sum(taps[i], edges.at[i], EDGE, -1, EDGE)
             convolved.append(jnp.concatenate([first, conv_ref[i, EDGE:, cols]], axis=0))
         query, key, value = convolved
         gated_ref[:, cols] = (query * mixed).astype(jnp.bfloat16)
         own = (wide(cotangent_ref[:, cols]) * mixed, product_grad * value, product_grad * key)
-        for i, after in enumerate((after_query, after_key, after_value)):
+        for i in range(3):
             grads[i, 0:rows, :] = own[i]
-            grads[i, rows:, :] = after
+            grads[i, rows : rows + reach, :] = afters[i]
             stream_ref[i, :, cols] = shifted_sum(taps[i], grads.at[i], 0, 1, rows).astype(jnp.bfloat16)
-        high_key, high_value = both(start + 3 * EDGE, EDGE, low_edge)
-        rest_key, rest_value = both(start + 4 * EDGE, EDGE, low_edge)
-        tap_ref[1, :, cols] = (high_key + rest_key)[:tap_count]
-        tap_ref[2, :, cols] = (high_value + rest_value)[:tap_count]
-        query_parts = [wide(blocks[2 * pair + k, start + 5 * EDGE : start + 6 * EDGE, :]) for k in range(2)]
-        query_sums = [part + turned(part) for part in query_parts]
-        tap_ref[0, :, cols] = jnp.where(low_edge, query_sums[0], query_sums[1])[:tap_count]
+        sums_kv = slice(3 * reach, 3 * reach + tap_count)
+        sums_q = slice(3 * reach + tap_count, 3 * reach + 2 * tap_count)
+        tap_ref[1, :, cols] = extras[0, sums_kv, :]
+        tap_ref[2, :, cols] = extras[1, sums_kv, :]
+        tap_ref[0, :, cols] = extras[0, sums_q, :] + extras[1, sums_q, :]
+        held = (gated_ref.at[:, cols], stream_ref.at[:, :, cols], lag_ref.at[:, cols])
+        there = (out_hbm[0].at[:, cols], out_hbm[1].at[:, :, cols], out_hbm[2].at[:, cols])
+        for k in range(3):
+            copies.append(pltpu.make_async_copy(held[k], there[k], sems.at[pair, k]))
+            copies[-1].start()
+    copies.append(pltpu.make_async_copy(tap_ref, out_hbm[3], tap_sem.at[0]))
+    copies[-1].start()
+    for copy in copies:
+        copy.wait()
 
 
 def exchanged(blocks):
@@ -351,7 +374,7 @@
         in_specs=[pl.BlockSpec(memory_space=pltpu.HBM)] * 4,
         out_specs=in_vmem(count + 1),
         scratch_shapes=[pltpu.VMEM(a.shape, a.dtype) for a in (streams, filters, cotangent, taps)]
-        + [pltpu.SemaphoreType.DMA((4,))],
+        + [pltpu.SemaphoreType.DMA((5,))],
         compiler_params=params,
         name="pack",
     )(*[in_hbm(a) for a in (streams, filters, cotangent, taps)])
@@ -377,7 +400,8 @@
         compiler_params=params,
         name="local",
     )(*[in_hbm(jnp.asarray(a)) for a in (streams, taps, cotangent, *tables)], arrived[count - 2])
-    back_rows = rows + rows // 2 + 6 * EDGE
+    extra_rows = -(-(5 * tap_count - 3) // ROW_TILE) * ROW_TILE
+    back_rows = rows + rows // 2 + extra_rows
     f32_rows = lambda extent: pltpu.VMEM((extent, LANES), jnp.float32)
     made = pl.pallas_call(
         functools.partial(main_kernel, count, tap_count, 1.0 / math.sqrt(total)),
@@ -389,27 +413,32 @@
             pltpu.VMEM((total, 2 * LANES), jnp.bfloat16),
             pltpu.VMEM((PHASES, 2 * quarter, 2 * LANES), jnp.float32),
             pltpu.VMEM((PHASES, 2 * quarter, 2 * LANES), jnp.bfloat16),
-            f32_rows(total), f32_rows(total + EDGE), f32_rows(total + EDGE), f32_rows(total),
+            f32_rows(total), f32_rows(total + EDGE), f32_rows(total + EDGE), f32_rows(total), f32_rows(extra_rows),
         ],
         compiler_params=params,
         name="channels",
     )(*arrived, packed[count], *tables_here)
     returned = exchanged(made)
+    outs = [
+        jax.ShapeDtypeStruct(filters.shape, jnp.bfloat16),
+        jax.ShapeDtypeStruct(streams.shape, jnp.bfloat16),
+        jax.ShapeDtypeStruct(filters.shape, jnp.bfloat16),
+        jax.ShapeDtypeStruct(taps.shape, jnp.float32),
+    ]
     return tuple(
         pl.pallas_call(
             functools.partial(finish_kernel, count, tap_count),
-            out_shape=[
-                jax.ShapeDtypeStruct(filters.shape, jnp.bfloat16),
-                jax.ShapeDtypeStruct(streams.shape, jnp.bfloat16),
-                jax.ShapeDtypeStruct(filters.shape, jnp.bfloat16),
-                jax.ShapeDtypeStruct(taps.shape, jnp.float32),
-            ],
+            out_shape=outs,
             in_specs=in_vmem(count + 3),
-            out_specs=in_vmem(4),
-            scratch_shapes=[
+            out_specs=[hbm] * len(outs),
+            scratch_shapes=[pltpu.VMEM(out.shape, out.dtype) for out in outs]
+            + [
                 pltpu.VMEM((count, back_rows, LANES), jnp.bfloat16),
-                f32_rows(2 * EDGE),
+                pltpu.VMEM((2, extra_rows, LANES), jnp.float32),
+                pltpu.VMEM((3, 2 * EDGE, LANES), jnp.float32),
                 pltpu.VMEM((3, rows + EDGE, LANES), jnp.float32),
+                pltpu.SemaphoreType.DMA((count // 2, 3)),
+                pltpu.SemaphoreType.DMA((1,)),
             ],
             compiler_params=params,
             name="finish",

time: 41.1 us -> 40.1 us (0.976)
  starting transfers between devices: 25.4 us -> 24.5 us
    ppermute x14, starting transfers between devices: 25.4 us -> 24.5 us  [exchanged(): lax.ppermute(block, 'ctx', [(source, partner(source, offset, 1, count)) f...]
  transfers between devices with their start and end apart: 14 -> 14, of which waited for: 7 -> 8; matrix products, arithmetic and copies ran while one was open for 0% -> 0% of each run, Pallas kernels for 5% -> 5%
where the time goes in v4:
time: 40.1 us; the launch traced here: 40 us
  starting transfers between devices  24.5 us (61%)
  Pallas kernels  8.45 us (21%)
  waiting for transfers between devices  6.4 us (16%)
  between operations  0.67 us (2%)
    ppermute x14, starting transfers between devices, exchanged(): lax.ppermute(block, 'ctx', [(source, partner(source, offset, 1, count)) f...  24.5 us
    ppermute x14, waiting for transfers between devices, exchanged(): lax.ppermute(block, 'ctx', [(source, partner(source, offset, 1, count)) f...  6.4 us
    pallas_call x1, Pallas kernels, local_dense(): pl.pallas_call(functools.partial(main_kernel, count, tap_count, 1.0 / mat...  3.1 us
    pallas_call x1, Pallas kernels, local_dense(): pl.pallas_call(functools.partial(local_kernel, tap_count), out_shape=[jax...  2.12 us
    pallas_call x1, Pallas kernels, local_dense(): pl.pallas_call(functools.partial(pack_kernel, count), out_shape=[jax.Shap...  1.65 us
    pallas_call x1, Pallas kernels, local_dense(): pl.pallas_call(functools.partial(finish_kernel, count, tap_count), out_sh...  1.57 us
  transfers between devices with their start and end apart: 14, of which 8 were waited for; matrix products, arithmetic and copies ran while one was open for 0% of the time, Pallas kernels for 5%

profile of v4, /device:TPU:0, one launch (start us, length us, event | category | flops | bytes accessed | tf_op | source)
XLA Modules:
  0.0 40.0 jit_solution(13689393860594330036)
XLA Ops:
  0.6 1.7 %pack.1 = (bf16[320,128]{1,0:T(8,128)(2,1)S(1)}, bf16[320,128]{1,0:T(8,128)(2,1)S(1)}, bf16[320,128]{1,0:T(8,128)(2,1)S(1)}, bf16[320,128]{1,0:T(8,128)(2,1)S(1)...) custom-call(bf16[3,128,512]{2,1,0:T(8,128)(2,1)} %streams_hbm.1, ...), custom_call_target="tpu_custom_call" | custom-call | tf_op jit(solution)/shard_map/pack/pallas_call | solution.py:370
  2.3 3.1 %collective-permute-start = (bf16[320,128]{1,0:T(8,128)(2,1)S(1)}, bf16[320,128]{1,0:T(8,128)(2,1)S(1)}, u32[]{:S(2)}, u32[]{:S(2)}) collective-permute-start(bf16[320,128]{1,0:T(8,128)(2,1)S(1)} %get-tuple-element.28), channel_id=1, source_target_pairs={{0,8},{4,12},{8,16},{12,20},{16,24},{20,28},{24,0},{28,4},{1,9},{5... | collective-permute-start | bytes 245768 | tf_op jit(solution)/shard_map/ppermute | solution.py:350
  5.4 1.5 %collective-permute-start.5 = (bf16[320,128]{1,0:T(8,128)(2,1)S(1)}, bf16[320,128]{1,0:T(8,128)(2,1)S(1)}, u32[]{:S(2)}, u32[]{:S(2)}) collective-permute-start(bf16[320,128]{1,0:T(8,128)(2,1)S(1)} %get-tuple-element.33), channel_id=1, source_target_pairs={{0,4},{4,0},{8,12},{12,8},{16,20},{20,16},{24,28},{28,24},{1,5},{5... | collective-permute-start | bytes 245768 | tf_op jit(solution)/shard_map/ppermute | solution.py:350
  6.9 2.6 %collective-permute-start.1 = (bf16[320,128]{1,0:T(8,128)(2,1)S(1)}, bf16[320,128]{1,0:T(8,128)(2,1)S(1)}, u32[]{:S(2)}, u32[]{:S(2)}) collective-permute-start(bf16[320,128]{1,0:T(8,128)(2,1)S(1)} %get-tuple-element.29), channel_id=1, source_target_pairs={{0,16},{4,20},{8,24},{12,28},{16,0},{20,4},{24,8},{28,12},{1,17},{... | collective-permute-start | bytes 245768 | tf_op jit(solution)/shard_map/ppermute | solution.py:350
  9.5 0.0 collective-permute-start.2
  9.5 2.8 %collective-permute-start.3 = (bf16[320,128]{1,0:T(8,128)(2,1)S(1)}, bf16[320,128]{1,0:T(8,128)(2,1)S(1)}, u32[]{:S(2)}, u32[]{:S(2)}) collective-permute-start(bf16[320,128]{1,0:T(8,128)(2,1)S(1)} %get-tuple-element.31), channel_id=1, source_target_pairs={{0,20},{4,16},{8,28},{12,24},{16,4},{20,0},{24,12},{28,8},{1,21},{... | collective-permute-start | bytes 245768 | tf_op jit(solution)/shard_map/ppermute | solution.py:350
  12.3 0.0 collective-permute-done.refs_1_
  12.3 1.9 %collective-permute-start.4 = (bf16[320,128]{1,0:T(8,128)(2,1)S(1)}, bf16[320,128]{1,0:T(8,128)(2,1)S(1)}, u32[]{:S(2)}, u32[]{:S(2)}) collective-permute-start(bf16[320,128]{1,0:T(8,128)(2,1)S(1)} %get-tuple-element.32), channel_id=1, source_target_pairs={{0,28},{4,24},{8,4},{12,0},{16,12},{20,8},{24,20},{28,16},{1,29},{... | collective-permute-start | bytes 245768 | tf_op jit(solution)/shard_map/ppermute | solution.py:350
  14.2 0.0 collective-permute-done.5.arrived_ref.refs_6_
  14.2 0.6 %collective-permute-start.6 = (bf16[320,128]{1,0:T(8,128)(2,1)S(1)}, bf16[320,128]{1,0:T(8,128)(2,1)S(1)}, u32[]{:S(2)}, u32[]{:S(2)}) collective-permute-start(bf16[320,128]{1,0:T(8,128)(2,1)S(1)} %get-tuple-element.34), channel_id=1, source_target_pairs={{0,24},{4,28},{8,0},{12,4},{16,8},{20,12},{24,16},{28,20},{1,25},{... | collective-permute-start | bytes 245768 | tf_op jit(solution)/shard_map/ppermute | solution.py:350
  14.8 2.1 %local.1 = (f32[3,128,512]{2,1,0:T(8,128)S(1)}, f32[3,7,512]{2,1,0:T(8,128)S(1)}, bf16[128,512]{1,0:T(8,128)(2,1)S(1)}, bf16[4,512,256]{2,1,0:T(8,128)(2,1)S(1)}...) custom-call(bf16[3,128,512]{2,1,0:T(8,128)(2,1)} %streams_hbm.1, f32[3,7,512]{2,1,0:T(8,128)} %taps_hbm.1, ...), custom_call_target="tpu_custom_call" | custom-call | tf_op jit(solution)/shard_map/local/pallas_call | solution.py:385
  16.9 0.0 collective-permute-done.1.refs_2_
  17.0 0.4 %collective-permute-done.2.refs_3_ = bf16[320,128]{1,0:T(8,128)(2,1)S(1)} collective-permute-done((bf16[320,128]{1,0:T(8,128)(2,1)S(1)}, bf16[320,128]{1,0:T(8,128)(2,1)S(1)}, u32[]{:S(2)}, u32[]{:S(2)}) %collective-permute-start.2) | collective-permute-done | bytes 81952 | tf_op jit(solution)/shard_map/ppermute | solution.py:350
  17.4 2.4 %collective-permute-done.3.refs_4_ = bf16[320,128]{1,0:T(8,128)(2,1)S(1)} collective-permute-done((bf16[320,128]{1,0:T(8,128)(2,1)S(1)}, bf16[320,128]{1,0:T(8,128)(2,1)S(1)}, u32[]{:S(2)}, u32[]{:S(2)}) %collective-permute-start.3) | collective-permute-done | bytes 81952 | tf_op jit(solution)/shard_map/ppermute | solution.py:350
  19.8 0.6 %collective-permute-done.4.refs_5_ = bf16[320,128]{1,0:T(8,128)(2,1)S(1)} collective-permute-done((bf16[320,128]{1,0:T(8,128)(2,1)S(1)}, bf16[320,128]{1,0:T(8,128)(2,1)S(1)}, u32[]{:S(2)}, u32[]{:S(2)}) %collective-permute-start.4) | collective-permute-done | bytes 81952 | tf_op jit(solution)/shard_map/ppermute | solution.py:350
  20.4 0.0 collective-permute-done.6.refs_7_
  20.5 3.1 %channels.1 = (bf16[224,128]{1,0:T(8,128)(2,1)S(1)}, bf16[224,128]{1,0:T(8,128)(2,1)S(1)}, bf16[224,128]{1,0:T(8,128)(2,1)S(1)}, bf16[224,128]{1,0:T(8,128)(2,1)...) custom-call(bf16[320,128]{1,0:T(8,128)(2,1)S(1)} %get-tuple-element., ...), custom_call_target="tpu_custom_call" | custom-call | tf_op jit(solution)/shard_map/channels/pallas_call | solution.py:406
  23.6 2.3 %collective-permute-start.7 = (bf16[224,128]{1,0:T(8,128)(2,1)S(1)}, bf16[224,128]{1,0:T(8,128)(2,1)S(1)}, u32[]{:S(2)}, u32[]{:S(2)}) collective-permute-start(bf16[224,128]{1,0:T(8,128)(2,1)S(1)} %get-tuple-element.40), channel_id=1, source_target_pairs={{0,8},{4,12},{8,16},{12,20},{16,24},{20,28},{24,0},{28,4},{1,9},{5... | collective-permute-start | bytes 172040 | tf_op jit(solution)/shard_map/ppermute | solution.py:350
  25.8 2.9 %collective-permute-start.8 = (bf16[224,128]{1,0:T(8,128)(2,1)S(1)}, bf16[224,128]{1,0:T(8,128)(2,1)S(1)}, u32[]{:S(2)}, u32[]{:S(2)}) collective-permute-start(bf16[224,128]{1,0:T(8,128)(2,1)S(1)} %get-tuple-element.41), channel_id=1, source_target_pairs={{0,16},{4,20},{8,24},{12,28},{16,0},{20,4},{24,8},{28,12},{1,17},{... | collective-permute-start | bytes 172040 | tf_op jit(solution)/shard_map/ppermute | solution.py:350
  28.7 0.3 collective-permute-start.9
  29.0 1.5 %collective-permute-start.10 = (bf16[224,128]{1,0:T(8,128)(2,1)S(1)}, bf16[224,128]{1,0:T(8,128)(2,1)S(1)}, u32[]{:S(2)}, u32[]{:S(2)}) collective-permute-start(bf16[224,128]{1,0:T(8,128)(2,1)S(1)} %get-tuple-element.43), channel_id=1, source_target_pairs={{0,20},{4,16},{8,28},{12,24},{16,4},{20,0},{24,12},{28,8},{1,21},{... | collective-permute-start | bytes 172040 | tf_op jit(solution)/shard_map/ppermute | solution.py:350
  30.6 3.0 %collective-permute-start.11 = (bf16[224,128]{1,0:T(8,128)(2,1)S(1)}, bf16[224,128]{1,0:T(8,128)(2,1)S(1)}, u32[]{:S(2)}, u32[]{:S(2)}) collective-permute-start(bf16[224,128]{1,0:T(8,128)(2,1)S(1)} %get-tuple-element.44), channel_id=1, source_target_pairs={{0,28},{4,24},{8,4},{12,0},{16,12},{20,8},{24,20},{28,16},{1,29},{... | collective-permute-start | bytes 172040 | tf_op jit(solution)/shard_map/ppermute | solution.py:350
  33.6 0.0 collective-permute-done.7.refs_1_
  33.6 0.7 %collective-permute-start.12 = (bf16[224,128]{1,0:T(8,128)(2,1)S(1)}, bf16[224,128]{1,0:T(8,128)(2,1)S(1)}, u32[]{:S(2)}, u32[]{:S(2)}) collective-permute-start(bf16[224,128]{1,0:T(8,128)(2,1)S(1)} %get-tuple-element.45), channel_id=1, source_target_pairs={{0,4},{4,0},{8,12},{12,8},{16,20},{20,16},{24,28},{28,24},{1,5},{5... | collective-permute-start | bytes 172040 | tf_op jit(solution)/shard_map/ppermute | solution.py:350
  34.2 0.0 collective-permute-done.8.refs_2_
  34.2 1.3 %collective-permute-start.13 = (bf16[224,128]{1,0:T(8,128)(2,1)S(1)}, bf16[224,128]{1,0:T(8,128)(2,1)S(1)}, u32[]{:S(2)}, u32[]{:S(2)}) collective-permute-start(bf16[224,128]{1,0:T(8,128)(2,1)S(1)} %get-tuple-element.46), channel_id=1, source_target_pairs={{0,24},{4,28},{8,0},{12,4},{16,8},{20,12},{24,16},{28,20},{1,25},{... | collective-permute-start | bytes 172040 | tf_op jit(solution)/shard_map/ppermute | solution.py:350
  35.5 0.2 collective-permute-done.9.refs_3_
  35.8 1.0 %collective-permute-done.10.refs_4_ = bf16[224,128]{1,0:T(8,128)(2,1)S(1)} collective-permute-done((bf16[224,128]{1,0:T(8,128)(2,1)S(1)}, bf16[224,128]{1,0:T(8,128)(2,1)S(1)}, u32[]{:S(2)}, u32[]{:S(2)}) %collective-permute-start.10) | collective-permute-done | bytes 57376 | tf_op jit(solution)/shard_map/ppermute | solution.py:350
  36.8 0.3 collective-permute-done.11.refs_5_
  37.1 0.6 %collective-permute-done.12.refs_6_ = bf16[224,128]{1,0:T(8,128)(2,1)S(1)} collective-permute-done((bf16[224,128]{1,0:T(8,128)(2,1)S(1)}, bf16[224,128]{1,0:T(8,128)(2,1)S(1)}, u32[]{:S(2)}, u32[]{:S(2)}) %collective-permute-start.12) | collective-permute-done | bytes 57376 | tf_op jit(solution)/shard_map/ppermute | solution.py:350
  37.8 0.7 %collective-permute-done.13.refs_7_ = bf16[224,128]{1,0:T(8,128)(2,1)S(1)} collective-permute-done((bf16[224,128]{1,0:T(8,128)(2,1)S(1)}, bf16[224,128]{1,0:T(8,128)(2,1)S(1)}, u32[]{:S(2)}, u32[]{:S(2)}) %collective-permute-start.13) | collective-permute-done | bytes 57376 | tf_op jit(solution)/shard_map/ppermute | solution.py:350
  38.4 1.6 %finish.1 = (bf16[128,512]{1,0:T(8,128)(2,1)}, bf16[3,128,512]{2,1,0:T(8,128)(2,1)}, bf16[128,512]{1,0:T(8,128)(2,1)}, f32[3,7,512]{2,1,0:T(8,128)}) custom-call(bf16[224,128]{1,0:T(8,128)(2,1)S(1)} %get-tuple-element.39.refs_0_, bf16[224,128]{1,0:T(8,128)(2,1)S(1)} %collective-permute-done.7.refs_1_, bf16[224,128]{1,0:T(8,128)(2,1)S(1)} %collective-permute-done.8.refs_2_, ...), custom_call_target="tpu_custom_call" | custom-call | tf_op jit(solution)/shard_map/finish/pallas_call | solution.py:429
Async XLA Ops:
  2.3 10.0 %collective-permute-start = (bf16[320,128]{1,0:T(8,128)(2,1)S(1)}, bf16[320,128]{1,0:T(8,128)(2,1)S(1)}, u32[]{:S(2)}, u32[]{:S(2)}) collective-permute-start(bf16[320,128]{1,0:T(8,128)(2,1)S(1)} %get-tuple-element.28), channel_id=1, source_target_pairs={{0,8},{4,12},{8,16},{12,20},{16,24},{20,28},{24,0},{28,4},{1,9},{5... | collective-permute-start | bytes 245768 | tf_op jit(solution)/shard_map/ppermute | solution.py:350
  5.4 8.8 %collective-permute-start.5 = (bf16[320,128]{1,0:T(8,128)(2,1)S(1)}, bf16[320,128]{1,0:T(8,128)(2,1)S(1)}, u32[]{:S(2)}, u32[]{:S(2)}) collective-permute-start(bf16[320,128]{1,0:T(8,128)(2,1)S(1)} %get-tuple-element.33), channel_id=1, source_target_pairs={{0,4},{4,0},{8,12},{12,8},{16,20},{20,16},{24,28},{28,24},{1,5},{5... | collective-permute-start | bytes 245768 | tf_op jit(solution)/shard_map/ppermute | solution.py:350
  6.9 10.1 %collective-permute-start.1 = (bf16[320,128]{1,0:T(8,128)(2,1)S(1)}, bf16[320,128]{1,0:T(8,128)(2,1)S(1)}, u32[]{:S(2)}, u32[]{:S(2)}) collective-permute-start(bf16[320,128]{1,0:T(8,128)(2,1)S(1)} %get-tuple-element.29), channel_id=1, source_target_pairs={{0,16},{4,20},{8,24},{12,28},{16,0},{20,4},{24,8},{28,12},{1,17},{... | collective-permute-start | bytes 245768 | tf_op jit(solution)/shard_map/ppermute | solution.py:350
  9.5 7.9 %collective-permute-start.2 = (bf16[320,128]{1,0:T(8,128)(2,1)S(1)}, bf16[320,128]{1,0:T(8,128)(2,1)S(1)}, u32[]{:S(2)}, u32[]{:S(2)}) collective-permute-start(bf16[320,128]{1,0:T(8,128)(2,1)S(1)} %get-tuple-element.30), channel_id=1, source_target_pairs={{0,12},{4,8},{8,20},{12,16},{16,28},{20,24},{24,4},{28,0},{1,13},{... | collective-permute-start | bytes 245768 | tf_op jit(solution)/shard_map/ppermute | solution.py:350
  9.5 10.3 %collective-permute-start.3 = (bf16[320,128]{1,0:T(8,128)(2,1)S(1)}, bf16[320,128]{1,0:T(8,128)(2,1)S(1)}, u32[]{:S(2)}, u32[]{:S(2)}) collective-permute-start(bf16[320,128]{1,0:T(8,128)(2,1)S(1)} %get-tuple-element.31), channel_id=1, source_target_pairs={{0,20},{4,16},{8,28},{12,24},{16,4},{20,0},{24,12},{28,8},{1,21},{... | collective-permute-start | bytes 245768 | tf_op jit(solution)/shard_map/ppermute | solution.py:350
  12.3 8.2 %collective-permute-start.4 = (bf16[320,128]{1,0:T(8,128)(2,1)S(1)}, bf16[320,128]{1,0:T(8,128)(2,1)S(1)}, u32[]{:S(2)}, u32[]{:S(2)}) collective-permute-start(bf16[320,128]{1,0:T(8,128)(2,1)S(1)} %get-tuple-element.32), channel_id=1, source_target_pairs={{0,28},{4,24},{8,4},{12,0},{16,12},{20,8},{24,20},{28,16},{1,29},{... | collective-permute-start | bytes 245768 | tf_op jit(solution)/shard_map/ppermute | solution.py:350
  14.2 6.2 %collective-permute-start.6 = (bf16[320,128]{1,0:T(8,128)(2,1)S(1)}, bf16[320,128]{1,0:T(8,128)(2,1)S(1)}, u32[]{:S(2)}, u32[]{:S(2)}) collective-permute-start(bf16[320,128]{1,0:T(8,128)(2,1)S(1)} %get-tuple-element.34), channel_id=1, source_target_pairs={{0,24},{4,28},{8,0},{12,4},{16,8},{20,12},{24,16},{28,20},{1,25},{... | collective-permute-start | bytes 245768 | tf_op jit(solution)/shard_map/ppermute | solution.py:350
  23.6 10.0 %collective-permute-start.7 = (bf16[224,128]{1,0:T(8,128)(2,1)S(1)}, bf16[224,128]{1,0:T(8,128)(2,1)S(1)}, u32[]{:S(2)}, u32[]{:S(2)}) collective-permute-start(bf16[224,128]{1,0:T(8,128)(2,1)S(1)} %get-tuple-element.40), channel_id=1, source_target_pairs={{0,8},{4,12},{8,16},{12,20},{16,24},{20,28},{24,0},{28,4},{1,9},{5... | collective-permute-start | bytes 172040 | tf_op jit(solution)/shard_map/ppermute | solution.py:350
  25.8 8.4 %collective-permute-start.8 = (bf16[224,128]{1,0:T(8,128)(2,1)S(1)}, bf16[224,128]{1,0:T(8,128)(2,1)S(1)}, u32[]{:S(2)}, u32[]{:S(2)}) collective-permute-start(bf16[224,128]{1,0:T(8,128)(2,1)S(1)} %get-tuple-element.41), channel_id=1, source_target_pairs={{0,16},{4,20},{8,24},{12,28},{16,0},{20,4},{24,8},{28,12},{1,17},{... | collective-permute-start | bytes 172040 | tf_op jit(solution)/shard_map/ppermute | solution.py:350
  28.7 7.1 %collective-permute-start.9 = (bf16[224,128]{1,0:T(8,128)(2,1)S(1)}, bf16[224,128]{1,0:T(8,128)(2,1)S(1)}, u32[]{:S(2)}, u32[]{:S(2)}) collective-permute-start(bf16[224,128]{1,0:T(8,128)(2,1)S(1)} %get-tuple-element.42), channel_id=1, source_target_pairs={{0,12},{4,8},{8,20},{12,16},{16,28},{20,24},{24,4},{28,0},{1,13},{... | collective-permute-start | bytes 172040 | tf_op jit(solution)/shard_map/ppermute | solution.py:350
  29.0 7.8 %collective-permute-start.10 = (bf16[224,128]{1,0:T(8,128)(2,1)S(1)}, bf16[224,128]{1,0:T(8,128)(2,1)S(1)}, u32[]{:S(2)}, u32[]{:S(2)}) collective-permute-start(bf16[224,128]{1,0:T(8,128)(2,1)S(1)} %get-tuple-element.43), channel_id=1, source_target_pairs={{0,20},{4,16},{8,28},{12,24},{16,4},{20,0},{24,12},{28,8},{1,21},{... | collective-permute-start | bytes 172040 | tf_op jit(solution)/shard_map/ppermute | solution.py:350
  30.6 6.6 %collective-permute-start.11 = (bf16[224,128]{1,0:T(8,128)(2,1)S(1)}, bf16[224,128]{1,0:T(8,128)(2,1)S(1)}, u32[]{:S(2)}, u32[]{:S(2)}) collective-permute-start(bf16[224,128]{1,0:T(8,128)(2,1)S(1)} %get-tuple-element.44), channel_id=1, source_target_pairs={{0,28},{4,24},{8,4},{12,0},{16,12},{20,8},{24,20},{28,16},{1,29},{... | collective-permute-start | bytes 172040 | tf_op jit(solution)/shard_map/ppermute | solution.py:350
  33.6 4.2 %collective-permute-start.12 = (bf16[224,128]{1,0:T(8,128)(2,1)S(1)}, bf16[224,128]{1,0:T(8,128)(2,1)S(1)}, u32[]{:S(2)}, u32[]{:S(2)}) collective-permute-start(bf16[224,128]{1,0:T(8,128)(2,1)S(1)} %get-tuple-element.45), channel_id=1, source_target_pairs={{0,4},{4,0},{8,12},{12,8},{16,20},{20,16},{24,28},{28,24},{1,5},{5... | collective-permute-start | bytes 172040 | tf_op jit(solution)/shard_map/ppermute | solution.py:350
  34.2 4.2 %collective-permute-start.13 = (bf16[224,128]{1,0:T(8,128)(2,1)S(1)}, bf16[224,128]{1,0:T(8,128)(2,1)S(1)}, u32[]{:S(2)}, u32[]{:S(2)}) collective-permute-start(bf16[224,128]{1,0:T(8,128)(2,1)S(1)} %get-tuple-element.46), channel_id=1, source_target_pairs={{0,24},{4,28},{8,0},{12,4},{16,8},{20,12},{24,16},{28,20},{1,25},{... | collective-permute-start | bytes 172040 | tf_op jit(solution)/shard_map/ppermute | solution.py:350

commit v5 on v4

--- a/solution.py
+++ b/solution.py
@@ -19,13 +19,18 @@
 VMEM_BYTES = 32 * 1024 * 1024
 
 
-def step_offsets(count):
+def step_offsets(count, back=False):
     groups = count // 2
     far = groups // 2
     near = [g for g in range(1, groups) if g != far]
-    order = [(g, 0) for g in near[:1]] + [(far, 0)] + [(g, 1) for g in near[:1]] + [(far, 1)]
-    order = order + [(g, 1) for g in near[1:]] + [(0, 1)] + [(g, 0) for g in near[1:]]
-    return [(0, 0)] + [offset for offset in order if offset != (0, 0)]
+    first, last = near[:1], near[1:]
+    if back:
+        order = [(far, 0)] + [(g, m) for g in first for m in (0, 1)] + [(far, 1)]
+        order = order + [(g, 1) for g in last] + [(g, 0) for g in last] + [(0, 1)]
+    else:
+        order = [(far, 0), (0, 1), (far, 1)] + [(g, m) for g in first for m in (1, 0)]
+        order = order + [(g, 1) for g in last] + [(g, 0) for g in last]
+    return [(0, 0)] + [offset for offset in dict.fromkeys(order) if offset != (0, 0)]
 
 
 def partner(index, offset, sign, count):
@@ -135,8 +140,8 @@
         2 * count + 4 :
     ]
     me = lax.axis_index("ctx")
-    offsets = step_offsets(count)
-    total = raw_lag.shape[0]
+    offsets, back_offsets = step_offsets(count), step_offsets(count, back=True)
+    total = signals.shape[0]
     quarter = total // PHASES
     rows = total // count
     half_rows = rows // 2
@@ -239,7 +244,7 @@
     extra[3 * reach : 3 * reach + tap_count, :] = sums_kv
     extra[3 * reach + tap_count : 3 * reach + 2 * tap_count, :] = jnp.where(low_taps, high_q, turned(sums_q - high_q))
     for step in range(count):
-        owner = partner(me, offsets[step], 1, count)
+        owner = partner(me, back_offsets[step], 1, count)
         base = pl.multiple_of(owner * rows, rows)
         out = out_refs[step]
         out[0:rows, :] = pairs[pl.ds(base, rows), :].astype(jnp.bfloat16)
@@ -251,7 +256,7 @@
         extra[2 * reach : 3 * reach, :] = jnp.where(
             low_reach, raw_qc[pl.ds(base + EDGE - reach, reach), :], turned(grad_q[pl.ds(base + rows, reach), :])
         )
-        out[rows + half_rows :, :] = extra[...].astype(jnp.bfloat16)
+        out[rows + half_rows :, :] = extra[: out.shape[0] - rows - half_rows, :].astype(jnp.bfloat16)
 
 
 def shifted_sum(taps, padded, first, direction, rows):
@@ -287,13 +292,14 @@
     out_hbm = refs[count + 3 : count + 7]
     gated_ref, stream_ref, lag_ref, tap_ref, blocks, extras, edges, grads, sems, tap_sem = refs[count + 7 :]
     me = lax.axis_index("ctx")
-    offsets = step_offsets(count)
+    offsets = step_offsets(count, back=True)
     rows = gated_ref.shape[0]
     half_rows = rows // 2
     reach = tap_count - 1
     low = lower_lanes(rows)
     low_half = lower_lanes(half_rows)
-    low_extra = lower_lanes(extras.shape[1])
+    extent = extras.shape[1] - EDGE
+    low_extra = lower_lanes(extent)
     low_taps = lower_lanes(tap_count)
     for step in range(count):
         owner = partner(me, offsets[step], -1, count)
@@ -308,7 +314,7 @@
             return jnp.where(mask, even, turned(odd)), jnp.where(mask, turned(even), odd)
 
         extra_rows = slice(rows + half_rows, None)
-        extras[0, :, :], extras[1, :, :] = both(extra_rows, low_extra)
+        extras[0, :extent, :], extras[1, :extent, :] = both(extra_rows, low_extra)
         mixed, product_grad = both(slice(0, rows), low)
         lag_lower, lag_upper = both(slice(rows, rows + half_rows), low_half)
         lag_ref[0:half_rows, cols] = lag_lower.astype(jnp.bfloat16)
@@ -344,11 +350,11 @@
         copy.wait()
 
 
-def exchanged(blocks):
+def exchanged(blocks, back=False):
     count = len(blocks)
     return [blocks[0]] + [
         lax.ppermute(block, "ctx", [(source, partner(source, offset, 1, count)) for source in range(count)])
-        for block, offset in zip(blocks[1:], step_offsets(count)[1:])
+        for block, offset in zip(blocks[1:], step_offsets(count, back)[1:])
     ]
 
 
@@ -399,7 +405,7 @@
         ],
         compiler_params=params,
         name="local",
-    )(*[in_hbm(jnp.asarray(a)) for a in (streams, taps, cotangent, *tables)], arrived[count - 2])
+    )(*[in_hbm(jnp.asarray(a)) for a in (streams, taps, cotangent, *tables)], arrived[min(2, count - 1)])
     extra_rows = -(-(5 * tap_count - 3) // ROW_TILE) * ROW_TILE
     back_rows = rows + rows // 2 + extra_rows
     f32_rows = lambda extent: pltpu.VMEM((extent, LANES), jnp.float32)
@@ -409,16 +415,17 @@
         in_specs=in_vmem(count + 1 + len(tables)),
         out_specs=in_vmem(count),
         scratch_shapes=[
-            f32_rows(total + EDGE), f32_rows(total + EDGE), f32_rows(total), f32_rows(total), f32_rows(total),
+            f32_rows(total + 2 * EDGE), f32_rows(total + 2 * EDGE), f32_rows(total + EDGE), f32_rows(total), f32_rows(total),
             pltpu.VMEM((total, 2 * LANES), jnp.bfloat16),
             pltpu.VMEM((PHASES, 2 * quarter, 2 * LANES), jnp.float32),
             pltpu.VMEM((PHASES, 2 * quarter, 2 * LANES), jnp.bfloat16),
-            f32_rows(total), f32_rows(total + EDGE), f32_rows(total + EDGE), f32_rows(total), f32_rows(extra_rows),
+            f32_rows(total + EDGE), f32_rows(total + EDGE), f32_rows(total + EDGE), f32_rows(total + EDGE),
+            f32_rows(extra_rows + EDGE),
         ],
         compiler_params=params,
         name="channels",
     )(*arrived, packed[count], *tables_here)
-    returned = exchanged(made)
+    returned = exchanged(made, back=True)
     outs = [
         jax.ShapeDtypeStruct(filters.shape, jnp.bfloat16),
         jax.ShapeDtypeStruct(streams.shape, jnp.bfloat16),
@@ -434,9 +441,9 @@
             scratch_shapes=[pltpu.VMEM(out.shape, out.dtype) for out in outs]
             + [
                 pltpu.VMEM((count, back_rows, LANES), jnp.bfloat16),
-                pltpu.VMEM((2, extra_rows, LANES), jnp.float32),
+                pltpu.VMEM((2, extra_rows + EDGE, LANES), jnp.float32),
                 pltpu.VMEM((3, 2 * EDGE, LANES), jnp.float32),
-                pltpu.VMEM((3, rows + EDGE, LANES), jnp.float32),
+                pltpu.VMEM((3, rows + 2 * EDGE, LANES), jnp.float32),
                 pltpu.SemaphoreType.DMA((count // 2, 3)),
                 pltpu.SemaphoreType.DMA((1,)),
             ],

time: 40.1 us -> 39.8 us (level)
  waiting for transfers between devices: 6.4 us -> 5.14 us
  starting transfers between devices: 24.5 us -> 25.4 us
    ppermute x14, waiting for transfers between devices: 6.4 us -> 5.14 us  [exchanged(): lax.ppermute(block, 'ctx', [(source, partner(source, offset, 1, count)) f...]
    ppermute x14, starting transfers between devices: 24.5 us -> 25.4 us  [exchanged(): lax.ppermute(block, 'ctx', [(source, partner(source, offset, 1, count)) f...]
  transfers between devices with their start and end apart: 14 -> 14, of which waited for: 8 -> 7; matrix products, arithmetic and copies ran while one was open for 0% -> 0% of each run, Pallas kernels for 5% -> 5%
where the time goes in v5:
time: 39.8 us; the launch traced here: 39.6 us
  starting transfers between devices  25.4 us (64%)
  Pallas kernels  8.44 us (21%)
  waiting for transfers between devices  5.14 us (13%)
  between operations  0.66 us (2%)
    ppermute x14, starting transfers between devices, exchanged(): lax.ppermute(block, 'ctx', [(source, partner(source, offset, 1, count)) f...  25.4 us
    ppermute x14, waiting for transfers between devices, exchanged(): lax.ppermute(block, 'ctx', [(source, partner(source, offset, 1, count)) f...  5.14 us
    pallas_call x1, Pallas kernels, local_dense(): pl.pallas_call(functools.partial(main_kernel, count, tap_count, 1.0 / mat...  3.1 us
    pallas_call x1, Pallas kernels, local_dense(): pl.pallas_call(functools.partial(local_kernel, tap_count), out_shape=[jax...  2.13 us
    pallas_call x1, Pallas kernels, local_dense(): pl.pallas_call(functools.partial(pack_kernel, count), out_shape=[jax.Shap...  1.65 us
    pallas_call x1, Pallas kernels, local_dense(): pl.pallas_call(functools.partial(finish_kernel, count, tap_count), out_sh...  1.57 us
  transfers between devices with their start and end apart: 14, of which 7 were waited for; matrix products, arithmetic and copies ran while one was open for 0% of the time, Pallas kernels for 5%

profile of v5, /device:TPU:0, one launch (start us, length us, event | category | flops | bytes accessed | tf_op | source)
XLA Modules:
  0.0 39.6 jit_solution(13580041619810466344)
XLA Ops:
  0.6 1.7 %pack.1 = (bf16[320,128]{1,0:T(8,128)(2,1)S(1)}, bf16[320,128]{1,0:T(8,128)(2,1)S(1)}, bf16[320,128]{1,0:T(8,128)(2,1)S(1)}, bf16[320,128]{1,0:T(8,128)(2,1)S(1)...) custom-call(bf16[3,128,512]{2,1,0:T(8,128)(2,1)} %streams_hbm.1, ...), custom_call_target="tpu_custom_call" | custom-call | tf_op jit(solution)/shard_map/pack/pallas_call | solution.py:376
  2.3 4.1 %collective-permute-start = (bf16[320,128]{1,0:T(8,128)(2,1)S(1)}, bf16[320,128]{1,0:T(8,128)(2,1)S(1)}, u32[]{:S(2)}, u32[]{:S(2)}) collective-permute-start(bf16[320,128]{1,0:T(8,128)(2,1)S(1)} %get-tuple-element.28), channel_id=1, source_target_pairs={{0,16},{4,20},{8,24},{12,28},{16,0},{20,4},{24,8},{28,12},{1,17},{... | collective-permute-start | bytes 245768 | tf_op jit(solution)/shard_map/ppermute | solution.py:356
  6.4 1.5 %collective-permute-start.1 = (bf16[320,128]{1,0:T(8,128)(2,1)S(1)}, bf16[320,128]{1,0:T(8,128)(2,1)S(1)}, u32[]{:S(2)}, u32[]{:S(2)}) collective-permute-start(bf16[320,128]{1,0:T(8,128)(2,1)S(1)} %get-tuple-element.29), channel_id=1, source_target_pairs={{0,4},{4,0},{8,12},{12,8},{16,20},{20,16},{24,28},{28,24},{1,5},{5... | collective-permute-start | bytes 245768 | tf_op jit(solution)/shard_map/ppermute | solution.py:356
  7.9 0.0 collective-permute-start.2
  7.9 2.8 %collective-permute-start.3 = (bf16[320,128]{1,0:T(8,128)(2,1)S(1)}, bf16[320,128]{1,0:T(8,128)(2,1)S(1)}, u32[]{:S(2)}, u32[]{:S(2)}) collective-permute-start(bf16[320,128]{1,0:T(8,128)(2,1)S(1)} %get-tuple-element.31), channel_id=1, source_target_pairs={{0,12},{4,8},{8,20},{12,16},{16,28},{20,24},{24,4},{28,0},{1,13},{... | collective-permute-start | bytes 245768 | tf_op jit(solution)/shard_map/ppermute | solution.py:356
  10.7 1.6 %collective-permute-start.4 = (bf16[320,128]{1,0:T(8,128)(2,1)S(1)}, bf16[320,128]{1,0:T(8,128)(2,1)S(1)}, u32[]{:S(2)}, u32[]{:S(2)}) collective-permute-start(bf16[320,128]{1,0:T(8,128)(2,1)S(1)} %get-tuple-element.32), channel_id=1, source_target_pairs={{0,8},{4,12},{8,16},{12,20},{16,24},{20,28},{24,0},{28,4},{1,9},{5... | collective-permute-start | bytes 245768 | tf_op jit(solution)/shard_map/ppermute | solution.py:356
  12.3 0.0 collective-permute-done.refs_1_
  12.3 4.8 %collective-permute-start.5 = (bf16[320,128]{1,0:T(8,128)(2,1)S(1)}, bf16[320,128]{1,0:T(8,128)(2,1)S(1)}, u32[]{:S(2)}, u32[]{:S(2)}) collective-permute-start(bf16[320,128]{1,0:T(8,128)(2,1)S(1)} %get-tuple-element.33), channel_id=1, source_target_pairs={{0,28},{4,24},{8,4},{12,0},{16,12},{20,8},{24,20},{28,16},{1,29},{... | collective-permute-start | bytes 245768 | tf_op jit(solution)/shard_map/ppermute | solution.py:356
  17.1 0.0 collective-permute-done.1.arrived_ref.refs_2_
  17.1 0.0 collective-permute-start.6
  17.1 2.1 %local.1 = (f32[3,128,512]{2,1,0:T(8,128)S(1)}, f32[3,7,512]{2,1,0:T(8,128)S(1)}, bf16[128,512]{1,0:T(8,128)(2,1)S(1)}, bf16[4,512,256]{2,1,0:T(8,128)(2,1)S(1)}...) custom-call(bf16[3,128,512]{2,1,0:T(8,128)(2,1)} %streams_hbm.1, f32[3,7,512]{2,1,0:T(8,128)} %taps_hbm.1, ...), custom_call_target="tpu_custom_call" | custom-call | tf_op jit(solution)/shard_map/local/pallas_call | solution.py:391
  19.2 0.3 collective-permute-done.2.refs_3_
  19.6 0.0 collective-permute-done.3.refs_4_
  19.6 0.0 collective-permute-done.4.refs_5_
  19.6 0.4 collective-permute-done.5.refs_6_
  20.0 1.6 %collective-permute-done.6.refs_7_ = bf16[320,128]{1,0:T(8,128)(2,1)S(1)} collective-permute-done((bf16[320,128]{1,0:T(8,128)(2,1)S(1)}, bf16[320,128]{1,0:T(8,128)(2,1)S(1)}, u32[]{:S(2)}, u32[]{:S(2)}) %collective-permute-start.6) | collective-permute-done | bytes 81952 | tf_op jit(solution)/shard_map/ppermute | solution.py:356
  21.5 3.1 %channels.1 = (bf16[224,128]{1,0:T(8,128)(2,1)S(1)}, bf16[224,128]{1,0:T(8,128)(2,1)S(1)}, bf16[224,128]{1,0:T(8,128)(2,1)S(1)}, bf16[224,128]{1,0:T(8,128)(2,1)...) custom-call(bf16[320,128]{1,0:T(8,128)(2,1)S(1)} %get-tuple-element., ...), custom_call_target="tpu_custom_call" | custom-call | tf_op jit(solution)/shard_map/channels/pallas_call | solution.py:412
  24.6 2.4 %collective-permute-start.7 = (bf16[224,128]{1,0:T(8,128)(2,1)S(1)}, bf16[224,128]{1,0:T(8,128)(2,1)S(1)}, u32[]{:S(2)}, u32[]{:S(2)}) collective-permute-start(bf16[224,128]{1,0:T(8,128)(2,1)S(1)} %get-tuple-element.40), channel_id=1, source_target_pairs={{0,16},{4,20},{8,24},{12,28},{16,0},{20,4},{24,8},{28,12},{1,17},{... | collective-permute-start | bytes 172040 | tf_op jit(solution)/shard_map/ppermute | solution.py:356
  27.0 1.4 %collective-permute-start.8 = (bf16[224,128]{1,0:T(8,128)(2,1)S(1)}, bf16[224,128]{1,0:T(8,128)(2,1)S(1)}, u32[]{:S(2)}, u32[]{:S(2)}) collective-permute-start(bf16[224,128]{1,0:T(8,128)(2,1)S(1)} %get-tuple-element.41), channel_id=1, source_target_pairs={{0,8},{4,12},{8,16},{12,20},{16,24},{20,28},{24,0},{28,4},{1,9},{5... | collective-permute-start | bytes 172040 | tf_op jit(solution)/shard_map/ppermute | solution.py:356
  28.4 0.1 collective-permute-start.9
  28.5 3.8 %collective-permute-start.10 = (bf16[224,128]{1,0:T(8,128)(2,1)S(1)}, bf16[224,128]{1,0:T(8,128)(2,1)S(1)}, u32[]{:S(2)}, u32[]{:S(2)}) collective-permute-start(bf16[224,128]{1,0:T(8,128)(2,1)S(1)} %get-tuple-element.43), channel_id=1, source_target_pairs={{0,20},{4,16},{8,28},{12,24},{16,4},{20,0},{24,12},{28,8},{1,21},{... | collective-permute-start | bytes 172040 | tf_op jit(solution)/shard_map/ppermute | solution.py:356
  32.3 0.9 %collective-permute-start.11 = (bf16[224,128]{1,0:T(8,128)(2,1)S(1)}, bf16[224,128]{1,0:T(8,128)(2,1)S(1)}, u32[]{:S(2)}, u32[]{:S(2)}) collective-permute-start(bf16[224,128]{1,0:T(8,128)(2,1)S(1)} %get-tuple-element.44), channel_id=1, source_target_pairs={{0,28},{4,24},{8,4},{12,0},{16,12},{20,8},{24,20},{28,16},{1,29},{... | collective-permute-start | bytes 172040 | tf_op jit(solution)/shard_map/ppermute | solution.py:356
  33.2 0.0 collective-permute-done.7.refs_1_
  33.2 0.6 %collective-permute-start.12 = (bf16[224,128]{1,0:T(8,128)(2,1)S(1)}, bf16[224,128]{1,0:T(8,128)(2,1)S(1)}, u32[]{:S(2)}, u32[]{:S(2)}) collective-permute-start(bf16[224,128]{1,0:T(8,128)(2,1)S(1)} %get-tuple-element.45), channel_id=1, source_target_pairs={{0,24},{4,28},{8,0},{12,4},{16,8},{20,12},{24,16},{28,20},{1,25},{... | collective-permute-start | bytes 172040 | tf_op jit(solution)/shard_map/ppermute | solution.py:356
  33.8 0.0 collective-permute-done.8.refs_2_
  33.8 1.4 %collective-permute-start.13 = (bf16[224,128]{1,0:T(8,128)(2,1)S(1)}, bf16[224,128]{1,0:T(8,128)(2,1)S(1)}, u32[]{:S(2)}, u32[]{:S(2)}) collective-permute-start(bf16[224,128]{1,0:T(8,128)(2,1)S(1)} %get-tuple-element.46), channel_id=1, source_target_pairs={{0,4},{4,0},{8,12},{12,8},{16,20},{20,16},{24,28},{28,24},{1,5},{5... | collective-permute-start | bytes 172040 | tf_op jit(solution)/shard_map/ppermute | solution.py:356
  35.2 0.7 %collective-permute-done.9.refs_3_ = bf16[224,128]{1,0:T(8,128)(2,1)S(1)} collective-permute-done((bf16[224,128]{1,0:T(8,128)(2,1)S(1)}, bf16[224,128]{1,0:T(8,128)(2,1)S(1)}, u32[]{:S(2)}, u32[]{:S(2)}) %collective-permute-start.9) | collective-permute-done | bytes 57376 | tf_op jit(solution)/shard_map/ppermute | solution.py:356
  35.9 1.0 %collective-permute-done.10.refs_4_ = bf16[224,128]{1,0:T(8,128)(2,1)S(1)} collective-permute-done((bf16[224,128]{1,0:T(8,128)(2,1)S(1)}, bf16[224,128]{1,0:T(8,128)(2,1)S(1)}, u32[]{:S(2)}, u32[]{:S(2)}) %collective-permute-start.10) | collective-permute-done | bytes 57376 | tf_op jit(solution)/shard_map/ppermute | solution.py:356
  36.9 0.5 %collective-permute-done.11.refs_5_ = bf16[224,128]{1,0:T(8,128)(2,1)S(1)} collective-permute-done((bf16[224,128]{1,0:T(8,128)(2,1)S(1)}, bf16[224,128]{1,0:T(8,128)(2,1)S(1)}, u32[]{:S(2)}, u32[]{:S(2)}) %collective-permute-start.11) | collective-permute-done | bytes 57376 | tf_op jit(solution)/shard_map/ppermute | solution.py:356
  37.4 0.6 %collective-permute-done.12.refs_6_ = bf16[224,128]{1,0:T(8,128)(2,1)S(1)} collective-permute-done((bf16[224,128]{1,0:T(8,128)(2,1)S(1)}, bf16[224,128]{1,0:T(8,128)(2,1)S(1)}, u32[]{:S(2)}, u32[]{:S(2)}) %collective-permute-start.12) | collective-permute-done | bytes 57376 | tf_op jit(solution)/shard_map/ppermute | solution.py:356
  38.0 0.0 collective-permute-done.13.refs_7_
  38.0 1.6 %finish.1 = (bf16[128,512]{1,0:T(8,128)(2,1)}, bf16[3,128,512]{2,1,0:T(8,128)(2,1)}, bf16[128,512]{1,0:T(8,128)(2,1)}, f32[3,7,512]{2,1,0:T(8,128)}) custom-call(bf16[224,128]{1,0:T(8,128)(2,1)S(1)} %get-tuple-element.39.refs_0_, bf16[224,128]{1,0:T(8,128)(2,1)S(1)} %collective-permute-done.7.refs_1_, bf16[224,128]{1,0:T(8,128)(2,1)S(1)} %collective-permute-done.8.refs_2_, ...), custom_call_target="tpu_custom_call" | custom-call | tf_op jit(solution)/shard_map/finish/pallas_call | solution.py:436
Async XLA Ops:
  2.3 10.0 %collective-permute-start = (bf16[320,128]{1,0:T(8,128)(2,1)S(1)}, bf16[320,128]{1,0:T(8,128)(2,1)S(1)}, u32[]{:S(2)}, u32[]{:S(2)}) collective-permute-start(bf16[320,128]{1,0:T(8,128)(2,1)S(1)} %get-tuple-element.28), channel_id=1, source_target_pairs={{0,16},{4,20},{8,24},{12,28},{16,0},{20,4},{24,8},{28,12},{1,17},{... | collective-permute-start | bytes 245768 | tf_op jit(solution)/shard_map/ppermute | solution.py:356
  6.4 10.7 %collective-permute-start.1 = (bf16[320,128]{1,0:T(8,128)(2,1)S(1)}, bf16[320,128]{1,0:T(8,128)(2,1)S(1)}, u32[]{:S(2)}, u32[]{:S(2)}) collective-permute-start(bf16[320,128]{1,0:T(8,128)(2,1)S(1)} %get-tuple-element.29), channel_id=1, source_target_pairs={{0,4},{4,0},{8,12},{12,8},{16,20},{20,16},{24,28},{28,24},{1,5},{5... | collective-permute-start | bytes 245768 | tf_op jit(solution)/shard_map/ppermute | solution.py:356
  7.9 11.6 %collective-permute-start.2 = (bf16[320,128]{1,0:T(8,128)(2,1)S(1)}, bf16[320,128]{1,0:T(8,128)(2,1)S(1)}, u32[]{:S(2)}, u32[]{:S(2)}) collective-permute-start(bf16[320,128]{1,0:T(8,128)(2,1)S(1)} %get-tuple-element.30), channel_id=1, source_target_pairs={{0,20},{4,16},{8,28},{12,24},{16,4},{20,0},{24,12},{28,8},{1,21},{... | collective-permute-start | bytes 245768 | tf_op jit(solution)/shard_map/ppermute | solution.py:356
  7.9 11.6 %collective-permute-start.3 = (bf16[320,128]{1,0:T(8,128)(2,1)S(1)}, bf16[320,128]{1,0:T(8,128)(2,1)S(1)}, u32[]{:S(2)}, u32[]{:S(2)}) collective-permute-start(bf16[320,128]{1,0:T(8,128)(2,1)S(1)} %get-tuple-element.31), channel_id=1, source_target_pairs={{0,12},{4,8},{8,20},{12,16},{16,28},{20,24},{24,4},{28,0},{1,13},{... | collective-permute-start | bytes 245768 | tf_op jit(solution)/shard_map/ppermute | solution.py:356
  10.7 8.8 %collective-permute-start.4 = (bf16[320,128]{1,0:T(8,128)(2,1)S(1)}, bf16[320,128]{1,0:T(8,128)(2,1)S(1)}, u32[]{:S(2)}, u32[]{:S(2)}) collective-permute-start(bf16[320,128]{1,0:T(8,128)(2,1)S(1)} %get-tuple-element.32), channel_id=1, source_target_pairs={{0,8},{4,12},{8,16},{12,20},{16,24},{20,28},{24,0},{28,4},{1,9},{5... | collective-permute-start | bytes 245768 | tf_op jit(solution)/shard_map/ppermute | solution.py:356
  12.3 7.6 %collective-permute-start.5 = (bf16[320,128]{1,0:T(8,128)(2,1)S(1)}, bf16[320,128]{1,0:T(8,128)(2,1)S(1)}, u32[]{:S(2)}, u32[]{:S(2)}) collective-permute-start(bf16[320,128]{1,0:T(8,128)(2,1)S(1)} %get-tuple-element.33), channel_id=1, source_target_pairs={{0,28},{4,24},{8,4},{12,0},{16,12},{20,8},{24,20},{28,16},{1,29},{... | collective-permute-start | bytes 245768 | tf_op jit(solution)/shard_map/ppermute | solution.py:356
  17.1 4.4 %collective-permute-start.6 = (bf16[320,128]{1,0:T(8,128)(2,1)S(1)}, bf16[320,128]{1,0:T(8,128)(2,1)S(1)}, u32[]{:S(2)}, u32[]{:S(2)}) collective-permute-start(bf16[320,128]{1,0:T(8,128)(2,1)S(1)} %get-tuple-element.34), channel_id=1, source_target_pairs={{0,24},{4,28},{8,0},{12,4},{16,8},{20,12},{24,16},{28,20},{1,25},{... | collective-permute-start | bytes 245768 | tf_op jit(solution)/shard_map/ppermute | solution.py:356
  24.6 8.5 %collective-permute-start.7 = (bf16[224,128]{1,0:T(8,128)(2,1)S(1)}, bf16[224,128]{1,0:T(8,128)(2,1)S(1)}, u32[]{:S(2)}, u32[]{:S(2)}) collective-permute-start(bf16[224,128]{1,0:T(8,128)(2,1)S(1)} %get-tuple-element.40), channel_id=1, source_target_pairs={{0,16},{4,20},{8,24},{12,28},{16,0},{20,4},{24,8},{28,12},{1,17},{... | collective-permute-start | bytes 172040 | tf_op jit(solution)/shard_map/ppermute | solution.py:356
  27.0 6.8 %collective-permute-start.8 = (bf16[224,128]{1,0:T(8,128)(2,1)S(1)}, bf16[224,128]{1,0:T(8,128)(2,1)S(1)}, u32[]{:S(2)}, u32[]{:S(2)}) collective-permute-start(bf16[224,128]{1,0:T(8,128)(2,1)S(1)} %get-tuple-element.41), channel_id=1, source_target_pairs={{0,8},{4,12},{8,16},{12,20},{16,24},{20,28},{24,0},{28,4},{1,9},{5... | collective-permute-start | bytes 172040 | tf_op jit(solution)/shard_map/ppermute | solution.py:356
  28.4 7.5 %collective-permute-start.9 = (bf16[224,128]{1,0:T(8,128)(2,1)S(1)}, bf16[224,128]{1,0:T(8,128)(2,1)S(1)}, u32[]{:S(2)}, u32[]{:S(2)}) collective-permute-start(bf16[224,128]{1,0:T(8,128)(2,1)S(1)} %get-tuple-element.42), channel_id=1, source_target_pairs={{0,12},{4,8},{8,20},{12,16},{16,28},{20,24},{24,4},{28,0},{1,13},{... | collective-permute-start | bytes 172040 | tf_op jit(solution)/shard_map/ppermute | solution.py:356
  28.5 8.4 %collective-permute-start.10 = (bf16[224,128]{1,0:T(8,128)(2,1)S(1)}, bf16[224,128]{1,0:T(8,128)(2,1)S(1)}, u32[]{:S(2)}, u32[]{:S(2)}) collective-permute-start(bf16[224,128]{1,0:T(8,128)(2,1)S(1)} %get-tuple-element.43), channel_id=1, source_target_pairs={{0,20},{4,16},{8,28},{12,24},{16,4},{20,0},{24,12},{28,8},{1,21},{... | collective-permute-start | bytes 172040 | tf_op jit(solution)/shard_map/ppermute | solution.py:356
  32.3 5.1 %collective-permute-start.11 = (bf16[224,128]{1,0:T(8,128)(2,1)S(1)}, bf16[224,128]{1,0:T(8,128)(2,1)S(1)}, u32[]{:S(2)}, u32[]{:S(2)}) collective-permute-start(bf16[224,128]{1,0:T(8,128)(2,1)S(1)} %get-tuple-element.44), channel_id=1, source_target_pairs={{0,28},{4,24},{8,4},{12,0},{16,12},{20,8},{24,20},{28,16},{1,29},{... | collective-permute-start | bytes 172040 | tf_op jit(solution)/shard_map/ppermute | solution.py:356
  33.2 4.8 %collective-permute-start.12 = (bf16[224,128]{1,0:T(8,128)(2,1)S(1)}, bf16[224,128]{1,0:T(8,128)(2,1)S(1)}, u32[]{:S(2)}, u32[]{:S(2)}) collective-permute-start(bf16[224,128]{1,0:T(8,128)(2,1)S(1)} %get-tuple-element.45), channel_id=1, source_target_pairs={{0,24},{4,28},{8,0},{12,4},{16,8},{20,12},{24,16},{28,20},{1,25},{... | collective-permute-start | bytes 172040 | tf_op jit(solution)/shard_map/ppermute | solution.py:356
  33.8 4.2 %collective-permute-start.13 = (bf16[224,128]{1,0:T(8,128)(2,1)S(1)}, bf16[224,128]{1,0:T(8,128)(2,1)S(1)}, u32[]{:S(2)}, u32[]{:S(2)}) collective-permute-start(bf16[224,128]{1,0:T(8,128)(2,1)S(1)} %get-tuple-element.46), channel_id=1, source_target_pairs={{0,4},{4,0},{8,12},{12,8},{16,20},{20,16},{24,28},{28,24},{1,5},{5... | collective-permute-start | bytes 172040 | tf_op jit(solution)/shard_map/ppermute | solution.py:356

commit v6 on v5

--- a/solution.py
+++ b/solution.py
@@ -329,6 +329,9 @@
             convolved.append(jnp.concatenate([first, conv_ref[i, EDGE:, cols]], axis=0))
         query, key, value = convolved
         gated_ref[:, cols] = (query * mixed).astype(jnp.bfloat16)
+        for k, held in ((0, gated_ref), (2, lag_ref)):
+            copies.append(pltpu.make_async_copy(held.at[:, cols], out_hbm[k].at[:, cols], sems.at[pair, k]))
+            copies[-1].start()
         own = (wide(cotangent_ref[:, cols]) * mixed, product_grad * value, product_grad * key)
         for i in range(3):
             grads[i, 0:rows, :] = own[i]
@@ -339,11 +342,8 @@
         tap_ref[1, :, cols] = extras[0, sums_kv, :]
         tap_ref[2, :, cols] = extras[1, sums_kv, :]
         tap_ref[0, :, cols] = extras[0, sums_q, :] + extras[1, sums_q, :]
-        held = (gated_ref.at[:, cols], stream_ref.at[:, :, cols], lag_ref.at[:, cols])
-        there = (out_hbm[0].at[:, cols], out_hbm[1].at[:, :, cols], out_hbm[2].at[:, cols])
-        for k in range(3):
-            copies.append(pltpu.make_async_copy(held[k], there[k], sems.at[pair, k]))
-            copies[-1].start()
+        copies.append(pltpu.make_async_copy(stream_ref.at[:, :, cols], out_hbm[1].at[:, :, cols], sems.at[pair, 1]))
+        copies[-1].start()
     copies.append(pltpu.make_async_copy(tap_ref, out_hbm[3], tap_sem.at[0]))
     copies[-1].start()
     for copy in copies:

time: 39.8 us -> 39.8 us (level)
  no operation moved by 1% of the time
where the time goes in v6:
time: 39.8 us; the launch traced here: 39.6 us
  starting transfers between devices  25.4 us (64%)
  Pallas kernels  8.45 us (21%)
  waiting for transfers between devices  5.14 us (13%)
  between operations  0.66 us (2%)
    ppermute x14, starting transfers between devices, exchanged(): lax.ppermute(block, 'ctx', [(source, partner(source, offset, 1, count)) f...  25.4 us
    ppermute x14, waiting for transfers between devices, exchanged(): lax.ppermute(block, 'ctx', [(source, partner(source, offset, 1, count)) f...  5.14 us
    pallas_call x1, Pallas kernels, local_dense(): pl.pallas_call(functools.partial(main_kernel, count, tap_count, 1.0 / mat...  3.1 us
    pallas_call x1, Pallas kernels, local_dense(): pl.pallas_call(functools.partial(local_kernel, tap_count), out_shape=[jax...  2.13 us
    pallas_call x1, Pallas kernels, local_dense(): pl.pallas_call(functools.partial(pack_kernel, count), out_shape=[jax.Shap...  1.65 us
    pallas_call x1, Pallas kernels, local_dense(): pl.pallas_call(functools.partial(finish_kernel, count, tap_count), out_sh...  1.58 us
  transfers between devices with their start and end apart: 14, of which 7 were waited for; matrix products, arithmetic and copies ran while one was open for 0% of the time, Pallas kernels for 5%

profile of v6, /device:TPU:0, one launch (start us, length us, event | category | flops | bytes accessed | tf_op | source)
XLA Modules:
  0.0 39.6 jit_solution(16771242175279826696)
XLA Ops:
  0.6 1.7 %pack.1 = (bf16[320,128]{1,0:T(8,128)(2,1)S(1)}, bf16[320,128]{1,0:T(8,128)(2,1)S(1)}, bf16[320,128]{1,0:T(8,128)(2,1)S(1)}, bf16[320,128]{1,0:T(8,128)(2,1)S(1)...) custom-call(bf16[3,128,512]{2,1,0:T(8,128)(2,1)} %streams_hbm.1, ...), custom_call_target="tpu_custom_call" | custom-call | tf_op jit(solution)/shard_map/pack/pallas_call | solution.py:376
  2.3 4.1 %collective-permute-start = (bf16[320,128]{1,0:T(8,128)(2,1)S(1)}, bf16[320,128]{1,0:T(8,128)(2,1)S(1)}, u32[]{:S(2)}, u32[]{:S(2)}) collective-permute-start(bf16[320,128]{1,0:T(8,128)(2,1)S(1)} %get-tuple-element.28), channel_id=1, source_target_pairs={{0,16},{4,20},{8,24},{12,28},{16,0},{20,4},{24,8},{28,12},{1,17},{... | collective-permute-start | bytes 245768 | tf_op jit(solution)/shard_map/ppermute | solution.py:356
  6.4 1.5 %collective-permute-start.1 = (bf16[320,128]{1,0:T(8,128)(2,1)S(1)}, bf16[320,128]{1,0:T(8,128)(2,1)S(1)}, u32[]{:S(2)}, u32[]{:S(2)}) collective-permute-start(bf16[320,128]{1,0:T(8,128)(2,1)S(1)} %get-tuple-element.29), channel_id=1, source_target_pairs={{0,4},{4,0},{8,12},{12,8},{16,20},{20,16},{24,28},{28,24},{1,5},{5... | collective-permute-start | bytes 245768 | tf_op jit(solution)/shard_map/ppermute | solution.py:356
  7.9 0.0 collective-permute-start.2
  7.9 2.8 %collective-permute-start.3 = (bf16[320,128]{1,0:T(8,128)(2,1)S(1)}, bf16[320,128]{1,0:T(8,128)(2,1)S(1)}, u32[]{:S(2)}, u32[]{:S(2)}) collective-permute-start(bf16[320,128]{1,0:T(8,128)(2,1)S(1)} %get-tuple-element.31), channel_id=1, source_target_pairs={{0,12},{4,8},{8,20},{12,16},{16,28},{20,24},{24,4},{28,0},{1,13},{... | collective-permute-start | bytes 245768 | tf_op jit(solution)/shard_map/ppermute | solution.py:356
  10.7 1.6 %collective-permute-start.4 = (bf16[320,128]{1,0:T(8,128)(2,1)S(1)}, bf16[320,128]{1,0:T(8,128)(2,1)S(1)}, u32[]{:S(2)}, u32[]{:S(2)}) collective-permute-start(bf16[320,128]{1,0:T(8,128)(2,1)S(1)} %get-tuple-element.32), channel_id=1, source_target_pairs={{0,8},{4,12},{8,16},{12,20},{16,24},{20,28},{24,0},{28,4},{1,9},{5... | collective-permute-start | bytes 245768 | tf_op jit(solution)/shard_map/ppermute | solution.py:356
  12.3 0.0 collective-permute-done.refs_1_
  12.3 4.8 %collective-permute-start.5 = (bf16[320,128]{1,0:T(8,128)(2,1)S(1)}, bf16[320,128]{1,0:T(8,128)(2,1)S(1)}, u32[]{:S(2)}, u32[]{:S(2)}) collective-permute-start(bf16[320,128]{1,0:T(8,128)(2,1)S(1)} %get-tuple-element.33), channel_id=1, source_target_pairs={{0,28},{4,24},{8,4},{12,0},{16,12},{20,8},{24,20},{28,16},{1,29},{... | collective-permute-start | bytes 245768 | tf_op jit(solution)/shard_map/ppermute | solution.py:356
  17.1 0.0 collective-permute-done.1.arrived_ref.refs_2_
  17.1 0.0 collective-permute-start.6
  17.1 2.1 %local.1 = (f32[3,128,512]{2,1,0:T(8,128)S(1)}, f32[3,7,512]{2,1,0:T(8,128)S(1)}, bf16[128,512]{1,0:T(8,128)(2,1)S(1)}, bf16[4,512,256]{2,1,0:T(8,128)(2,1)S(1)}...) custom-call(bf16[3,128,512]{2,1,0:T(8,128)(2,1)} %streams_hbm.1, f32[3,7,512]{2,1,0:T(8,128)} %taps_hbm.1, ...), custom_call_target="tpu_custom_call" | custom-call | tf_op jit(solution)/shard_map/local/pallas_call | solution.py:391
  19.2 0.3 collective-permute-done.2.refs_3_
  19.6 0.0 collective-permute-done.3.refs_4_
  19.6 0.0 collective-permute-done.4.refs_5_
  19.6 0.4 collective-permute-done.5.refs_6_
  20.0 1.6 %collective-permute-done.6.refs_7_ = bf16[320,128]{1,0:T(8,128)(2,1)S(1)} collective-permute-done((bf16[320,128]{1,0:T(8,128)(2,1)S(1)}, bf16[320,128]{1,0:T(8,128)(2,1)S(1)}, u32[]{:S(2)}, u32[]{:S(2)}) %collective-permute-start.6) | collective-permute-done | bytes 81952 | tf_op jit(solution)/shard_map/ppermute | solution.py:356
  21.5 3.1 %channels.1 = (bf16[224,128]{1,0:T(8,128)(2,1)S(1)}, bf16[224,128]{1,0:T(8,128)(2,1)S(1)}, bf16[224,128]{1,0:T(8,128)(2,1)S(1)}, bf16[224,128]{1,0:T(8,128)(2,1)...) custom-call(bf16[320,128]{1,0:T(8,128)(2,1)S(1)} %get-tuple-element., ...), custom_call_target="tpu_custom_call" | custom-call | tf_op jit(solution)/shard_map/channels/pallas_call | solution.py:412
  24.6 2.4 %collective-permute-start.7 = (bf16[224,128]{1,0:T(8,128)(2,1)S(1)}, bf16[224,128]{1,0:T(8,128)(2,1)S(1)}, u32[]{:S(2)}, u32[]{:S(2)}) collective-permute-start(bf16[224,128]{1,0:T(8,128)(2,1)S(1)} %get-tuple-element.40), channel_id=1, source_target_pairs={{0,16},{4,20},{8,24},{12,28},{16,0},{20,4},{24,8},{28,12},{1,17},{... | collective-permute-start | bytes 172040 | tf_op jit(solution)/shard_map/ppermute | solution.py:356
  27.0 1.4 %collective-permute-start.8 = (bf16[224,128]{1,0:T(8,128)(2,1)S(1)}, bf16[224,128]{1,0:T(8,128)(2,1)S(1)}, u32[]{:S(2)}, u32[]{:S(2)}) collective-permute-start(bf16[224,128]{1,0:T(8,128)(2,1)S(1)} %get-tuple-element.41), channel_id=1, source_target_pairs={{0,8},{4,12},{8,16},{12,20},{16,24},{20,28},{24,0},{28,4},{1,9},{5... | collective-permute-start | bytes 172040 | tf_op jit(solution)/shard_map/ppermute | solution.py:356
  28.4 0.1 collective-permute-start.9
  28.5 3.8 %collective-permute-start.10 = (bf16[224,128]{1,0:T(8,128)(2,1)S(1)}, bf16[224,128]{1,0:T(8,128)(2,1)S(1)}, u32[]{:S(2)}, u32[]{:S(2)}) collective-permute-start(bf16[224,128]{1,0:T(8,128)(2,1)S(1)} %get-tuple-element.43), channel_id=1, source_target_pairs={{0,20},{4,16},{8,28},{12,24},{16,4},{20,0},{24,12},{28,8},{1,21},{... | collective-permute-start | bytes 172040 | tf_op jit(solution)/shard_map/ppermute | solution.py:356
  32.3 0.9 %collective-permute-start.11 = (bf16[224,128]{1,0:T(8,128)(2,1)S(1)}, bf16[224,128]{1,0:T(8,128)(2,1)S(1)}, u32[]{:S(2)}, u32[]{:S(2)}) collective-permute-start(bf16[224,128]{1,0:T(8,128)(2,1)S(1)} %get-tuple-element.44), channel_id=1, source_target_pairs={{0,28},{4,24},{8,4},{12,0},{16,12},{20,8},{24,20},{28,16},{1,29},{... | collective-permute-start | bytes 172040 | tf_op jit(solution)/shard_map/ppermute | solution.py:356
  33.2 0.0 collective-permute-done.7.refs_1_
  33.2 0.6 %collective-permute-start.12 = (bf16[224,128]{1,0:T(8,128)(2,1)S(1)}, bf16[224,128]{1,0:T(8,128)(2,1)S(1)}, u32[]{:S(2)}, u32[]{:S(2)}) collective-permute-start(bf16[224,128]{1,0:T(8,128)(2,1)S(1)} %get-tuple-element.45), channel_id=1, source_target_pairs={{0,24},{4,28},{8,0},{12,4},{16,8},{20,12},{24,16},{28,20},{1,25},{... | collective-permute-start | bytes 172040 | tf_op jit(solution)/shard_map/ppermute | solution.py:356
  33.8 0.0 collective-permute-done.8.refs_2_
  33.8 1.4 %collective-permute-start.13 = (bf16[224,128]{1,0:T(8,128)(2,1)S(1)}, bf16[224,128]{1,0:T(8,128)(2,1)S(1)}, u32[]{:S(2)}, u32[]{:S(2)}) collective-permute-start(bf16[224,128]{1,0:T(8,128)(2,1)S(1)} %get-tuple-element.46), channel_id=1, source_target_pairs={{0,4},{4,0},{8,12},{12,8},{16,20},{20,16},{24,28},{28,24},{1,5},{5... | collective-permute-start | bytes 172040 | tf_op jit(solution)/shard_map/ppermute | solution.py:356
  35.2 0.7 %collective-permute-done.9.refs_3_ = bf16[224,128]{1,0:T(8,128)(2,1)S(1)} collective-permute-done((bf16[224,128]{1,0:T(8,128)(2,1)S(1)}, bf16[224,128]{1,0:T(8,128)(2,1)S(1)}, u32[]{:S(2)}, u32[]{:S(2)}) %collective-permute-start.9) | collective-permute-done | bytes 57376 | tf_op jit(solution)/shard_map/ppermute | solution.py:356
  35.9 1.0 %collective-permute-done.10.refs_4_ = bf16[224,128]{1,0:T(8,128)(2,1)S(1)} collective-permute-done((bf16[224,128]{1,0:T(8,128)(2,1)S(1)}, bf16[224,128]{1,0:T(8,128)(2,1)S(1)}, u32[]{:S(2)}, u32[]{:S(2)}) %collective-permute-start.10) | collective-permute-done | bytes 57376 | tf_op jit(solution)/shard_map/ppermute | solution.py:356
  36.9 0.5 %collective-permute-done.11.refs_5_ = bf16[224,128]{1,0:T(8,128)(2,1)S(1)} collective-permute-done((bf16[224,128]{1,0:T(8,128)(2,1)S(1)}, bf16[224,128]{1,0:T(8,128)(2,1)S(1)}, u32[]{:S(2)}, u32[]{:S(2)}) %collective-permute-start.11) | collective-permute-done | bytes 57376 | tf_op jit(solution)/shard_map/ppermute | solution.py:356
  37.4 0.6 %collective-permute-done.12.refs_6_ = bf16[224,128]{1,0:T(8,128)(2,1)S(1)} collective-permute-done((bf16[224,128]{1,0:T(8,128)(2,1)S(1)}, bf16[224,128]{1,0:T(8,128)(2,1)S(1)}, u32[]{:S(2)}, u32[]{:S(2)}) %collective-permute-start.12) | collective-permute-done | bytes 57376 | tf_op jit(solution)/shard_map/ppermute | solution.py:356
  38.0 0.0 collective-permute-done.13.refs_7_
  38.0 1.6 %finish.1 = (bf16[128,512]{1,0:T(8,128)(2,1)}, bf16[3,128,512]{2,1,0:T(8,128)(2,1)}, bf16[128,512]{1,0:T(8,128)(2,1)}, f32[3,7,512]{2,1,0:T(8,128)}) custom-call(bf16[224,128]{1,0:T(8,128)(2,1)S(1)} %get-tuple-element.39.refs_0_, bf16[224,128]{1,0:T(8,128)(2,1)S(1)} %collective-permute-done.7.refs_1_, bf16[224,128]{1,0:T(8,128)(2,1)S(1)} %collective-permute-done.8.refs_2_, ...), custom_call_target="tpu_custom_call" | custom-call | tf_op jit(solution)/shard_map/finish/pallas_call | solution.py:436
Async XLA Ops:
  2.3 10.0 %collective-permute-start = (bf16[320,128]{1,0:T(8,128)(2,1)S(1)}, bf16[320,128]{1,0:T(8,128)(2,1)S(1)}, u32[]{:S(2)}, u32[]{:S(2)}) collective-permute-start(bf16[320,128]{1,0:T(8,128)(2,1)S(1)} %get-tuple-element.28), channel_id=1, source_target_pairs={{0,16},{4,20},{8,24},{12,28},{16,0},{20,4},{24,8},{28,12},{1,17},{... | collective-permute-start | bytes 245768 | tf_op jit(solution)/shard_map/ppermute | solution.py:356
  6.4 10.7 %collective-permute-start.1 = (bf16[320,128]{1,0:T(8,128)(2,1)S(1)}, bf16[320,128]{1,0:T(8,128)(2,1)S(1)}, u32[]{:S(2)}, u32[]{:S(2)}) collective-permute-start(bf16[320,128]{1,0:T(8,128)(2,1)S(1)} %get-tuple-element.29), channel_id=1, source_target_pairs={{0,4},{4,0},{8,12},{12,8},{16,20},{20,16},{24,28},{28,24},{1,5},{5... | collective-permute-start | bytes 245768 | tf_op jit(solution)/shard_map/ppermute | solution.py:356
  7.9 11.6 %collective-permute-start.2 = (bf16[320,128]{1,0:T(8,128)(2,1)S(1)}, bf16[320,128]{1,0:T(8,128)(2,1)S(1)}, u32[]{:S(2)}, u32[]{:S(2)}) collective-permute-start(bf16[320,128]{1,0:T(8,128)(2,1)S(1)} %get-tuple-element.30), channel_id=1, source_target_pairs={{0,20},{4,16},{8,28},{12,24},{16,4},{20,0},{24,12},{28,8},{1,21},{... | collective-permute-start | bytes 245768 | tf_op jit(solution)/shard_map/ppermute | solution.py:356
  7.9 11.6 %collective-permute-start.3 = (bf16[320,128]{1,0:T(8,128)(2,1)S(1)}, bf16[320,128]{1,0:T(8,128)(2,1)S(1)}, u32[]{:S(2)}, u32[]{:S(2)}) collective-permute-start(bf16[320,128]{1,0:T(8,128)(2,1)S(1)} %get-tuple-element.31), channel_id=1, source_target_pairs={{0,12},{4,8},{8,20},{12,16},{16,28},{20,24},{24,4},{28,0},{1,13},{... | collective-permute-start | bytes 245768 | tf_op jit(solution)/shard_map/ppermute | solution.py:356
  10.7 8.8 %collective-permute-start.4 = (bf16[320,128]{1,0:T(8,128)(2,1)S(1)}, bf16[320,128]{1,0:T(8,128)(2,1)S(1)}, u32[]{:S(2)}, u32[]{:S(2)}) collective-permute-start(bf16[320,128]{1,0:T(8,128)(2,1)S(1)} %get-tuple-element.32), channel_id=1, source_target_pairs={{0,8},{4,12},{8,16},{12,20},{16,24},{20,28},{24,0},{28,4},{1,9},{5... | collective-permute-start | bytes 245768 | tf_op jit(solution)/shard_map/ppermute | solution.py:356
  12.3 7.6 %collective-permute-start.5 = (bf16[320,128]{1,0:T(8,128)(2,1)S(1)}, bf16[320,128]{1,0:T(8,128)(2,1)S(1)}, u32[]{:S(2)}, u32[]{:S(2)}) collective-permute-start(bf16[320,128]{1,0:T(8,128)(2,1)S(1)} %get-tuple-element.33), channel_id=1, source_target_pairs={{0,28},{4,24},{8,4},{12,0},{16,12},{20,8},{24,20},{28,16},{1,29},{... | collective-permute-start | bytes 245768 | tf_op jit(solution)/shard_map/ppermute | solution.py:356
  17.1 4.4 %collective-permute-start.6 = (bf16[320,128]{1,0:T(8,128)(2,1)S(1)}, bf16[320,128]{1,0:T(8,128)(2,1)S(1)}, u32[]{:S(2)}, u32[]{:S(2)}) collective-permute-start(bf16[320,128]{1,0:T(8,128)(2,1)S(1)} %get-tuple-element.34), channel_id=1, source_target_pairs={{0,24},{4,28},{8,0},{12,4},{16,8},{20,12},{24,16},{28,20},{1,25},{... | collective-permute-start | bytes 245768 | tf_op jit(solution)/shard_map/ppermute | solution.py:356
  24.6 8.5 %collective-permute-start.7 = (bf16[224,128]{1,0:T(8,128)(2,1)S(1)}, bf16[224,128]{1,0:T(8,128)(2,1)S(1)}, u32[]{:S(2)}, u32[]{:S(2)}) collective-permute-start(bf16[224,128]{1,0:T(8,128)(2,1)S(1)} %get-tuple-element.40), channel_id=1, source_target_pairs={{0,16},{4,20},{8,24},{12,28},{16,0},{20,4},{24,8},{28,12},{1,17},{... | collective-permute-start | bytes 172040 | tf_op jit(solution)/shard_map/ppermute | solution.py:356
  27.0 6.8 %collective-permute-start.8 = (bf16[224,128]{1,0:T(8,128)(2,1)S(1)}, bf16[224,128]{1,0:T(8,128)(2,1)S(1)}, u32[]{:S(2)}, u32[]{:S(2)}) collective-permute-start(bf16[224,128]{1,0:T(8,128)(2,1)S(1)} %get-tuple-element.41), channel_id=1, source_target_pairs={{0,8},{4,12},{8,16},{12,20},{16,24},{20,28},{24,0},{28,4},{1,9},{5... | collective-permute-start | bytes 172040 | tf_op jit(solution)/shard_map/ppermute | solution.py:356
  28.4 7.5 %collective-permute-start.9 = (bf16[224,128]{1,0:T(8,128)(2,1)S(1)}, bf16[224,128]{1,0:T(8,128)(2,1)S(1)}, u32[]{:S(2)}, u32[]{:S(2)}) collective-permute-start(bf16[224,128]{1,0:T(8,128)(2,1)S(1)} %get-tuple-element.42), channel_id=1, source_target_pairs={{0,12},{4,8},{8,20},{12,16},{16,28},{20,24},{24,4},{28,0},{1,13},{... | collective-permute-start | bytes 172040 | tf_op jit(solution)/shard_map/ppermute | solution.py:356
  28.5 8.4 %collective-permute-start.10 = (bf16[224,128]{1,0:T(8,128)(2,1)S(1)}, bf16[224,128]{1,0:T(8,128)(2,1)S(1)}, u32[]{:S(2)}, u32[]{:S(2)}) collective-permute-start(bf16[224,128]{1,0:T(8,128)(2,1)S(1)} %get-tuple-element.43), channel_id=1, source_target_pairs={{0,20},{4,16},{8,28},{12,24},{16,4},{20,0},{24,12},{28,8},{1,21},{... | collective-permute-start | bytes 172040 | tf_op jit(solution)/shard_map/ppermute | solution.py:356
  32.3 5.1 %collective-permute-start.11 = (bf16[224,128]{1,0:T(8,128)(2,1)S(1)}, bf16[224,128]{1,0:T(8,128)(2,1)S(1)}, u32[]{:S(2)}, u32[]{:S(2)}) collective-permute-start(bf16[224,128]{1,0:T(8,128)(2,1)S(1)} %get-tuple-element.44), channel_id=1, source_target_pairs={{0,28},{4,24},{8,4},{12,0},{16,12},{20,8},{24,20},{28,16},{1,29},{... | collective-permute-start | bytes 172040 | tf_op jit(solution)/shard_map/ppermute | solution.py:356
  33.2 4.8 %collective-permute-start.12 = (bf16[224,128]{1,0:T(8,128)(2,1)S(1)}, bf16[224,128]{1,0:T(8,128)(2,1)S(1)}, u32[]{:S(2)}, u32[]{:S(2)}) collective-permute-start(bf16[224,128]{1,0:T(8,128)(2,1)S(1)} %get-tuple-element.45), channel_id=1, source_target_pairs={{0,24},{4,28},{8,0},{12,4},{16,8},{20,12},{24,16},{28,20},{1,25},{... | collective-permute-start | bytes 172040 | tf_op jit(solution)/shard_map/ppermute | solution.py:356
  33.8 4.2 %collective-permute-start.13 = (bf16[224,128]{1,0:T(8,128)(2,1)S(1)}, bf16[224,128]{1,0:T(8,128)(2,1)S(1)}, u32[]{:S(2)}, u32[]{:S(2)}) collective-permute-start(bf16[224,128]{1,0:T(8,128)(2,1)S(1)} %get-tuple-element.46), channel_id=1, source_target_pairs={{0,4},{4,0},{8,12},{12,8},{16,20},{20,16},{24,28},{28,24},{1,5},{5... | collective-permute-start | bytes 172040 | tf_op jit(solution)/shard_map/ppermute | solution.py:356
